TPU v7x, 32 devices: a whole 2x2x4 slice. The times are simulated.
32 devices in a mesh: dp: 4 (over y, core), shard: 8 (over z, x).
Axes of the slice: x: 2, y: 2, z: 4, core: 2. Of those that a mesh axis runs over, the one named last changes fastest.
Arguments:
- grads: bfloat16 [4, 18, 7168, 128], P('dp', None, 'shard'), may hold values from -230 to 230
- params: float32 [18, 7168, 128], P(None, 'shard'), may hold values from -6 to 6
- table: int32 [18], replicated, may hold values from 0 to 17, each once
Outputs:
- new_params: float32 [18, 7168, 128], P(None, 'shard')
- update: bfloat16 [18, 7168, 128], P(None, 'shard')
Inputs may be any that keep to these rules, and one draw needn't show every extreme that they name: A permutation: gradient block j belongs to head table[j].
All inputs are finite; a program needn't handle non-finite values.
Results may differ from a plain program's by a relative error of at most 0.006.
Values may be sent and summed in bfloat16 or wider, within the bound.
No kernel may reach another device: no remote copies, remote signals or barrier semaphores. Data moves between devices by JAX's collectives and lax.ppermute only.
A program may use at most 128 MiB of HBM per device.

v0:
```python
import math

import jax
import jax.numpy as jnp
from jax import lax
from jax.sharding import PartitionSpec as P

D = 7168
V = 128
ITERS = 5


quintic_one = 3.4445
quintic_two = -4.775
quintic_three = 2.0315
epsilon = 1e-07
learning_rate = 0.02
decay_rate = 0.1


def local_gram(current):
    return jnp.einsum(
        "mrv,mrw->mvw",
        current,
        current,
        precision=lax.Precision.HIGHEST,
        preferred_element_type=jnp.float32,
    )


def newton_schulz(blocks, squares, gram_fn):
    norm_value = jnp.sqrt(squares)[:, None, None]
    current = blocks.astype(jnp.float32) / (norm_value + epsilon)
    for index in range(ITERS):
        gram = gram_fn(current)
        poly = quintic_two * gram + quintic_three * jnp.einsum(
            "mvu,muw->mvw",
            gram,
            gram,
            precision=lax.Precision.HIGHEST,
            preferred_element_type=jnp.float32,
        )
        current = quintic_one * current + jnp.einsum(
            "mrv,mvw->mrw",
            current,
            poly,
            precision=lax.Precision.HIGHEST,
            preferred_element_type=jnp.float32,
        )
    return current.astype(jnp.bfloat16)


def pad_blocks(blocks, total_count):
    count, rows, width = blocks.shape
    filler = jnp.zeros((total_count - count, rows, width), blocks.dtype)
    return jnp.concatenate([blocks, filler], axis=0)


def solve_whole(received, groups):
    items, _, rows, width = received.shape
    whole = received.reshape(items, groups * rows, width)
    wide = whole.astype(jnp.float32)
    squares = jnp.sum(wide * wide, axis=(1, 2))
    result = newton_schulz(whole, squares, local_gram)
    return result.reshape(received.shape)


def per_device(grads, params, table):
    count = grads.shape[1]
    rows = grads.shape[2]
    width = grads.shape[3]
    groups = lax.axis_size("shard")
    total = lax.psum(grads[0].astype(jnp.float32), "dp")
    blocks = total.astype(jnp.bfloat16)
    slots = (count + groups - 1) // groups
    outgoing = pad_blocks(blocks, slots * groups).reshape(slots, groups, rows, width)
    result = solve_whole(
        lax.all_to_all(outgoing, "shard", split_axis=1, concat_axis=1, tiled=True), groups
    )
    returned = lax.all_to_all(result, "shard", split_axis=1, concat_axis=1, tiled=True)
    ortho = returned.reshape(slots * groups, rows, width)[:count]
    positions = jnp.arange(count, dtype=jnp.int32)
    matches = (table[None, :] == positions[:, None]).astype(jnp.int32)
    inverse = jnp.sum(matches * positions[None, :], axis=1)
    heads = ortho[inverse]
    scaled = 0.2 * math.sqrt(max(D, V)) * heads.astype(jnp.float32)
    new_params = params - learning_rate * (scaled + decay_rate * params)
    return (new_params, scaled.astype(jnp.bfloat16))


def solution(mesh):
    return jax.shard_map(
        per_device,
        mesh=mesh,
        in_specs=(P("dp", None, "shard", None), P(None, "shard", None), P()),
        out_specs=(P(None, "shard", None), P(None, "shard", None)),
        check_vma=False,
    )
```

profile of v0, /device:TPU:0, one launch (start us, length us, event | category | flops | bytes accessed | tf_op | source)
XLA Modules:
  0.0 596.2 jit_solution(11635803318478411239)
XLA Ops:
  0.6 6.4 %bitcast_convert_fusion = f32[18,896,128]{2,1,0:T(8,128)} fusion(bf16[1,18,896,128]{3,2,1,0:T(8,128)(2,1)} %param.3), kind=kLoop, calls=%fused_computation.11 | loop fusion | flops 2064384 | bytes 12386304 | tf_op jit(solution)/shard_map/convert_element_type | solution.py:73
  7.0 146.9 %all-reduce.2 = bf16[18,896,128]{2,1,0:T(8,128)(2,1)} all-reduce(f32[18,896,128]{2,1,0:T(8,128)} %bitcast_convert_fusion), channel_id=1, replica_groups=mesh['dp'=4,'shard'=8] {'dp'}, use_global_device_ids=true, to_apply=%region_0.0 | all-reduce | flops 2064384 | bytes 12386304 | tf_op jit(solution)/shard_map/psum | solution.py:73
  153.9 2.7 concatenate.3
  156.7 0.5 copy.32
  157.2 127.3 %all_to_all.10 = bf16[3,8,896,128]{3,2,0,1:T(8,128)(2,1)S(1)} all-to-all(bf16[3,8,896,128]{3,2,0,1:T(8,128)(2,1)S(1)} %copy.32), channel_id=1, replica_groups=mesh['dp'=4,'shard'=8] {'shard'}, dimensions={1} | all-to-all | bytes 11010048 | tf_op jit(solution)/shard_map/all_to_all | solution.py:78
  284.5 1.4 multiply_reduce_fusion
  286.0 5.4 copy.33
  291.4 4.9 bitcast_divide_fusion
  296.3 17.7 %fusion.7 = f32[3,128,128]{2,1,0:T(8,128)S(1)} fusion(f32[3,7168,128]{2,1,0:T(8,128)S(1)} %bitcast_divide_fusion), kind=kOutput, calls=%fused_computation.28 | convolution fusion | flops 4227858432 | bytes 11206656 | tf_op jit(solution)/shard_map/mrv,mrw->mvw/dot_general | solution.py:22
  314.0 0.3 fusion.5
  314.3 11.7 %multiply_add_fusion.3 = f32[3,7168,128]{2,1,0:T(8,128)S(1)} fusion(f32[3,7168,128]{2,1,0:T(8,128)S(1)} %bitcast_divide_fusion, f32[3,128,128]{2,1,0:T(8,128)S(1)} %fusion.5), kind=kOutput, calls=%fused_computation.6 | convolution fusion | flops 4233363456 | bytes 22216704 | tf_op jit(solution)/shard_map/mrv,mvw->mrw/dot_general | solution.py:43
  326.0 18.6 %fusion.8 = f32[3,128,128]{2,1,0:T(8,128)S(1)} fusion(f32[3,7168,128]{2,1,0:T(8,128)S(1)} %multiply_add_fusion.3), kind=kOutput, calls=%fused_computation.29 | convolution fusion | flops 4227858432 | bytes 11206656 | tf_op jit(solution)/shard_map/mrv,mrw->mvw/dot_general | solution.py:22
  344.6 0.3 fusion.4
  344.9 11.9 %multiply_add_fusion.2 = f32[3,7168,128]{2,1,0:T(8,128)S(1)} fusion(f32[3,7168,128]{2,1,0:T(8,128)S(1)} %multiply_add_fusion.3, f32[3,128,128]{2,1,0:T(8,128)S(1)} %fusion.4), kind=kOutput, calls=%fused_computation.5 | convolution fusion | flops 4233363456 | bytes 22216704 | tf_op jit(solution)/shard_map/mrv,mvw->mrw/dot_general | solution.py:43
  356.8 18.4 %fusion.9 = f32[3,128,128]{2,1,0:T(8,128)S(1)} fusion(f32[3,7168,128]{2,1,0:T(8,128)S(1)} %multiply_add_fusion.2), kind=kOutput, calls=%fused_computation.30 | convolution fusion | flops 4227858432 | bytes 11206656 | tf_op jit(solution)/shard_map/mrv,mrw->mvw/dot_general | solution.py:22
  375.2 0.3 fusion.3
  375.6 11.7 %multiply_add_fusion.1 = f32[3,7168,128]{2,1,0:T(8,128)S(1)} fusion(f32[3,7168,128]{2,1,0:T(8,128)S(1)} %multiply_add_fusion.2, f32[3,128,128]{2,1,0:T(8,128)S(1)} %fusion.3), kind=kOutput, calls=%fused_computation.4 | convolution fusion | flops 4233363456 | bytes 22216704 | tf_op jit(solution)/shard_map/mrv,mvw->mrw/dot_general | solution.py:43
  387.2 18.6 %fusion.10 = f32[3,128,128]{2,1,0:T(8,128)S(1)} fusion(f32[3,7168,128]{2,1,0:T(8,128)S(1)} %multiply_add_fusion.1), kind=kOutput, calls=%fused_computation.31 | convolution fusion | flops 4227858432 | bytes 11206656 | tf_op jit(solution)/shard_map/mrv,mrw->mvw/dot_general | solution.py:22
  405.9 0.3 fusion.2
  406.2 11.6 %multiply_add_fusion = f32[3,7168,128]{2,1,0:T(8,128)S(1)} fusion(f32[3,7168,128]{2,1,0:T(8,128)S(1)} %multiply_add_fusion.1, f32[3,128,128]{2,1,0:T(8,128)S(1)} %fusion.2), kind=kOutput, calls=%fused_computation.3 | convolution fusion | flops 4233363456 | bytes 22216704 | tf_op jit(solution)/shard_map/mrv,mvw->mrw/dot_general | solution.py:43
  417.8 18.8 %fusion.11 = f32[3,128,128]{2,1,0:T(8,128)S(1)} fusion(f32[3,7168,128]{2,1,0:T(8,128)S(1)} %multiply_add_fusion), kind=kOutput, calls=%fused_computation.32 | convolution fusion | flops 4227858432 | bytes 11206656 | tf_op jit(solution)/shard_map/mrv,mrw->mvw/dot_general | solution.py:22
  436.7 0.3 fusion.1
  437.0 10.9 %add_convert_fusion = bf16[3,7168,128]{2,1,0:T(8,128)(2,1)S(1)} fusion(f32[3,7168,128]{2,1,0:T(8,128)S(1)} %multiply_add_fusion, f32[3,128,128]{2,1,0:T(8,128)S(1)} %fusion.1), kind=kOutput, calls=%fused_computation.2 | convolution fusion | flops 4236115968 | bytes 16711680 | tf_op jit(solution)/shard_map/mrv,mvw->mrw/dot_general | solution.py:43
  447.9 0.0 copy-start
  447.9 3.0 copy.39
  450.9 4.8 all-to-all-start.1
  455.8 0.1 select_reduce_fusion
  455.9 120.8 %all-to-all-done.1 = bf16[3,8,896,128]{3,2,0,1:T(8,128)(2,1)} async-done(((bf16[3,8,896,128]{3,2,0,1:T(8,128)(2,1)}), bf16[3,8,896,128]{3,2,0,1:T(8,128)(2,1)}, u32[]{:S(2)}, u32[]{:S(2)}) %all-to-all-start.1) | async-done | bytes 5505056 | tf_op jit(solution)/shard_map/all_to_all | solution.py:80
  576.7 3.1 copy.40
  579.8 2.3 slice.6
  582.1 5.5 gather_fusion
  587.6 8.4 %fusion = (bf16[18,896,128]{2,1,0:T(8,128)(2,1)}, f32[18,896,128]{2,1,0:T(8,128)}) fusion(bf16[18,896,128]{2,1,0:T(8,128)(2,1)} %gather_fusion, f32[18,896,128]{2,1,0:T(8,128)} %param.4), kind=kLoop, calls=%fused_computation.10 | loop fusion | flops 14450688 | bytes 24772608 | tf_op jit(solution)/shard_map/convert_element_type | solution.py:88
  (4 shorter events, 0.0 us)
Async XLA Ops:
  447.9 7.8 %copy-start = (s32[18]{0:T(128)S(1)}, s32[18]{0:T(128)}, u32[]{:S(2)}) copy-start(s32[18]{0:T(128)} %param.5) | copy-start | bytes 220
  450.9 125.8 %all-to-all-start.1 = ((bf16[3,8,896,128]{3,2,0,1:T(8,128)(2,1)}), bf16[3,8,896,128]{3,2,0,1:T(8,128)(2,1)}, u32[]{:S(2)}, u32[]{:S(2)}) async-start(bf16[3,8,896,128]{3,2,0,1:T(8,128)(2,1)} %copy.39), calls=%async_computation.1 | async-start | bytes 11010048 | tf_op jit(solution)/shard_map/all_to_all | solution.py:80
where the time goes:
time: 599 us; the launch traced here: 596 us
  blocking collectives  274 us (46%)
  matrix products  152 us (25%)
  waiting for transfers between devices  121 us (20%)
  local copies, waits for them, and re-layouts  22.6 us (4%)
  other arithmetic  21.3 us (4%)
    psum x1, blocking collectives, per_device(): total = lax.psum(grads[0].astype(jnp.float32), 'dp')  147 us
    all_to_all x1, blocking collectives, per_device(): lax.all_to_all(outgoing, 'shard', split_axis=1, concat_axis=1, tiled=True)  127 us
    all_to_all x1, waiting for transfers between devices, per_device(): lax.all_to_all(result, 'shard', split_axis=1, concat_axis=1, tiled=True)  121 us
    dot_general x5, matrix products, local_gram(): jnp.einsum('mrv,mrw->mvw', current, current, precision=lax.Precision.HIGH...  92.1 us
    dot_general x5, matrix products, newton_schulz(): jnp.einsum('mrv,mvw->mrw', current, poly, precision=lax.Precision.HIGHEST...  57.8 us
  transfers between devices with their start and end apart: 1, of which 1 were waited for; matrix products, arithmetic and copies ran while one was open for 0% of the time, Pallas kernels for 0%

commit v1 on v0

v1 whole, which is shorter than its diff:
```python
import functools
import math

import jax
import jax.numpy as jnp
from jax import lax
from jax.experimental import pallas as pl
from jax.experimental.pallas import tpu as pltpu
from jax.sharding import PartitionSpec as P

D = 7168
V = 128
ITERS = 5
CORES = 2

quintic_one = 3.4445
quintic_two = -4.775
quintic_three = 2.0315
epsilon = 1e-07
learning_rate = 0.02
decay_rate = 0.1
HIGHEST = lax.Precision.HIGHEST


def dot32(left, right):
    return jnp.dot(left, right, precision=HIGHEST, preferred_element_type=jnp.float32)


def newton_kernel(parts_ref, out_ref):
    gram = parts_ref[0, 0]
    for index in range(1, parts_ref.shape[0]):
        gram = gram + parts_ref[index, 0]
    rows = lax.broadcasted_iota(jnp.int32, (V, V), 0)
    columns = lax.broadcasted_iota(jnp.int32, (V, V), 1)
    eye = (rows == columns).astype(jnp.float32)
    norm_value = jnp.sqrt(jnp.sum(gram * eye))
    scale = 1.0 / (norm_value + epsilon)
    gram = (gram * scale) * scale
    product = None
    for index in range(ITERS):
        poly = quintic_one * eye + quintic_two * gram + quintic_three * dot32(gram, gram)
        product = poly if product is None else dot32(product, poly)
        if index < ITERS - 1:
            gram = dot32(dot32(gram, poly), poly)
    out_ref[0] = product * scale


def newton_schulz(parts):
    groups, items = parts.shape[:2]
    return pl.pallas_call(
        newton_kernel,
        out_shape=jax.ShapeDtypeStruct((items, V, V), jnp.float32),
        grid=(items,),
        in_specs=[pl.BlockSpec((groups, 1, V, V), lambda i: (0, i, 0, 0))],
        out_specs=pl.BlockSpec((1, V, V), lambda i: (i, 0, 0)),
        cost_estimate=pl.CostEstimate(
            flops=items * 18 * 12 * V**3, bytes_accessed=groups * items * V * V * 4, transcendentals=0
        ),
    )(parts)


def apply_kernel(starts, heads_ref, picks_ref, *refs):
    count = len(starts) - 1
    sources = refs[:count]
    q_ref, params_ref, new_ref, update_ref = refs[count:]
    step = pl.program_id(0)
    q = q_ref[0]
    high = q.astype(jnp.bfloat16)
    low = (q - high.astype(jnp.float32)).astype(jnp.bfloat16)

    def work(source):
        rows = source[0]
        ortho = jnp.dot(rows, high, preferred_element_type=jnp.float32)
        ortho = ortho + jnp.dot(rows, low, preferred_element_type=jnp.float32)
        ortho = ortho.astype(jnp.bfloat16).astype(jnp.float32)
        scaled = 0.2 * math.sqrt(max(D, V)) * ortho
        params = params_ref[0]
        new_ref[0] = params - learning_rate * (scaled + decay_rate * params)
        update_ref[0] = scaled.astype(jnp.bfloat16)

    for index, source in enumerate(sources):
        if count == 1:
            work(source)
        else:
            inside = (step >= starts[index]) & (step < starts[index + 1])
            pl.when(inside)(functools.partial(work, source))


def apply_all(sources, q, params, heads, picks):
    count, rows, width = params.shape
    starts = [0]
    for source in sources:
        starts.append(starts[-1] + source.shape[0])
    assert starts[-1] == count

    def source_map(start, items, i, heads_ref, picks_ref):
        return (jnp.clip(i - start, 0, items - 1), 0, 0)

    def head_map(i, heads_ref, picks_ref):
        return (heads_ref[i], 0, 0)

    source_specs = [
        pl.BlockSpec((1, rows, width), functools.partial(source_map, start, source.shape[0]))
        for start, source in zip(starts, sources)
    ]
    grid_spec = pltpu.PrefetchScalarGridSpec(
        num_scalar_prefetch=2,
        grid=(count,),
        in_specs=source_specs
        + [
            pl.BlockSpec((1, V, V), lambda i, heads_ref, picks_ref: (picks_ref[i], 0, 0)),
            pl.BlockSpec((1, rows, width), head_map),
        ],
        out_specs=[pl.BlockSpec((1, rows, width), head_map)] * 2,
    )
    size = count * rows * width
    return pl.pallas_call(
        functools.partial(apply_kernel, tuple(starts)),
        grid_spec=grid_spec,
        out_shape=[
            jax.ShapeDtypeStruct(params.shape, jnp.float32),
            jax.ShapeDtypeStruct(params.shape, jnp.bfloat16),
        ],
        cost_estimate=pl.CostEstimate(flops=4 * size * V, bytes_accessed=12 * size, transcendentals=0),
        compiler_params=pltpu.CompilerParams(vmem_limit_bytes=32 * 1024 * 1024),
    )(heads, picks, *sources, q, params)


def per_device(grads, params, table):
    local = grads[0]
    count, rows, width = local.shape
    replicas = lax.axis_size("dp")
    groups = lax.axis_size("shard")
    members = replicas // CORES
    own = -(-count // members)
    half = own // CORES
    odd = own % CORES
    place = lax.axis_index("dp")
    core = place % CORES
    member = place // CORES
    if members * own > count:
        filler = jnp.zeros((members * own - count, rows, width), local.dtype)
        local = jnp.concatenate([local, filler], axis=0)

    def pairs_of(shift):
        return [
            (m * CORES + c, ((m + shift) % members) * CORES + c)
            for m in range(members)
            for c in range(CORES)
        ]

    core_pairs = [(m * CORES + c, m * CORES + 1 - c) for m in range(members) for c in range(CORES)]
    odd_pairs = [(m * CORES + 1, m * CORES) for m in range(members)]

    def owned_by(array, owner):
        return lax.dynamic_slice_in_dim(array, owner * own, own, axis=0)

    raws = [owned_by(local, member)]
    for shift in range(1, members):
        outgoing = owned_by(local, (member + shift) % members)
        raws.append(lax.ppermute(outgoing, "dp", pairs_of(shift)))

    def of_core(array, which):
        return lax.dynamic_slice_in_dim(array, which * half, half, axis=0)

    mains, odds = [], []
    for raw in raws:
        arrived = lax.ppermute(of_core(raw, 1 - core), "dp", core_pairs)
        mains.append(of_core(raw, core).astype(jnp.float32) + arrived.astype(jnp.float32))
        if odd:
            last = raw[own - 1 :]
            arrived = lax.ppermute(last, "dp", odd_pairs)
            odds.append(last.astype(jnp.float32) + arrived.astype(jnp.float32))
    main = functools.reduce(jnp.add, mains).astype(jnp.bfloat16)
    pieces = [main]
    if odd:
        extra = functools.reduce(jnp.add, odds).astype(jnp.bfloat16)
        pieces.append(extra)

    gram = jnp.concatenate(
        [
            jnp.einsum("mrv,mrw->mvw", piece, piece, preferred_element_type=jnp.float32)
            for piece in pieces
        ],
        axis=0,
    )
    slots = half + odd
    items = -(-slots // groups)
    gram = jnp.concatenate([gram, jnp.zeros((items * groups - slots, V, V), jnp.float32)], axis=0)
    gram = gram.reshape(groups, items, V, V)
    parts = lax.all_to_all(gram, "shard", split_axis=0, concat_axis=0, tiled=True)
    solved = newton_schulz(parts)
    q_core = lax.all_gather(solved, "shard", axis=0, tiled=True)[:slots]

    def spread(array):
        return [array] + [lax.ppermute(array, "dp", pairs_of(shift)) for shift in range(1, members)]

    main_all = spread(main)
    main_other = [lax.ppermute(array, "dp", core_pairs) for array in main_all]
    extra_all = []
    if odd:
        down_pairs = [(m * CORES, m * CORES + 1) for m in range(members)]
        extra_all = [extra]
        for shift in range(1, members):
            pairs = [pair for pair in pairs_of(shift) if pair[0] % CORES == 0]
            extra_all.append(lax.ppermute(extra, "dp", pairs))
        extra_all = [
            jnp.where(core == 0, array, lax.ppermute(array, "dp", down_pairs)) for array in extra_all
        ]
    q_all = spread(q_core)
    q_other = [lax.ppermute(array, "dp", core_pairs) for array in q_all]

    sources, blocks, qs = [], [], []
    for shift in range(members):
        owner = (member - shift) % members
        for which, array in ((core, main_all[shift]), (1 - core, main_other[shift])):
            sources.append(array)
            blocks.append(owner * own + which * half + jnp.arange(half, dtype=jnp.int32))
        qs.append(q_all[shift][:half])
        qs.append(q_other[shift][:half])
        if odd:
            sources.append(extra_all[shift])
            blocks.append((owner * own + own - 1)[None])
            qs.append(jnp.where(core == 0, q_all[shift][half:], q_other[shift][half:]))
    blocks = jnp.concatenate(blocks).astype(jnp.int32)
    q = jnp.concatenate(qs, axis=0)
    picks = jnp.arange(count, dtype=jnp.int32)
    if members * own > count:
        order = jnp.argsort(blocks)[:count]
        sources = [jnp.concatenate(sources, axis=0)[order]]
        blocks = blocks[order]
        picks = order.astype(jnp.int32)
    heads = table[blocks]
    new_params, update = apply_all(sources, q, params, heads, picks)
    return (new_params, update)


def solution(mesh):
    return jax.shard_map(
        per_device,
        mesh=mesh,
        in_specs=(P("dp", None, "shard", None), P(None, "shard", None), P()),
        out_specs=(P(None, "shard", None), P(None, "shard", None)),
        check_vma=False,
    )
```

time: 599 us -> 148 us (0.25)
  blocking collectives: 274 us -> 31.6 us
  matrix products: 152 us -> 0.72 us
  waiting for transfers between devices: 121 us -> 59.5 us
  other arithmetic: 21.3 us -> 4.57 us
  Pallas kernels: 0 us -> 16.2 us
  starting transfers between devices: 4.85 us -> 20.4 us
  local copies, waits for them, and re-layouts: 22.6 us -> 13.2 us
    dot_general x15 -> x2, matrix products: 152 us -> 0.72 us  [per_device(): jnp.einsum('mrv,mrw->mvw', piece, piece, preferred_element_type=jnp.float32)]
    psum x1 -> x0, blocking collectives: 147 us -> none  [per_device(): total = lax.psum(grads[0].astype(jnp.float32), 'dp')]
    all_to_all x1 -> x0, blocking collectives: 127 us -> none  [per_device(): lax.all_to_all(outgoing, 'shard', split_axis=1, concat_axis=1, tiled=True)]
    all_to_all x1, waiting for transfers between devices: 121 us -> 2.96 us  [per_device(): lax.all_to_all(gram, 'shard', split_axis=0, concat_axis=0, tiled=True)]
    ppermute x0 -> x14, waiting for transfers between devices: none -> 56.5 us  [the longest x1 43 us: per_device(): raws.append(lax.ppermute(outgoing, 'dp', pairs_of(shift)))]
    all_gather x0 -> x1, blocking collectives: none -> 31.6 us  [per_device(): q_core = lax.all_gather(solved, 'shard', axis=0, tiled=True)[:slots]]
    pallas_call x0 -> x2, Pallas kernels: none -> 16.2 us  [the longest x1 11.3 us: apply_all(): pl.pallas_call(functools.partial(apply_kernel, tuple(starts)), grid_spec=...]
    ppermute x0 -> x14, starting transfers between devices: none -> 14.4 us  [the longest x1 3.42 us: per_device(): extra_all.append(lax.ppermute(extra, 'dp', pairs))]
  transfers between devices with their start and end apart: 1 -> 15, of which waited for: 1 -> 7; matrix products, arithmetic and copies ran while one was open for 0% -> 5% of each run, Pallas kernels for 0% -> 3%
where the time goes in v1:
time: 148 us; the launch traced here: 147 us
  waiting for transfers between devices  59.5 us (40%)
  blocking collectives  31.6 us (21%)
  starting transfers between devices  20.4 us (14%)
  Pallas kernels  16.2 us (11%)
  local copies, waits for them, and re-layouts  13.2 us (9%)
  other arithmetic  4.57 us (3%)
    ppermute x1, waiting for transfers between devices, per_device(): raws.append(lax.ppermute(outgoing, 'dp', pairs_of(shift)))  43 us
    all_gather x1, blocking collectives, per_device(): q_core = lax.all_gather(solved, 'shard', axis=0, tiled=True)[:slots]  31.6 us
    pallas_call x1, Pallas kernels, apply_all(): pl.pallas_call(functools.partial(apply_kernel, tuple(starts)), grid_spec=...  11.3 us
    all_to_all x1, starting transfers between devices, per_device(): lax.all_to_all(gram, 'shard', split_axis=0, concat_axis=0, tiled=True)  6.03 us
    unnamed x12, local copies, waits for them, and re-layouts  5.13 us
    pallas_call x1, Pallas kernels, newton_schulz(): pl.pallas_call(newton_kernel, out_shape=jax.ShapeDtypeStruct((items, V, V...  4.98 us
    ppermute x2, waiting for transfers between devices, spread(): lax.ppermute(array, 'dp', pairs_of(shift))  4.84 us
    ppermute x1, waiting for transfers between devices, per_device(): extra_all.append(lax.ppermute(extra, 'dp', pairs))  4.32 us
  transfers between devices with their start and end apart: 15, of which 7 were waited for; matrix products, arithmetic and copies ran while one was open for 5% of the time, Pallas kernels for 3%

profile of v1, /device:TPU:0, one launch (start us, length us, event | category | flops | bytes accessed | tf_op | source)
XLA Modules:
  0.0 147.1 jit_solution(11951016812162895825)
XLA Ops:
  0.7 3.0 %dynamic-slice_bitcast_fusion = bf16[9,896,128]{2,1,0:T(8,128)(2,1)} fusion(bf16[1,18,896,128]{3,2,1,0:T(8,128)(2,1)} %param.3, s32[]{:T(128)S(6)} %select_n.89), kind=kLoop, calls=%fused_computation.1 | loop fusion | bytes 4128772 | tf_op jit(solution)/shard_map/dynamic_slice | solution.py:156
  3.7 3.0 %collective-permute-start.1 = (bf16[9,896,128]{2,1,0:T(8,128)(2,1)}, bf16[9,896,128]{2,1,0:T(8,128)(2,1)S(1)}, u32[]{:S(2)}, u32[]{:S(2)}) collective-permute-start(bf16[9,896,128]{2,1,0:T(8,128)(2,1)} %dynamic-slice_bitcast_fusion), channel_id=1, source_target_pairs={{0,16},{8,24},{16,0},{24,8},{1,17},{9,25},{17,1},{25,9},{2,18},{10... | collective-permute-start | bytes 6193160 | tf_op jit(solution)/shard_map/ppermute | solution.py:161
  6.7 2.2 %dynamic-slice_bitcast_fusion.1 = bf16[4,896,128]{2,1,0:T(8,128)(2,1)} fusion(bf16[1,18,896,128]{3,2,1,0:T(8,128)(2,1)} %param.3, s32[]{:T(128)S(6)} %dynamic_slice.28), kind=kLoop, calls=%fused_computation.6 | loop fusion | bytes 1835012 | tf_op jit(solution)/shard_map/dynamic_slice | solution.py:164
  8.8 43.0 %collective-permute-done.1 = bf16[9,896,128]{2,1,0:T(8,128)(2,1)S(1)} collective-permute-done((bf16[9,896,128]{2,1,0:T(8,128)(2,1)}, bf16[9,896,128]{2,1,0:T(8,128)(2,1)S(1)}, u32[]{:S(2)}, u32[]{:S(2)}) %collective-permute-start.1) | collective-permute-done | bytes 2064416 | tf_op jit(solution)/shard_map/ppermute | solution.py:161
  51.8 1.0 constant_dynamic-slice_fusion
  52.8 1.0 dynamic-slice_bitcast_fusion.2
  53.7 1.3 collective-permute-start.4
  55.1 1.3 collective-permute-start.5
  56.5 0.8 collective-permute-done.4
  57.3 2.0 %collective-permute-done.5 = bf16[1,896,128]{2,1,0:T(8,128)(2,1)} collective-permute-done((bf16[1,896,128]{2,1,0:T(8,128)(2,1)S(1)}, bf16[1,896,128]{2,1,0:T(8,128)(2,1)}, u32[]{:S(2)}, u32[]{:S(2)}) %collective-permute-start.5) | collective-permute-done | bytes 229408 | tf_op jit(solution)/shard_map/ppermute | solution.py:172
  59.3 1.3 add_convert_fusion
  60.8 0.9 copy-done.2
  61.8 2.3 %fusion.1.refs_0_ = bf16[4,896,128]{2,1,0:T(8,128)(2,1)S(1)} fusion(bf16[4,896,128]{2,1,0:T(8,128)(2,1)} %collective-permute-done.2, bf16[4,896,128]{2,1,0:T(8,128)(2,1)} %copy-done.2, bf16[9,896,128]{2,1,0:T(8,128)(2,1)S(1)} %collective-permute-done.1, s32[]{:T(128)S(6)} %select_n.82, bf16[1,18,896,128]{3,2,1,0:T(8,128)(2,1)} %param.3, s32[]{:T(128)S(6)} %dynamic_slice.26), kind=kLoop, calls=%fused_computation.4 | loop fusion | flops 3670016 | bytes 4587528 | tf_op jit(solution)/shard_map/convert_element_type | solution.py:174
  64.0 0.5 fusion.6
  64.5 0.9 maximum_bitcast_fusion
  65.4 6.0 %all-to-all-start = ((f32[8,1,128,128]{3,2,1,0:T(8,128)}), f32[8,1,128,128]{3,2,1,0:T(8,128)S(1)}, u32[]{:S(2)}, u32[]{:S(2)}) async-start(f32[8,1,128,128]{3,2,1,0:T(8,128)} %maximum_bitcast_fusion), calls=%async_computation | async-start | bytes 1048576 | tf_op jit(solution)/shard_map/all_to_all | solution.py:191
  71.6 3.4 %collective-permute-start.9 = (bf16[1,896,128]{2,1,0:T(8,128)(2,1)S(1)}, bf16[1,896,128]{2,1,0:T(8,128)(2,1)S(1)}, u32[]{:S(2)}, u32[]{:S(2)}) collective-permute-start(bf16[1,896,128]{2,1,0:T(8,128)(2,1)S(1)} %add_convert_fusion), channel_id=1, source_target_pairs={{0,16},{16,0},{1,17},{17,1},{2,18},{18,2},{3,19},{19,3},{4,20},{20... | collective-permute-start | bytes 688136 | tf_op jit(solution)/shard_map/ppermute | solution.py:206
  75.0 1.3 collective-permute-start.6
  76.3 0.6 collective-permute-start.7
  76.9 0.7 gather_fusion
  77.6 4.3 %collective-permute-done.9 = bf16[1,896,128]{2,1,0:T(8,128)(2,1)S(1)} collective-permute-done((bf16[1,896,128]{2,1,0:T(8,128)(2,1)S(1)}, bf16[1,896,128]{2,1,0:T(8,128)(2,1)S(1)}, u32[]{:S(2)}, u32[]{:S(2)}) %collective-permute-start.9) | collective-permute-done | bytes 229408 | tf_op jit(solution)/shard_map/ppermute | solution.py:206
  81.9 1.3 collective-permute-start.10
  83.3 3.0 %all-to-all-done.parts_ref = f32[8,1,128,128]{3,2,1,0:T(8,128)S(1)} async-done(((f32[8,1,128,128]{3,2,1,0:T(8,128)}), f32[8,1,128,128]{3,2,1,0:T(8,128)S(1)}, u32[]{:S(2)}, u32[]{:S(2)}) %all-to-all-start) | async-done | bytes 524320 | tf_op jit(solution)/shard_map/all_to_all | solution.py:191
  86.2 0.8 copy-done.3
  87.0 5.0 %shard_map.50 = f32[1,128,128]{2,1,0:T(8,128)} custom-call(f32[8,1,128,128]{3,2,1,0:T(8,128)} %copy-done.3), custom_call_target="tpu_custom_call" | custom-call | flops 452984832 | bytes 524288 | tf_op jit(solution)/shard_map/pallas_call | solution.py:50
  92.0 31.6 %all_gather.3 = f32[8,128,128]{2,1,0:T(8,128)S(1)} all-gather(f32[1,128,128]{2,1,0:T(8,128)} %shard_map.50), channel_id=1, replica_groups=mesh['dp'=4,'shard'=8] {'shard'}, dimensions={0}, use_global_device_ids=true | all-gather | bytes 589824 | tf_op jit(solution)/shard_map/all_gather | solution.py:193
  123.6 1.6 %collective-permute-start.12 = (f32[5,128,128]{2,1,0:T(8,128)S(1)}, f32[5,128,128]{2,1,0:T(8,128)S(1)}, u32[]{:S(2)}, u32[]{:S(2)}) collective-permute-start(f32[5,128,128]{2,1,0:T(8,128)S(1)} %slice.54), channel_id=1, source_target_pairs={{0,16},{8,24},{16,0},{24,8},{1,17},{9,25},{17,1},{25,9},{2,18},{10... | collective-permute-start | bytes 983048 | tf_op jit(solution)/shard_map/ppermute | solution.py:196
  125.2 0.6 collective-permute-start.3
  125.9 4.8 %collective-permute-done.12 = f32[5,128,128]{2,1,0:T(8,128)S(1)} collective-permute-done((f32[5,128,128]{2,1,0:T(8,128)S(1)}, f32[5,128,128]{2,1,0:T(8,128)S(1)}, u32[]{:S(2)}, u32[]{:S(2)}) %collective-permute-start.12) | collective-permute-done | bytes 327712 | tf_op jit(solution)/shard_map/ppermute | solution.py:196
  130.8 1.6 %collective-permute-done.13 = f32[5,128,128]{2,1,0:T(8,128)S(1)} collective-permute-done((f32[5,128,128]{2,1,0:T(8,128)S(1)}, f32[5,128,128]{2,1,0:T(8,128)S(1)}, u32[]{:S(2)}, u32[]{:S(2)}) %collective-permute-start.13) | collective-permute-done | bytes 327712 | tf_op jit(solution)/shard_map/ppermute | solution.py:211
  132.5 3.3 %copy-done.1 = f32[18,896,128]{2,1,0:T(8,128)S(1)} copy-done((f32[18,896,128]{2,1,0:T(8,128)S(1)}, f32[18,896,128]{2,1,0:T(8,128)}, u32[]{:S(2)}) %copy-start.1) | copy-done | bytes 8257560
  135.8 11.3 %shard_map.51 = (f32[18,896,128]{2,1,0:T(8,128)}, bf16[18,896,128]{2,1,0:T(8,128)(2,1)}) custom-call(s32[18]{0:T(128)S(1)} %gather_fusion, s32[18]{0:T(128)S(1)} %iota.19.picks_ref, bf16[4,896,128]{2,1,0:T(8,128)(2,1)S(1)} %fusion.1.refs_0_, bf16[4,896,128]{2,1,0:T(8,128)(2,1)S(1)} %collective-permute-done.3.refs_1_, ...), custom_call_target="tpu_custom_call" | custom-call | flops 1056964608 | bytes 24772608 | tf_op jit(solution)/shard_map/pallas_call | solution.py:117
  (37 shorter events, 0.8 us)
Async XLA Ops:
  0.6 76.2 %copy-start = (s32[18]{0:T(128)S(1)}, s32[18]{0:T(128)}, u32[]{:S(2)}) copy-start(s32[18]{0:T(128)} %param.5) | copy-start | bytes 220
  3.7 48.1 %collective-permute-start.1 = (bf16[9,896,128]{2,1,0:T(8,128)(2,1)}, bf16[9,896,128]{2,1,0:T(8,128)(2,1)S(1)}, u32[]{:S(2)}, u32[]{:S(2)}) collective-permute-start(bf16[9,896,128]{2,1,0:T(8,128)(2,1)} %dynamic-slice_bitcast_fusion), channel_id=1, source_target_pairs={{0,16},{8,24},{16,0},{24,8},{1,17},{9,25},{17,1},{25,9},{2,18},{10... | collective-permute-start | bytes 6193160 | tf_op jit(solution)/shard_map/ppermute | solution.py:161
  8.8 52.0 %collective-permute-start = (bf16[4,896,128]{2,1,0:T(8,128)(2,1)}, bf16[4,896,128]{2,1,0:T(8,128)(2,1)S(1)}, u32[]{:S(2)}, u32[]{:S(2)}) collective-permute-start(bf16[4,896,128]{2,1,0:T(8,128)(2,1)} %dynamic-slice_bitcast_fusion.1), channel_id=1, source_target_pairs={{0,8},{8,0},{16,24},{24,16},{1,9},{9,1},{17,25},{25,17},{2,10},{10... | collective-permute-start | bytes 2752520 | tf_op jit(solution)/shard_map/ppermute | solution.py:168
  52.8 9.0 %collective-permute-start.2 = (bf16[4,896,128]{2,1,0:T(8,128)(2,1)}, bf16[4,896,128]{2,1,0:T(8,128)(2,1)}, u32[]{:S(2)}, u32[]{:S(2)}) collective-permute-start(bf16[4,896,128]{2,1,0:T(8,128)(2,1)} %constant_dynamic-slice_fusion), channel_id=1, source_target_pairs={{0,8},{8,0},{16,24},{24,16},{1,9},{9,1},{17,25},{25,17},{2,10},{10... | collective-permute-start | bytes 2752520 | tf_op jit(solution)/shard_map/ppermute | solution.py:168
  53.7 3.5 %collective-permute-start.4 = (bf16[1,896,128]{2,1,0:T(8,128)(2,1)S(1)}, bf16[1,896,128]{2,1,0:T(8,128)(2,1)}, u32[]{:S(2)}, u32[]{:S(2)}) collective-permute-start(bf16[1,896,128]{2,1,0:T(8,128)(2,1)S(1)} %dynamic-slice_bitcast_fusion.2), channel_id=1, source_target_pairs={{8,0},{24,16},{9,1},{25,17},{10,2},{26,18},{11,3},{27,19},{12,4},{... | collective-permute-start | bytes 688136 | tf_op jit(solution)/shard_map/ppermute | solution.py:172
  55.1 4.2 %collective-permute-start.5 = (bf16[1,896,128]{2,1,0:T(8,128)(2,1)S(1)}, bf16[1,896,128]{2,1,0:T(8,128)(2,1)}, u32[]{:S(2)}, u32[]{:S(2)}) collective-permute-start(bf16[1,896,128]{2,1,0:T(8,128)(2,1)S(1)} %slice.52), channel_id=1, source_target_pairs={{8,0},{24,16},{9,1},{25,17},{10,2},{26,18},{11,3},{27,19},{12,4},{... | collective-permute-start | bytes 688136 | tf_op jit(solution)/shard_map/ppermute | solution.py:172
  60.8 0.9 copy-start.2
  65.4 20.8 %all-to-all-start = ((f32[8,1,128,128]{3,2,1,0:T(8,128)}), f32[8,1,128,128]{3,2,1,0:T(8,128)S(1)}, u32[]{:S(2)}, u32[]{:S(2)}) async-start(f32[8,1,128,128]{3,2,1,0:T(8,128)} %maximum_bitcast_fusion), calls=%async_computation | async-start | bytes 1048576 | tf_op jit(solution)/shard_map/all_to_all | solution.py:191
  71.6 10.4 %collective-permute-start.9 = (bf16[1,896,128]{2,1,0:T(8,128)(2,1)S(1)}, bf16[1,896,128]{2,1,0:T(8,128)(2,1)S(1)}, u32[]{:S(2)}, u32[]{:S(2)}) collective-permute-start(bf16[1,896,128]{2,1,0:T(8,128)(2,1)S(1)} %add_convert_fusion), channel_id=1, source_target_pairs={{0,16},{16,0},{1,17},{17,1},{2,18},{18,2},{3,19},{19,3},{4,20},{20... | collective-permute-start | bytes 688136 | tf_op jit(solution)/shard_map/ppermute | solution.py:206
  75.0 8.2 %collective-permute-start.6 = (bf16[1,896,128]{2,1,0:T(8,128)(2,1)S(1)}, bf16[1,896,128]{2,1,0:T(8,128)(2,1)S(1)}, u32[]{:S(2)}, u32[]{:S(2)}) collective-permute-start(bf16[1,896,128]{2,1,0:T(8,128)(2,1)S(1)} %add_convert_fusion), channel_id=1, source_target_pairs={{0,8},{16,24},{1,9},{17,25},{2,10},{18,26},{3,11},{19,27},{4,12},{... | collective-permute-start | bytes 688136 | tf_op jit(solution)/shard_map/ppermute | solution.py:208
  76.3 49.5 %collective-permute-start.7 = (bf16[4,896,128]{2,1,0:T(8,128)(2,1)S(1)}, bf16[4,896,128]{2,1,0:T(8,128)(2,1)S(1)}, u32[]{:S(2)}, u32[]{:S(2)}) collective-permute-start(bf16[4,896,128]{2,1,0:T(8,128)(2,1)S(1)} %fusion.1.refs_0_), channel_id=1, source_target_pairs={{0,16},{8,24},{16,0},{24,8},{1,17},{9,25},{17,1},{25,9},{2,18},{10... | collective-permute-start | bytes 2752520 | tf_op jit(solution)/shard_map/ppermute | solution.py:196
  81.9 43.3 %collective-permute-start.10 = (bf16[1,896,128]{2,1,0:T(8,128)(2,1)S(1)}, bf16[1,896,128]{2,1,0:T(8,128)(2,1)S(1)}, u32[]{:S(2)}, u32[]{:S(2)}) collective-permute-start(bf16[1,896,128]{2,1,0:T(8,128)(2,1)S(1)} %collective-permute-done.9), channel_id=1, source_target_pairs={{0,8},{16,24},{1,9},{17,25},{2,10},{18,26},{3,11},{19,27},{4,12},{... | collective-permute-start | bytes 688136 | tf_op jit(solution)/shard_map/ppermute | solution.py:208
  86.2 0.8 copy-start.3
  123.6 7.1 %collective-permute-start.12 = (f32[5,128,128]{2,1,0:T(8,128)S(1)}, f32[5,128,128]{2,1,0:T(8,128)S(1)}, u32[]{:S(2)}, u32[]{:S(2)}) collective-permute-start(f32[5,128,128]{2,1,0:T(8,128)S(1)} %slice.54), channel_id=1, source_target_pairs={{0,16},{8,24},{16,0},{24,8},{1,17},{9,25},{17,1},{25,9},{2,18},{10... | collective-permute-start | bytes 983048 | tf_op jit(solution)/shard_map/ppermute | solution.py:196
  125.2 5.6 %collective-permute-start.11 = (f32[5,128,128]{2,1,0:T(8,128)S(1)}, f32[5,128,128]{2,1,0:T(8,128)S(1)}, u32[]{:S(2)}, u32[]{:S(2)}) collective-permute-start(f32[5,128,128]{2,1,0:T(8,128)S(1)} %slice.54), channel_id=1, source_target_pairs={{0,8},{8,0},{16,24},{24,16},{1,9},{9,1},{17,25},{25,17},{2,10},{10... | collective-permute-start | bytes 983048 | tf_op jit(solution)/shard_map/ppermute | solution.py:211
  125.2 7.2 %collective-permute-start.3 = (bf16[4,896,128]{2,1,0:T(8,128)(2,1)S(1)}, bf16[4,896,128]{2,1,0:T(8,128)(2,1)S(1)}, u32[]{:S(2)}, u32[]{:S(2)}) collective-permute-start(bf16[4,896,128]{2,1,0:T(8,128)(2,1)S(1)} %fusion.1.refs_0_), channel_id=1, source_target_pairs={{0,8},{8,0},{16,24},{24,16},{1,9},{9,1},{17,25},{25,17},{2,10},{10... | collective-permute-start | bytes 2752520 | tf_op jit(solution)/shard_map/ppermute | solution.py:199
  125.8 6.6 %collective-permute-start.8 = (bf16[4,896,128]{2,1,0:T(8,128)(2,1)S(1)}, bf16[4,896,128]{2,1,0:T(8,128)(2,1)S(1)}, u32[]{:S(2)}, u32[]{:S(2)}) collective-permute-start(bf16[4,896,128]{2,1,0:T(8,128)(2,1)S(1)} %collective-permute-done.7.refs_3_), channel_id=1, source_target_pairs={{0,8},{8,0},{16,24},{24,16},{1,9},{9,1},{17,25},{25,17},{2,10},{10... | collective-permute-start | bytes 2752520 | tf_op jit(solution)/shard_map/ppermute | solution.py:199
  130.8 1.6 %collective-permute-start.13 = (f32[5,128,128]{2,1,0:T(8,128)S(1)}, f32[5,128,128]{2,1,0:T(8,128)S(1)}, u32[]{:S(2)}, u32[]{:S(2)}) collective-permute-start(f32[5,128,128]{2,1,0:T(8,128)S(1)} %collective-permute-done.12), channel_id=1, source_target_pairs={{0,8},{8,0},{16,24},{24,16},{1,9},{9,1},{17,25},{25,17},{2,10},{10... | collective-permute-start | bytes 983048 | tf_op jit(solution)/shard_map/ppermute | solution.py:211
  132.5 3.3 %copy-start.1 = (f32[18,896,128]{2,1,0:T(8,128)S(1)}, f32[18,896,128]{2,1,0:T(8,128)}, u32[]{:S(2)}) copy-start(f32[18,896,128]{2,1,0:T(8,128)} %refs_7_.1) | copy-start | bytes 24772612

commit v2 on v0

v2 whole, which is shorter than its diff:
```python
import functools
import math

import jax
import jax.numpy as jnp
from jax import lax
from jax.experimental import pallas as pl
from jax.experimental.pallas import tpu as pltpu
from jax.sharding import PartitionSpec as P

D = 7168
V = 128
ITERS = 5
CORES = 2

quintic_one = 3.4445
quintic_two = -4.775
quintic_three = 2.0315
epsilon = 1e-07
learning_rate = 0.02
decay_rate = 0.1
HIGHEST = lax.Precision.HIGHEST


def dot32(left, right):
    return jnp.dot(left, right, precision=HIGHEST, preferred_element_type=jnp.float32)


def newton_kernel(gram_ref, out_ref):
    items = gram_ref.shape[0]
    rows = lax.broadcasted_iota(jnp.int32, (V, V), 0)
    columns = lax.broadcasted_iota(jnp.int32, (V, V), 1)
    eye = (rows == columns).astype(jnp.float32)
    grams, scales = [], []
    for item in range(items):
        gram = gram_ref[item]
        norm_value = jnp.sqrt(jnp.sum(gram * eye))
        scale = 1.0 / (norm_value + epsilon)
        scales.append(scale)
        grams.append((gram * scale) * scale)
    products = [None] * items
    for index in range(ITERS):
        squares = [dot32(gram, gram) for gram in grams]
        polys = [
            quintic_one * eye + quintic_two * gram + quintic_three * square
            for gram, square in zip(grams, squares)
        ]
        if index < ITERS - 1:
            halves = [dot32(gram, poly) for gram, poly in zip(grams, polys)]
        if index == 0:
            products = polys
        else:
            products = [dot32(product, poly) for product, poly in zip(products, polys)]
        if index < ITERS - 1:
            grams = [dot32(half, poly) for half, poly in zip(halves, polys)]
    for item in range(items):
        out_ref[item] = products[item] * scales[item]


def newton_schulz(gram):
    items = gram.shape[0]
    return pl.pallas_call(
        newton_kernel,
        out_shape=jax.ShapeDtypeStruct((items, V, V), jnp.float32),
        in_specs=[pl.BlockSpec(memory_space=pltpu.VMEM)],
        out_specs=pl.BlockSpec(memory_space=pltpu.VMEM),
        cost_estimate=pl.CostEstimate(
            flops=items * 18 * 12 * V**3, bytes_accessed=items * V * V * 8, transcendentals=0
        ),
        compiler_params=pltpu.CompilerParams(vmem_limit_bytes=16 * 1024 * 1024),
    )(gram)


def apply_kernel(starts, heads_ref, places_ref, picks_ref, valid_ref, *refs):
    count = len(starts) - 1
    sources = refs[:count]
    q_ref, params_ref = refs[count : count + 2]
    new_ref, update_ref = refs[-2:]
    step = pl.program_id(0)

    def work(source):
        q = q_ref[0]
        high = q.astype(jnp.bfloat16)
        low = (q - high.astype(jnp.float32)).astype(jnp.bfloat16)
        rows = source[0]
        ortho = jnp.dot(rows, high, preferred_element_type=jnp.float32)
        ortho = ortho + jnp.dot(rows, low, preferred_element_type=jnp.float32)
        ortho = ortho.astype(jnp.bfloat16).astype(jnp.float32)
        scaled = 0.2 * math.sqrt(max(D, V)) * ortho
        params = params_ref[0]
        new_ref[0] = params - learning_rate * (scaled + decay_rate * params)
        update_ref[0] = scaled.astype(jnp.bfloat16)

    for index, source in enumerate(sources):
        inside = (step >= starts[index]) & (step < starts[index + 1]) & (valid_ref[step] > 0)
        pl.when(inside)(functools.partial(work, source))


def apply_chunk(sources, q, params, previous, heads, places, picks, valid):
    count, rows, width = params.shape
    unit = sources[0].shape[1]
    starts = [0]
    for source in sources:
        starts.append(starts[-1] + source.shape[0])

    def source_map(start, items, i, *refs):
        return (jnp.clip(i - start, 0, items - 1), 0, 0)

    def head_map(i, heads_ref, places_ref, picks_ref, valid_ref):
        return (heads_ref[i], places_ref[i], 0)

    def pick_map(i, heads_ref, places_ref, picks_ref, valid_ref):
        return (picks_ref[i], 0, 0)

    in_specs = [
        pl.BlockSpec((1, unit, width), functools.partial(source_map, start, source.shape[0]))
        for start, source in zip(starts, sources)
    ]
    in_specs.append(pl.BlockSpec((1, V, V), pick_map))
    in_specs.append(pl.BlockSpec((1, unit, width), head_map))
    operands = [heads, places, picks, valid, *sources, q, params]
    aliases = {}
    for index, array in enumerate(previous):
        aliases[len(operands)] = index
        operands.append(array)
        in_specs.append(pl.BlockSpec(memory_space=pl.ANY))
    size = starts[-1] * unit * width
    return pl.pallas_call(
        functools.partial(apply_kernel, tuple(starts)),
        grid_spec=pltpu.PrefetchScalarGridSpec(
            num_scalar_prefetch=4,
            grid=(starts[-1],),
            in_specs=in_specs,
            out_specs=[pl.BlockSpec((1, unit, width), head_map)] * 2,
        ),
        out_shape=[
            jax.ShapeDtypeStruct(params.shape, jnp.float32),
            jax.ShapeDtypeStruct(params.shape, jnp.bfloat16),
        ],
        input_output_aliases=aliases,
        cost_estimate=pl.CostEstimate(flops=4 * size * V, bytes_accessed=12 * size, transcendentals=0),
        compiler_params=pltpu.CompilerParams(vmem_limit_bytes=16 * 1024 * 1024),
    )(*operands)


def chunk_sizes(own):
    if own <= 3:
        return [own]
    first = 3 if own % 2 else 2
    rest = own - first
    last = 2 if rest > 2 else 0
    return [size for size in (first, rest - last, last) if size]


def swap(array, axis, distance):
    size = lax.axis_size(axis)
    return lax.ppermute(array, axis, [(i, i ^ distance) for i in range(size)])


def gram_of(rows_array, rows):
    blocks = rows_array.reshape(-1, rows, V)
    return jnp.einsum("mrv,mrw->mvw", blocks, blocks, preferred_element_type=jnp.float32)


def per_device(grads, params, table):
    local = grads[0]
    count, rows, width = local.shape
    replicas = lax.axis_size("dp")
    groups = lax.axis_size("shard")
    members = replicas // CORES
    own = -(-count // members)
    place = lax.axis_index("dp")
    core = place % CORES
    member = place // CORES
    if members * own > count:
        filler = jnp.zeros((members * own - count, rows, width), local.dtype)
        local = jnp.concatenate([local, filler], axis=0)
    flat = local.reshape(members * own * rows, width)

    sizes = chunk_sizes(own)
    offsets = [sum(sizes[:k]) for k in range(len(sizes))]

    sums = []
    for size, offset in zip(sizes, offsets):
        share = size * rows // CORES

        def part_of(index):
            start = ((index // CORES) * own + offset) * rows + (index % CORES) * share
            return lax.dynamic_slice_in_dim(flat, start, share, axis=0)

        terms = [part_of(place)]
        for distance in range(1, replicas):
            terms.append(swap(part_of(place ^ distance), "dp", distance))
        terms = [term.astype(jnp.float32) for term in terms]
        while len(terms) > 1:
            terms = [left + right for left, right in zip(terms[::2], terms[1::2])]
        sums.append(terms[0].astype(jnp.bfloat16))

    qs = []
    for size, total in zip(sizes, sums):
        if size % 2:
            whole = size // 2
            half = lax.dynamic_slice_in_dim(total, (1 - core) * whole * rows, rows // 2, axis=0)
            gram = gram_of(half, rows // 2)
            gram = gram + swap(gram, "dp", 1)
            if whole:
                full = lax.dynamic_slice_in_dim(total, core * (rows // 2), whole * rows, axis=0)
                gram = jnp.concatenate([gram_of(full, rows), gram], axis=0)
        else:
            gram = gram_of(total, rows)
        distance = 1
        while distance < groups:
            gram = gram + swap(gram, "shard", distance)
            distance *= 2
        qs.append(newton_schulz(gram))

    def spread(array):
        result = []
        for distance in range(members):
            mine = swap(array, "dp", distance * CORES) if distance else array
            result.append(mine)
            result.append(swap(mine, "dp", 1))
        return result

    outputs = []
    for size, offset, total, q in zip(sizes, offsets, sums, qs):
        per_block = 2 if size % 2 else 1
        units = size * per_block // CORES
        sources = [array.reshape(units, rows // per_block, width) for array in spread(total)]
        q_all = jnp.concatenate(spread(q), axis=0)
        slots = q.shape[0]
        shape = (members, CORES, units)
        distance = lax.broadcasted_iota(jnp.int32, shape, 0)
        other = lax.broadcasted_iota(jnp.int32, shape, 1)
        unit = lax.broadcasted_iota(jnp.int32, shape, 2)
        holder = core ^ other
        within = holder * units + unit
        block = within // per_block
        places = (within % per_block).reshape(-1)
        slot = block - holder * slots
        if size % 2:
            slot = jnp.where(block == size // 2, slots - 1, slot)
        picks = ((distance * CORES + other) * slots + slot).reshape(-1)
        block = ((member ^ distance) * own + offset + block).reshape(-1)
        valid = block < count
        heads = table[jnp.minimum(block, count - 1)]
        if members * own > count:
            order = jnp.arange(valid.shape[0], dtype=jnp.int32)
            latest = lax.cummax(jnp.where(valid, order, -1))
            latest = jnp.where(latest < 0, jnp.argmax(valid).astype(jnp.int32), latest)
            heads, places = heads[latest], places[latest]
        outputs = apply_chunk(
            sources, q_all, params, outputs, heads, places, picks, valid.astype(jnp.int32)
        )
    new_params, update = outputs
    return (new_params, update)


def solution(mesh):
    return jax.shard_map(
        per_device,
        mesh=mesh,
        in_specs=(P("dp", None, "shard", None), P(None, "shard", None), P()),
        out_specs=(P(None, "shard", None), P(None, "shard", None)),
        check_vma=False,
    )
```

time: 599 us -> 132 us (0.22)
  blocking collectives: 274 us -> 0 us
  matrix products: 152 us -> 1.06 us
  waiting for transfers between devices: 121 us -> 39.3 us
  starting transfers between devices: 4.85 us -> 32.3 us
  Pallas kernels: 0 us -> 26.1 us
  other arithmetic: 21.3 us -> 10.3 us
    dot_general x15 -> x4, matrix products: 152 us -> 1.06 us  [gram_of(): jnp.einsum('mrv,mrw->mvw', blocks, blocks, preferred_element_type=jnp.flo...]
    psum x1 -> x0, blocking collectives: 147 us -> none  [per_device(): total = lax.psum(grads[0].astype(jnp.float32), 'dp')]
    all_to_all x1 -> x0, blocking collectives: 127 us -> none  [per_device(): lax.all_to_all(outgoing, 'shard', split_axis=1, concat_axis=1, tiled=True)]
    all_to_all x1 -> x0, waiting for transfers between devices: 121 us -> none  [per_device(): lax.all_to_all(result, 'shard', split_axis=1, concat_axis=1, tiled=True)]
    ppermute x0 -> x37, waiting for transfers between devices: none -> 39.3 us  [swap(): return lax.ppermute(array, axis, [(i, i ^ distance) for i in range(size)])]
    ppermute x0 -> x37, starting transfers between devices: none -> 32.3 us  [swap(): return lax.ppermute(array, axis, [(i, i ^ distance) for i in range(size)])]
    pallas_call x0 -> x6, Pallas kernels: none -> 26.1 us  [the longest x3 15.4 us: apply_chunk(): pl.pallas_call(functools.partial(apply_kernel, tuple(starts)), grid_spec=...]
    convert_element_type x2 -> x6, other arithmetic: 14.8 us -> 4.7 us  [the longest x3 3.93 us: per_device(): sums.append(terms[0].astype(jnp.bfloat16))]
  transfers between devices with their start and end apart: 1 -> 37, of which waited for: 1 -> 12; matrix products, arithmetic and copies ran while one was open for 0% -> 17% of each run, Pallas kernels for 0% -> 17%
where the time goes in v2:
time: 132 us
  waiting for transfers between devices  39.3 us (30%)
  starting transfers between devices  32.3 us (24%)
  Pallas kernels  26.1 us (20%)
  local copies, waits for them, and re-layouts  21.6 us (16%)
  other arithmetic  10.3 us (8%)
    ppermute x37, waiting for transfers between devices, swap(): return lax.ppermute(array, axis, [(i, i ^ distance) for i in range(size)])  39.3 us
    ppermute x37, starting transfers between devices, swap(): return lax.ppermute(array, axis, [(i, i ^ distance) for i in range(size)])  32.3 us
    pallas_call x3, Pallas kernels, apply_chunk(): pl.pallas_call(functools.partial(apply_kernel, tuple(starts)), grid_spec=...  15.4 us
    pallas_call x3, Pallas kernels, newton_schulz(): pl.pallas_call(newton_kernel, out_shape=jax.ShapeDtypeStruct((items, V, V...  10.7 us
    unnamed x42, local copies, waits for them, and re-layouts  8.78 us
    dynamic_slice x3, local copies, waits for them, and re-layouts, part_of(): return lax.dynamic_slice_in_dim(flat, start, share, axis=0)  4.69 us
    convert_element_type x3, other arithmetic, per_device(): sums.append(terms[0].astype(jnp.bfloat16))  3.93 us
    concatenate x3, other arithmetic, per_device(): q_all = jnp.concatenate(spread(q), axis=0)  3.07 us
  transfers between devices with their start and end apart: 37, of which 12 were waited for; matrix products, arithmetic and copies ran while one was open for 17% of the time, Pallas kernels for 17%

profile of v2, /device:TPU:0, one launch (start us, length us, event | category | flops | bytes accessed | tf_op | source)
XLA Modules:
  0.0 131.8 jit_solution(14277791912101155336)
XLA Ops:
  0.8 2.1 %constant_dynamic-slice_fusion.2 = (bf16[1344,128]{1,0:T(8,128)(2,1)S(1)}, bf16[1344,128]{1,0:T(8,128)(2,1)}, bf16[1344,128]{1,0:T(8,128)(2,1)}) fusion(bf16[16128,128]{1,0:T(8,128)(2,1)} %bitcast.48, s32[]{:T(128)S(6)} %select_n.218, s32[]{:T(128)S(6)} %select_n.220, s32[]{:T(128)S(6)} %select_n.219), kind=kLoop, calls=%fused_computation.23 | loop fusion | bytes 2064396 | tf_op jit(solution)/shard_map/dynamic_slice | solution.py:189
  3.3 2.5 %collective-permute-start.25 = (bf16[1344,128]{1,0:T(8,128)(2,1)}, bf16[1344,128]{1,0:T(8,128)(2,1)}, u32[]{:S(2)}, u32[]{:S(2)}) collective-permute-start(bf16[1344,128]{1,0:T(8,128)(2,1)} %get-tuple-element.14), channel_id=1, source_target_pairs={{0,16},{8,24},{16,0},{24,8},{1,17},{9,25},{17,1},{25,9},{2,18},{10... | collective-permute-start | bytes 1032200 | tf_op jit(solution)/shard_map/ppermute | solution.py:157
  10.5 1.4 %constant_dynamic-slice_fusion.5 = (bf16[1792,128]{1,0:T(8,128)(2,1)S(1)}, bf16[1792,128]{1,0:T(8,128)(2,1)S(1)}, bf16[1792,128]{1,0:T(8,128)(2,1)S(1)}) fusion(bf16[16128,128]{1,0:T(8,128)(2,1)} %bitcast.50, s32[]{:T(128)S(6)} %select_n.207, s32[]{:T(128)S(6)} %select_n.209, s32[]{:T(128)S(6)} %select_n.208), kind=kLoop, calls=%fused_computation.26 | loop fusion | bytes 2752524 | tf_op jit(solution)/shard_map/dynamic_slice | solution.py:189
  13.7 6.1 %collective-permute-done.1 = bf16[896,128]{1,0:T(8,128)(2,1)S(1)} collective-permute-done((bf16[896,128]{1,0:T(8,128)(2,1)S(1)}, bf16[896,128]{1,0:T(8,128)(2,1)S(1)}, u32[]{:S(2)}, u32[]{:S(2)}) %collective-permute-start.1) | collective-permute-done | bytes 229408 | tf_op jit(solution)/shard_map/ppermute | solution.py:157
  20.6 3.9 %collective-permute-done.2 = bf16[896,128]{1,0:T(8,128)(2,1)S(1)} collective-permute-done((bf16[896,128]{1,0:T(8,128)(2,1)S(1)}, bf16[896,128]{1,0:T(8,128)(2,1)S(1)}, u32[]{:S(2)}, u32[]{:S(2)}) %collective-permute-start.2) | collective-permute-done | bytes 229408 | tf_op jit(solution)/shard_map/ppermute | solution.py:157
  25.1 1.5 %collective-permute-start.13 = (bf16[1792,128]{1,0:T(8,128)(2,1)S(1)}, bf16[1792,128]{1,0:T(8,128)(2,1)S(1)}, u32[]{:S(2)}, u32[]{:S(2)}) collective-permute-start(bf16[1792,128]{1,0:T(8,128)(2,1)S(1)} %get-tuple-element.17), channel_id=1, source_target_pairs={{0,16},{8,24},{16,0},{24,8},{1,17},{9,25},{17,1},{25,9},{2,18},{10... | collective-permute-start | bytes 1376264 | tf_op jit(solution)/shard_map/ppermute | solution.py:157
  28.8 1.7 %collective-permute-start.6 = (f32[1,128,128]{2,1,0:T(8,128)S(1)}, f32[1,128,128]{2,1,0:T(8,128)S(1)}, u32[]{:S(2)}, u32[]{:S(2)}) collective-permute-start(f32[1,128,128]{2,1,0:T(8,128)S(1)} %convolution_bitcast_fusion.2), channel_id=1, source_target_pairs={{0,1},{1,0},{2,3},{3,2},{4,5},{5,4},{6,7},{7,6},{8,9},{9,8},{10,11... | collective-permute-start | bytes 196616 | tf_op jit(solution)/shard_map/ppermute | solution.py:157
  31.8 1.4 %add_convert_fusion.1 = bf16[1344,128]{1,0:T(8,128)(2,1)S(1)} fusion(bf16[1344,128]{1,0:T(8,128)(2,1)S(1)} %collective-permute-done.26, bf16[1344,128]{1,0:T(8,128)(2,1)} %collective-permute-done.25, bf16[1344,128]{1,0:T(8,128)(2,1)} %copy-done.6, bf16[16128,128]{1,0:T(8,128)(2,1)} %bitcast.52, s32[]{:T(128)S(6)} %select_n.217), kind=kLoop, calls=%fused_computation.7 | loop fusion | flops 1376256 | bytes 1720324 | tf_op jit(solution)/shard_map/convert_element_type | solution.py:197
  36.9 2.4 %collective-permute-start.7 = (f32[1,128,128]{2,1,0:T(8,128)S(1)}, f32[1,128,128]{2,1,0:T(8,128)S(1)}, u32[]{:S(2)}, u32[]{:S(2)}) collective-permute-start(f32[1,128,128]{2,1,0:T(8,128)S(1)} %add.424), channel_id=1, source_target_pairs={{0,2},{1,3},{2,0},{3,1},{4,6},{5,7},{6,4},{7,5},{8,10},{9,11},{10,... | collective-permute-start | bytes 196616 | tf_op jit(solution)/shard_map/ppermute | solution.py:157
  40.4 1.6 %collective-permute-start.31 = (f32[2,128,128]{2,1,0:T(8,128)S(1)}, f32[2,128,128]{2,1,0:T(8,128)S(1)}, u32[]{:S(2)}, u32[]{:S(2)}) collective-permute-start(f32[2,128,128]{2,1,0:T(8,128)S(1)} %pad_maximum_fusion.3), channel_id=1, source_target_pairs={{0,1},{1,0},{2,3},{3,2},{4,5},{5,4},{6,7},{7,6},{8,9},{9,8},{10,11... | collective-permute-start | bytes 393224 | tf_op jit(solution)/shard_map/ppermute | solution.py:157
  42.0 9.5 %collective-permute-done.14 = bf16[1792,128]{1,0:T(8,128)(2,1)S(1)} collective-permute-done((bf16[1792,128]{1,0:T(8,128)(2,1)S(1)}, bf16[1792,128]{1,0:T(8,128)(2,1)S(1)}, u32[]{:S(2)}, u32[]{:S(2)}) %collective-permute-start.14) | collective-permute-done | bytes 458784 | tf_op jit(solution)/shard_map/ppermute | solution.py:157
  53.1 1.6 %collective-permute-start.18 = (f32[2,128,128]{2,1,0:T(8,128)S(1)}, f32[2,128,128]{2,1,0:T(8,128)S(1)}, u32[]{:S(2)}, u32[]{:S(2)}) collective-permute-start(f32[2,128,128]{2,1,0:T(8,128)S(1)} %fusion.10), channel_id=1, source_target_pairs={{0,1},{1,0},{2,3},{3,2},{4,5},{5,4},{6,7},{7,6},{8,9},{9,8},{10,11... | collective-permute-start | bytes 393224 | tf_op jit(solution)/shard_map/ppermute | solution.py:157
  54.7 1.6 %collective-permute-start.32 = (f32[2,128,128]{2,1,0:T(8,128)S(1)}, f32[2,128,128]{2,1,0:T(8,128)S(1)}, u32[]{:S(2)}, u32[]{:S(2)}) collective-permute-start(f32[2,128,128]{2,1,0:T(8,128)S(1)} %fusion.9), channel_id=1, source_target_pairs={{0,2},{1,3},{2,0},{3,1},{4,6},{5,7},{6,4},{7,5},{8,10},{9,11},{10,... | collective-permute-start | bytes 393224 | tf_op jit(solution)/shard_map/ppermute | solution.py:157
  56.3 2.7 %collective-permute-start.8 = (f32[1,128,128]{2,1,0:T(8,128)S(1)}, f32[1,128,128]{2,1,0:T(8,128)S(1)}, u32[]{:S(2)}, u32[]{:S(2)}) collective-permute-start(f32[1,128,128]{2,1,0:T(8,128)S(1)} %add.425), channel_id=1, source_target_pairs={{0,4},{1,5},{2,6},{3,7},{4,0},{5,1},{6,2},{7,3},{8,12},{9,13},{10,... | collective-permute-start | bytes 196616 | tf_op jit(solution)/shard_map/ppermute | solution.py:157
  59.0 1.4 %collective-permute-start.19 = (f32[2,128,128]{2,1,0:T(8,128)S(1)}, f32[2,128,128]{2,1,0:T(8,128)S(1)}, u32[]{:S(2)}, u32[]{:S(2)}) collective-permute-start(f32[2,128,128]{2,1,0:T(8,128)S(1)} %add.450), channel_id=1, source_target_pairs={{0,2},{1,3},{2,0},{3,1},{4,6},{5,7},{6,4},{7,5},{8,10},{9,11},{10,... | collective-permute-start | bytes 393224 | tf_op jit(solution)/shard_map/ppermute | solution.py:157
  60.8 2.7 %collective-permute-start.33 = (f32[2,128,128]{2,1,0:T(8,128)S(1)}, f32[2,128,128]{2,1,0:T(8,128)S(1)}, u32[]{:S(2)}, u32[]{:S(2)}) collective-permute-start(f32[2,128,128]{2,1,0:T(8,128)S(1)} %fusion.15), channel_id=1, source_target_pairs={{0,4},{1,5},{2,6},{3,7},{4,0},{5,1},{6,2},{7,3},{8,12},{9,13},{10,... | collective-permute-start | bytes 393224 | tf_op jit(solution)/shard_map/ppermute | solution.py:157
  63.5 1.5 %collective-permute-start.4 = (bf16[896,128]{1,0:T(8,128)(2,1)S(1)}, bf16[896,128]{1,0:T(8,128)(2,1)S(1)}, u32[]{:S(2)}, u32[]{:S(2)}) collective-permute-start(bf16[896,128]{1,0:T(8,128)(2,1)S(1)} %add_convert_fusion.2), channel_id=1, source_target_pairs={{0,16},{8,24},{16,0},{24,8},{1,17},{9,25},{17,1},{25,9},{2,18},{10... | collective-permute-start | bytes 688136 | tf_op jit(solution)/shard_map/ppermute | solution.py:157
  66.3 1.6 %collective-permute-start.16 = (bf16[1792,128]{1,0:T(8,128)(2,1)S(1)}, bf16[1792,128]{1,0:T(8,128)(2,1)S(1)}, u32[]{:S(2)}, u32[]{:S(2)}) collective-permute-start(bf16[1792,128]{1,0:T(8,128)(2,1)S(1)} %add_convert_fusion), channel_id=1, source_target_pairs={{0,16},{8,24},{16,0},{24,8},{1,17},{9,25},{17,1},{25,9},{2,18},{10... | collective-permute-start | bytes 1376264 | tf_op jit(solution)/shard_map/ppermute | solution.py:157
  67.9 1.6 %collective-permute-done.33 = f32[2,128,128]{2,1,0:T(8,128)S(1)} collective-permute-done((f32[2,128,128]{2,1,0:T(8,128)S(1)}, f32[2,128,128]{2,1,0:T(8,128)S(1)}, u32[]{:S(2)}, u32[]{:S(2)}) %collective-permute-start.33) | collective-permute-done | bytes 131104 | tf_op jit(solution)/shard_map/ppermute | solution.py:157
  69.7 3.3 %shard_map.50 = f32[1,128,128]{2,1,0:T(8,128)S(1)} custom-call(f32[1,128,128]{2,1,0:T(8,128)S(1)} %add.426.gram_ref), custom_call_target="tpu_custom_call" | custom-call | flops 452984832 | bytes 131072 | tf_op jit(solution)/shard_map/pallas_call | solution.py:62
  73.1 4.2 %collective-permute-done.20 = f32[2,128,128]{2,1,0:T(8,128)S(1)} collective-permute-done((f32[2,128,128]{2,1,0:T(8,128)S(1)}, f32[2,128,128]{2,1,0:T(8,128)S(1)}, u32[]{:S(2)}, u32[]{:S(2)}) %collective-permute-start.20) | collective-permute-done | bytes 131104 | tf_op jit(solution)/shard_map/ppermute | solution.py:157
  78.3 3.4 %shard_map.52 = f32[2,128,128]{2,1,0:T(8,128)S(1)} custom-call(f32[2,128,128]{2,1,0:T(8,128)S(1)} %add.478.gram_ref), custom_call_target="tpu_custom_call" | custom-call | flops 905969664 | bytes 262144 | tf_op jit(solution)/shard_map/pallas_call | solution.py:62
  81.8 6.3 %collective-permute-done.10 = f32[1,128,128]{2,1,0:T(8,128)S(1)} collective-permute-done((f32[1,128,128]{2,1,0:T(8,128)S(1)}, f32[1,128,128]{2,1,0:T(8,128)S(1)}, u32[]{:S(2)}, u32[]{:S(2)}) %collective-permute-start.10) | collective-permute-done | bytes 65568 | tf_op jit(solution)/shard_map/ppermute | solution.py:157
  88.1 4.0 %shard_map.51 = f32[2,128,128]{2,1,0:T(8,128)} custom-call(f32[2,128,128]{2,1,0:T(8,128)S(1)} %add.452.gram_ref), custom_call_target="tpu_custom_call" | custom-call | flops 905969664 | bytes 262144 | tf_op jit(solution)/shard_map/pallas_call | solution.py:62
  92.7 1.5 %collective-permute-start.35 = (f32[2,128,128]{2,1,0:T(8,128)S(1)}, f32[2,128,128]{2,1,0:T(8,128)}, u32[]{:S(2)}, u32[]{:S(2)}) collective-permute-start(f32[2,128,128]{2,1,0:T(8,128)S(1)} %shard_map.52), channel_id=1, source_target_pairs={{0,16},{8,24},{16,0},{24,8},{1,17},{9,25},{17,1},{25,9},{2,18},{10... | collective-permute-start | bytes 393224 | tf_op jit(solution)/shard_map/ppermute | solution.py:157
  95.1 3.7 %collective-permute-done.35 = f32[2,128,128]{2,1,0:T(8,128)} collective-permute-done((f32[2,128,128]{2,1,0:T(8,128)S(1)}, f32[2,128,128]{2,1,0:T(8,128)}, u32[]{:S(2)}, u32[]{:S(2)}) %collective-permute-start.35) | collective-permute-done | bytes 131104 | tf_op jit(solution)/shard_map/ppermute | solution.py:157
  99.4 1.5 %collective-permute-done.22 = f32[2,128,128]{2,1,0:T(8,128)S(1)} collective-permute-done((f32[2,128,128]{2,1,0:T(8,128)}, f32[2,128,128]{2,1,0:T(8,128)S(1)}, u32[]{:S(2)}, u32[]{:S(2)}) %collective-permute-start.22) | collective-permute-done | bytes 131104 | tf_op jit(solution)/shard_map/ppermute | solution.py:157
  108.6 3.3 %copy-done.1 = f32[18,896,128]{2,1,0:T(8,128)S(1)} copy-done((f32[18,896,128]{2,1,0:T(8,128)S(1)}, f32[18,896,128]{2,1,0:T(8,128)}, u32[]{:S(2)}) %copy-start.1) | copy-done | bytes 8257560
  112.0 6.7 %shard_map.53 = (f32[18,896,128]{2,1,0:T(8,128)}, bf16[18,896,128]{2,1,0:T(8,128)(2,1)}) custom-call(s32[12]{0:T(128)S(1)} %gather_fusion.2, s32[12]{0:T(128)S(1)} %and_select_fusion.1.places_ref, s32[12]{0:T(128)S(1)} %fusion.5.picks_ref, s32[12]{0:T(128)S(1)} %get-tuple-element.10.valid_ref, bf16[3,448,128]{2,1,0:T(8,128)(2,1)S(1)} %bitcast.38, ...), custom_call_target="tpu_custom_call" | custom-call | flops 352321536 | bytes 8257536 | tf_op jit(solution)/shard_map/pallas_call | solution.py:128
  119.7 3.3 %copy-done.2 = f32[18,896,128]{2,1,0:T(8,128)S(1)} copy-done((f32[18,896,128]{2,1,0:T(8,128)S(1)}, f32[18,896,128]{2,1,0:T(8,128)}, u32[]{:S(2)}) %copy-start.2) | copy-done | bytes 8257560
  123.0 5.5 %shard_map.54 = (f32[18,896,128]{2,1,0:T(8,128)}, bf16[18,896,128]{2,1,0:T(8,128)(2,1)}) custom-call(s32[8]{0:T(128)S(1)} %gather_fusion.1, s32[8]{0:T(128)S(1)} %rem.162.places_ref, s32[8]{0:T(128)S(1)} %add.433.picks_ref, s32[8]{0:T(128)S(1)} %reshape.396.valid_ref, ...), custom_call_target="tpu_custom_call", output_to_operand_aliasing={{0}: (10, {}), {1}: (11, {})} | custom-call | flops 469762048 | bytes 11010048 | tf_op jit(solution)/shard_map/pallas_call | solution.py:128
  128.6 3.2 %shard_map.55 = (f32[18,896,128]{2,1,0:T(8,128)}, bf16[18,896,128]{2,1,0:T(8,128)(2,1)}) custom-call(s32[4]{0:T(128)S(1)} %gather_fusion, s32[4]{0:T(128)S(1)} %iota.93.places_ref, s32[4]{0:T(128)S(1)} %add.403.picks_ref, s32[4]{0:T(128)S(1)} %compare_convert_fusion.2.valid_ref, ...), custom_call_target="tpu_custom_call", output_to_operand_aliasing={{0}: (10, {}), {1}: (11, {})} | custom-call | flops 234881024 | bytes 5505024 | tf_op jit(solution)/shard_map/pallas_call | solution.py:128
  (161 shorter events, 31.9 us)
Async XLA Ops:
  2.9 25.3 %collective-permute-start.24 = (bf16[1344,128]{1,0:T(8,128)(2,1)S(1)}, bf16[1344,128]{1,0:T(8,128)(2,1)S(1)}, u32[]{:S(2)}, u32[]{:S(2)}) collective-permute-start(bf16[1344,128]{1,0:T(8,128)(2,1)S(1)} %get-tuple-element.12), channel_id=1, source_target_pairs={{0,8},{8,0},{16,24},{24,16},{1,9},{9,1},{17,25},{25,17},{2,10},{10... | collective-permute-start | bytes 1032200 | tf_op jit(solution)/shard_map/ppermute | solution.py:157
  3.3 25.5 %collective-permute-start.25 = (bf16[1344,128]{1,0:T(8,128)(2,1)}, bf16[1344,128]{1,0:T(8,128)(2,1)}, u32[]{:S(2)}, u32[]{:S(2)}) collective-permute-start(bf16[1344,128]{1,0:T(8,128)(2,1)} %get-tuple-element.14), channel_id=1, source_target_pairs={{0,16},{8,24},{16,0},{24,8},{1,17},{9,25},{17,1},{25,9},{2,18},{10... | collective-permute-start | bytes 1032200 | tf_op jit(solution)/shard_map/ppermute | solution.py:157
  7.0 6.3 %collective-permute-start = (bf16[896,128]{1,0:T(8,128)(2,1)S(1)}, bf16[896,128]{1,0:T(8,128)(2,1)S(1)}, u32[]{:S(2)}, u32[]{:S(2)}) collective-permute-start(bf16[896,128]{1,0:T(8,128)(2,1)S(1)} %get-tuple-element.18), channel_id=1, source_target_pairs={{0,8},{8,0},{16,24},{24,16},{1,9},{9,1},{17,25},{25,17},{2,10},{10... | collective-permute-start | bytes 688136 | tf_op jit(solution)/shard_map/ppermute | solution.py:157
  7.3 12.5 %collective-permute-start.1 = (bf16[896,128]{1,0:T(8,128)(2,1)S(1)}, bf16[896,128]{1,0:T(8,128)(2,1)S(1)}, u32[]{:S(2)}, u32[]{:S(2)}) collective-permute-start(bf16[896,128]{1,0:T(8,128)(2,1)S(1)} %get-tuple-element.20), channel_id=1, source_target_pairs={{0,16},{8,24},{16,0},{24,8},{1,17},{9,25},{17,1},{25,9},{2,18},{10... | collective-permute-start | bytes 688136 | tf_op jit(solution)/shard_map/ppermute | solution.py:157
  7.6 16.8 %collective-permute-start.2 = (bf16[896,128]{1,0:T(8,128)(2,1)S(1)}, bf16[896,128]{1,0:T(8,128)(2,1)S(1)}, u32[]{:S(2)}, u32[]{:S(2)}) collective-permute-start(bf16[896,128]{1,0:T(8,128)(2,1)S(1)} %get-tuple-element.19), channel_id=1, source_target_pairs={{0,24},{8,16},{16,8},{24,0},{1,25},{9,17},{17,9},{25,1},{2,26},{10... | collective-permute-start | bytes 688136 | tf_op jit(solution)/shard_map/ppermute | solution.py:157
  13.3 18.5 %collective-permute-start.26 = (bf16[1344,128]{1,0:T(8,128)(2,1)}, bf16[1344,128]{1,0:T(8,128)(2,1)S(1)}, u32[]{:S(2)}, u32[]{:S(2)}) collective-permute-start(bf16[1344,128]{1,0:T(8,128)(2,1)} %get-tuple-element.13), channel_id=1, source_target_pairs={{0,24},{8,16},{16,8},{24,0},{1,25},{9,17},{17,9},{25,1},{2,26},{10... | collective-permute-start | bytes 1032200 | tf_op jit(solution)/shard_map/ppermute | solution.py:157
  20.6 21.4 %collective-permute-start.12 = (bf16[1792,128]{1,0:T(8,128)(2,1)S(1)}, bf16[1792,128]{1,0:T(8,128)(2,1)S(1)}, u32[]{:S(2)}, u32[]{:S(2)}) collective-permute-start(bf16[1792,128]{1,0:T(8,128)(2,1)S(1)} %get-tuple-element.15), channel_id=1, source_target_pairs={{0,8},{8,0},{16,24},{24,16},{1,9},{9,1},{17,25},{25,17},{2,10},{10... | collective-permute-start | bytes 1376264 | tf_op jit(solution)/shard_map/ppermute | solution.py:157
  25.1 16.9 %collective-permute-start.13 = (bf16[1792,128]{1,0:T(8,128)(2,1)S(1)}, bf16[1792,128]{1,0:T(8,128)(2,1)S(1)}, u32[]{:S(2)}, u32[]{:S(2)}) collective-permute-start(bf16[1792,128]{1,0:T(8,128)(2,1)S(1)} %get-tuple-element.17), channel_id=1, source_target_pairs={{0,16},{8,24},{16,0},{24,8},{1,17},{9,25},{17,1},{25,9},{2,18},{10... | collective-permute-start | bytes 1376264 | tf_op jit(solution)/shard_map/ppermute | solution.py:157
  28.2 23.2 %collective-permute-start.14 = (bf16[1792,128]{1,0:T(8,128)(2,1)S(1)}, bf16[1792,128]{1,0:T(8,128)(2,1)S(1)}, u32[]{:S(2)}, u32[]{:S(2)}) collective-permute-start(bf16[1792,128]{1,0:T(8,128)(2,1)S(1)} %get-tuple-element.16), channel_id=1, source_target_pairs={{0,24},{8,16},{16,8},{24,0},{1,25},{9,17},{17,9},{25,1},{2,26},{10... | collective-permute-start | bytes 1376264 | tf_op jit(solution)/shard_map/ppermute | solution.py:157
  28.8 8.0 %collective-permute-start.6 = (f32[1,128,128]{2,1,0:T(8,128)S(1)}, f32[1,128,128]{2,1,0:T(8,128)S(1)}, u32[]{:S(2)}, u32[]{:S(2)}) collective-permute-start(f32[1,128,128]{2,1,0:T(8,128)S(1)} %convolution_bitcast_fusion.2), channel_id=1, source_target_pairs={{0,1},{1,0},{2,3},{3,2},{4,5},{5,4},{6,7},{7,6},{8,9},{9,8},{10,11... | collective-permute-start | bytes 196616 | tf_op jit(solution)/shard_map/ppermute | solution.py:157
  36.9 19.4 %collective-permute-start.7 = (f32[1,128,128]{2,1,0:T(8,128)S(1)}, f32[1,128,128]{2,1,0:T(8,128)S(1)}, u32[]{:S(2)}, u32[]{:S(2)}) collective-permute-start(f32[1,128,128]{2,1,0:T(8,128)S(1)} %add.424), channel_id=1, source_target_pairs={{0,2},{1,3},{2,0},{3,1},{4,6},{5,7},{6,4},{7,5},{8,10},{9,11},{10,... | collective-permute-start | bytes 196616 | tf_op jit(solution)/shard_map/ppermute | solution.py:157
  40.4 14.3 %collective-permute-start.31 = (f32[2,128,128]{2,1,0:T(8,128)S(1)}, f32[2,128,128]{2,1,0:T(8,128)S(1)}, u32[]{:S(2)}, u32[]{:S(2)}) collective-permute-start(f32[2,128,128]{2,1,0:T(8,128)S(1)} %pad_maximum_fusion.3), channel_id=1, source_target_pairs={{0,1},{1,0},{2,3},{3,2},{4,5},{5,4},{6,7},{7,6},{8,9},{9,8},{10,11... | collective-permute-start | bytes 393224 | tf_op jit(solution)/shard_map/ppermute | solution.py:157
  56.3 10.0 %collective-permute-start.8 = (f32[1,128,128]{2,1,0:T(8,128)S(1)}, f32[1,128,128]{2,1,0:T(8,128)S(1)}, u32[]{:S(2)}, u32[]{:S(2)}) collective-permute-start(f32[1,128,128]{2,1,0:T(8,128)S(1)} %add.425), channel_id=1, source_target_pairs={{0,4},{1,5},{2,6},{3,7},{4,0},{5,1},{6,2},{7,3},{8,12},{9,13},{10,... | collective-permute-start | bytes 196616 | tf_op jit(solution)/shard_map/ppermute | solution.py:157
  59.0 7.2 %collective-permute-start.19 = (f32[2,128,128]{2,1,0:T(8,128)S(1)}, f32[2,128,128]{2,1,0:T(8,128)S(1)}, u32[]{:S(2)}, u32[]{:S(2)}) collective-permute-start(f32[2,128,128]{2,1,0:T(8,128)S(1)} %add.450), channel_id=1, source_target_pairs={{0,2},{1,3},{2,0},{3,1},{4,6},{5,7},{6,4},{7,5},{8,10},{9,11},{10,... | collective-permute-start | bytes 393224 | tf_op jit(solution)/shard_map/ppermute | solution.py:157
  60.8 8.7 %collective-permute-start.33 = (f32[2,128,128]{2,1,0:T(8,128)S(1)}, f32[2,128,128]{2,1,0:T(8,128)S(1)}, u32[]{:S(2)}, u32[]{:S(2)}) collective-permute-start(f32[2,128,128]{2,1,0:T(8,128)S(1)} %fusion.15), channel_id=1, source_target_pairs={{0,4},{1,5},{2,6},{3,7},{4,0},{5,1},{6,2},{7,3},{8,12},{9,13},{10,... | collective-permute-start | bytes 393224 | tf_op jit(solution)/shard_map/ppermute | solution.py:157
  63.5 18.2 %collective-permute-start.4 = (bf16[896,128]{1,0:T(8,128)(2,1)S(1)}, bf16[896,128]{1,0:T(8,128)(2,1)S(1)}, u32[]{:S(2)}, u32[]{:S(2)}) collective-permute-start(bf16[896,128]{1,0:T(8,128)(2,1)S(1)} %add_convert_fusion.2), channel_id=1, source_target_pairs={{0,16},{8,24},{16,0},{24,8},{1,17},{9,25},{17,1},{25,9},{2,18},{10... | collective-permute-start | bytes 688136 | tf_op jit(solution)/shard_map/ppermute | solution.py:157
  65.0 27.1 %collective-permute-start.28 = (bf16[1344,128]{1,0:T(8,128)(2,1)S(1)}, bf16[1344,128]{1,0:T(8,128)(2,1)S(1)}, u32[]{:S(2)}, u32[]{:S(2)}) collective-permute-start(bf16[1344,128]{1,0:T(8,128)(2,1)S(1)} %add_convert_fusion.1), channel_id=1, source_target_pairs={{0,16},{8,24},{16,0},{24,8},{1,17},{9,25},{17,1},{25,9},{2,18},{10... | collective-permute-start | bytes 1032200 | tf_op jit(solution)/shard_map/ppermute | solution.py:157
  66.3 28.0 %collective-permute-start.27 = (bf16[1344,128]{1,0:T(8,128)(2,1)S(1)}, bf16[1344,128]{1,0:T(8,128)(2,1)S(1)}, u32[]{:S(2)}, u32[]{:S(2)}) collective-permute-start(bf16[1344,128]{1,0:T(8,128)(2,1)S(1)} %add_convert_fusion.1), channel_id=1, source_target_pairs={{0,8},{8,0},{16,24},{24,16},{1,9},{9,1},{17,25},{25,17},{2,10},{10... | collective-permute-start | bytes 1032200 | tf_op jit(solution)/shard_map/ppermute | solution.py:157
  66.3 28.6 %collective-permute-start.16 = (bf16[1792,128]{1,0:T(8,128)(2,1)S(1)}, bf16[1792,128]{1,0:T(8,128)(2,1)S(1)}, u32[]{:S(2)}, u32[]{:S(2)}) collective-permute-start(bf16[1792,128]{1,0:T(8,128)(2,1)S(1)} %add_convert_fusion), channel_id=1, source_target_pairs={{0,16},{8,24},{16,0},{24,8},{1,17},{9,25},{17,1},{25,9},{2,18},{10... | collective-permute-start | bytes 1376264 | tf_op jit(solution)/shard_map/ppermute | solution.py:157
  69.5 7.7 %collective-permute-start.20 = (f32[2,128,128]{2,1,0:T(8,128)S(1)}, f32[2,128,128]{2,1,0:T(8,128)S(1)}, u32[]{:S(2)}, u32[]{:S(2)}) collective-permute-start(f32[2,128,128]{2,1,0:T(8,128)S(1)} %add.451), channel_id=1, source_target_pairs={{0,4},{1,5},{2,6},{3,7},{4,0},{5,1},{6,2},{7,3},{8,12},{9,13},{10,... | collective-permute-start | bytes 393224 | tf_op jit(solution)/shard_map/ppermute | solution.py:157
  77.2 10.9 %collective-permute-start.10 = (f32[1,128,128]{2,1,0:T(8,128)S(1)}, f32[1,128,128]{2,1,0:T(8,128)S(1)}, u32[]{:S(2)}, u32[]{:S(2)}) collective-permute-start(f32[1,128,128]{2,1,0:T(8,128)S(1)} %shard_map.50), channel_id=1, source_target_pairs={{0,16},{8,24},{16,0},{24,8},{1,17},{9,25},{17,1},{25,9},{2,18},{10... | collective-permute-start | bytes 196616 | tf_op jit(solution)/shard_map/ppermute | solution.py:157
  81.7 10.9 %collective-permute-start.9 = (f32[1,128,128]{2,1,0:T(8,128)S(1)}, f32[1,128,128]{2,1,0:T(8,128)S(1)}, u32[]{:S(2)}, u32[]{:S(2)}) collective-permute-start(f32[1,128,128]{2,1,0:T(8,128)S(1)} %shard_map.50), channel_id=1, source_target_pairs={{0,8},{8,0},{16,24},{24,16},{1,9},{9,1},{17,25},{25,17},{2,10},{10... | collective-permute-start | bytes 196616 | tf_op jit(solution)/shard_map/ppermute | solution.py:157
  92.2 14.7 %collective-permute-start.29 = (bf16[1344,128]{1,0:T(8,128)(2,1)S(1)}, bf16[1344,128]{1,0:T(8,128)(2,1)S(1)}, u32[]{:S(2)}, u32[]{:S(2)}) collective-permute-start(bf16[1344,128]{1,0:T(8,128)(2,1)S(1)} %collective-permute-done.28), channel_id=1, source_target_pairs={{0,8},{8,0},{16,24},{24,16},{1,9},{9,1},{17,25},{25,17},{2,10},{10... | collective-permute-start | bytes 1032200 | tf_op jit(solution)/shard_map/ppermute | solution.py:157
  92.7 6.2 %collective-permute-start.35 = (f32[2,128,128]{2,1,0:T(8,128)S(1)}, f32[2,128,128]{2,1,0:T(8,128)}, u32[]{:S(2)}, u32[]{:S(2)}) collective-permute-start(f32[2,128,128]{2,1,0:T(8,128)S(1)} %shard_map.52), channel_id=1, source_target_pairs={{0,16},{8,24},{16,0},{24,8},{1,17},{9,25},{17,1},{25,9},{2,18},{10... | collective-permute-start | bytes 393224 | tf_op jit(solution)/shard_map/ppermute | solution.py:157
  94.2 6.7 %collective-permute-start.22 = (f32[2,128,128]{2,1,0:T(8,128)}, f32[2,128,128]{2,1,0:T(8,128)S(1)}, u32[]{:S(2)}, u32[]{:S(2)}) collective-permute-start(f32[2,128,128]{2,1,0:T(8,128)} %shard_map.51), channel_id=1, source_target_pairs={{0,16},{8,24},{16,0},{24,8},{1,17},{9,25},{17,1},{25,9},{2,18},{10... | collective-permute-start | bytes 393224 | tf_op jit(solution)/shard_map/ppermute | solution.py:157
  94.9 24.8 %collective-permute-start.15 = (bf16[1792,128]{1,0:T(8,128)(2,1)S(1)}, bf16[1792,128]{1,0:T(8,128)(2,1)S(1)}, u32[]{:S(2)}, u32[]{:S(2)}) collective-permute-start(bf16[1792,128]{1,0:T(8,128)(2,1)S(1)} %add_convert_fusion), channel_id=1, source_target_pairs={{0,8},{8,0},{16,24},{24,16},{1,9},{9,1},{17,25},{25,17},{2,10},{10... | collective-permute-start | bytes 1376264 | tf_op jit(solution)/shard_map/ppermute | solution.py:157
  98.8 8.0 %collective-permute-start.21 = (f32[2,128,128]{2,1,0:T(8,128)}, f32[2,128,128]{2,1,0:T(8,128)}, u32[]{:S(2)}, u32[]{:S(2)}) collective-permute-start(f32[2,128,128]{2,1,0:T(8,128)} %shard_map.51), channel_id=1, source_target_pairs={{0,8},{8,0},{16,24},{24,16},{1,9},{9,1},{17,25},{25,17},{2,10},{10... | collective-permute-start | bytes 393224 | tf_op jit(solution)/shard_map/ppermute | solution.py:157
  98.9 20.8 %collective-permute-start.17 = (bf16[1792,128]{1,0:T(8,128)(2,1)S(1)}, bf16[1792,128]{1,0:T(8,128)(2,1)S(1)}, u32[]{:S(2)}, u32[]{:S(2)}) collective-permute-start(bf16[1792,128]{1,0:T(8,128)(2,1)S(1)} %collective-permute-done.16), channel_id=1, source_target_pairs={{0,8},{8,0},{16,24},{24,16},{1,9},{9,1},{17,25},{25,17},{2,10},{10... | collective-permute-start | bytes 1376264 | tf_op jit(solution)/shard_map/ppermute | solution.py:157
  101.0 6.4 %collective-permute-start.36 = (f32[2,128,128]{2,1,0:T(8,128)}, f32[2,128,128]{2,1,0:T(8,128)}, u32[]{:S(2)}, u32[]{:S(2)}) collective-permute-start(f32[2,128,128]{2,1,0:T(8,128)} %collective-permute-done.35), channel_id=1, source_target_pairs={{0,8},{8,0},{16,24},{24,16},{1,9},{9,1},{17,25},{25,17},{2,10},{10... | collective-permute-start | bytes 393224 | tf_op jit(solution)/shard_map/ppermute | solution.py:157
  106.8 21.7 %collective-permute-start.3 = (bf16[896,128]{1,0:T(8,128)(2,1)S(1)}, bf16[896,128]{1,0:T(8,128)(2,1)S(1)}, u32[]{:S(2)}, u32[]{:S(2)}) collective-permute-start(bf16[896,128]{1,0:T(8,128)(2,1)S(1)} %add_convert_fusion.2), channel_id=1, source_target_pairs={{0,8},{8,0},{16,24},{24,16},{1,9},{9,1},{17,25},{25,17},{2,10},{10... | collective-permute-start | bytes 688136 | tf_op jit(solution)/shard_map/ppermute | solution.py:157
  106.9 21.7 %collective-permute-start.5 = (bf16[896,128]{1,0:T(8,128)(2,1)}, bf16[896,128]{1,0:T(8,128)(2,1)S(1)}, u32[]{:S(2)}, u32[]{:S(2)}) collective-permute-start(bf16[896,128]{1,0:T(8,128)(2,1)} %copy-done.3), channel_id=1, source_target_pairs={{0,8},{8,0},{16,24},{24,16},{1,9},{9,1},{17,25},{25,17},{2,10},{10... | collective-permute-start | bytes 688136 | tf_op jit(solution)/shard_map/ppermute | solution.py:157
  107.4 11.2 %collective-permute-start.23 = (f32[2,128,128]{2,1,0:T(8,128)}, f32[2,128,128]{2,1,0:T(8,128)S(1)}, u32[]{:S(2)}, u32[]{:S(2)}) collective-permute-start(f32[2,128,128]{2,1,0:T(8,128)} %copy-done.9), channel_id=1, source_target_pairs={{0,8},{8,0},{16,24},{24,16},{1,9},{9,1},{17,25},{25,17},{2,10},{10... | collective-permute-start | bytes 393224 | tf_op jit(solution)/shard_map/ppermute | solution.py:157
  (26 other events, 289.0 us)

commit v3 on v2

v3 whole, which is shorter than its diff:
```python
import functools
import math

import jax
import jax.numpy as jnp
from jax import lax
from jax.experimental import pallas as pl
from jax.experimental.pallas import tpu as pltpu
from jax.sharding import PartitionSpec as P

D = 7168
V = 128
ITERS = 5
CORES = 2

quintic_one = 3.4445
quintic_two = -4.775
quintic_three = 2.0315
epsilon = 1e-07
learning_rate = 0.02
decay_rate = 0.1
HIGHEST = lax.Precision.HIGHEST


def dot32(left, right):
    return jnp.dot(left, right, precision=HIGHEST, preferred_element_type=jnp.float32)


def newton_kernel(gram_ref, arrived_ref, *refs):
    *earlier, out_ref = refs
    skip = 0
    for ref in earlier:
        out_ref[: ref.shape[0]] = ref[...]
        skip = ref.shape[0]
    items = gram_ref.shape[0]
    rows = lax.broadcasted_iota(jnp.int32, (V, V), 0)
    columns = lax.broadcasted_iota(jnp.int32, (V, V), 1)
    eye = (rows == columns).astype(jnp.float32)
    grams, scales = [], []
    for item in range(items):
        gram = gram_ref[item] + arrived_ref[item]
        norm_value = jnp.sqrt(jnp.sum(gram * eye))
        scale = 1.0 / (norm_value + epsilon)
        scales.append(scale)
        grams.append((gram * scale) * scale)
    products = [None] * items
    for index in range(ITERS):
        squares = [dot32(gram, gram) for gram in grams]
        polys = [
            quintic_one * eye + quintic_two * gram + quintic_three * square
            for gram, square in zip(grams, squares)
        ]
        if index < ITERS - 1:
            halves = [dot32(gram, poly) for gram, poly in zip(grams, polys)]
        if index == 0:
            products = polys
        else:
            products = [dot32(product, poly) for product, poly in zip(products, polys)]
        if index < ITERS - 1:
            grams = [dot32(half, poly) for half, poly in zip(halves, polys)]
    for item in range(items):
        out_ref[skip + item] = products[item] * scales[item]


def newton_schulz(gram, arrived, *earlier):
    items = gram.shape[0]
    slots = items + sum(q.shape[0] for q in earlier)
    return pl.pallas_call(
        newton_kernel,
        out_shape=jax.ShapeDtypeStruct((slots, V, V), jnp.float32),
        in_specs=[pl.BlockSpec(memory_space=pltpu.VMEM)] * (2 + len(earlier)),
        out_specs=pl.BlockSpec(memory_space=pltpu.VMEM),
        cost_estimate=pl.CostEstimate(
            flops=items * 18 * 12 * V**3, bytes_accessed=items * V * V * 12, transcendentals=0
        ),
        compiler_params=pltpu.CompilerParams(vmem_limit_bytes=16 * 1024 * 1024),
    )(gram, arrived, *earlier)


def apply_kernel(layout, place_ref, table_ref, *refs):
    count, first, base, size, offset, own, total, padded = layout
    sources, qs = refs[:count], refs[count : 2 * count]
    params_ref = refs[2 * count]
    new_ref, update_ref, new_buf, update_buf, new_sems, update_sems = refs[-6:]
    per_block = 2 if size % 2 else 1
    units, unit_rows = sources[0].shape[:2]
    whole = size // 2
    place = place_ref[0]

    def locate(source, unit):
        holder = (place ^ source) & (CORES - 1)
        within = holder * units + unit
        block = within >> (per_block - 1)
        index = ((place ^ source) >> (CORES - 1)) * own + offset + block
        head = table_ref[jnp.minimum(index, total - 1) if padded else index]
        start = pl.multiple_of((within & (per_block - 1)) * unit_rows, unit_rows)
        slot = unit
        if per_block > 1:
            slot = jnp.where(block == whole, whole, block - holder * (whole + 1))
        return index < total, head, pl.ds(start, unit_rows), base + slot

    items = [
        (index, unit, index * units + unit, locate(first + index, unit))
        for index in range(count)
        for unit in range(units)
    ]

    def compute(index, unit, item, head, span, slot):
        q = qs[index][slot]
        high = q.astype(jnp.bfloat16)
        low = (q - high.astype(jnp.float32)).astype(jnp.bfloat16)
        rows = sources[index][unit]
        ortho = jnp.dot(
            jnp.concatenate([rows, rows], axis=1),
            jnp.concatenate([high, low], axis=0),
            preferred_element_type=jnp.float32,
        )
        ortho = ortho.astype(jnp.bfloat16).astype(jnp.float32)
        scaled = 0.2 * math.sqrt(max(D, V)) * ortho
        params = params_ref[head, span]
        new_buf[item] = params - learning_rate * (scaled + decay_rate * params)
        update_buf[item] = scaled.astype(jnp.bfloat16)
        pltpu.make_async_copy(new_buf.at[item], new_ref.at[head, span], new_sems.at[item]).start()
        pltpu.make_async_copy(
            update_buf.at[item], update_ref.at[head, span], update_sems.at[item]
        ).start()

    def finish(item):
        span = pl.ds(0, unit_rows)
        pltpu.make_async_copy(new_buf.at[item], new_ref.at[0, span], new_sems.at[item]).wait()
        pltpu.make_async_copy(
            update_buf.at[item], update_ref.at[0, span], update_sems.at[item]
        ).wait()

    for index, unit, item, (valid, head, span, slot) in items:
        run = functools.partial(compute, index, unit, item, head, span, slot)
        pl.when(valid)(run) if padded else run()
    for index, unit, item, (valid, head, span, slot) in items:
        run = functools.partial(finish, item)
        pl.when(valid)(run) if padded else run()


def apply_side(sources, qs, params, previous, place, table, first, base, size, offset, own, padded):
    total, rows, width = params.shape
    count = len(sources)
    units, unit_rows = sources[0].shape[:2]
    steps = count * units
    vmem = pl.BlockSpec(memory_space=pltpu.VMEM)
    hbm = pl.BlockSpec(memory_space=pltpu.HBM)
    smem = pl.BlockSpec(memory_space=pltpu.SMEM)
    operands = [place, table, *sources, *qs, params]
    in_specs = [smem, smem] + [vmem] * (2 * count + 1)
    aliases = {}
    for index, array in enumerate(previous):
        aliases[len(operands)] = index
        operands.append(array)
        in_specs.append(hbm)
    work = steps * unit_rows * width
    layout = (count, first, base, size, offset, own, total, padded)
    return pl.pallas_call(
        functools.partial(apply_kernel, layout),
        in_specs=in_specs,
        out_specs=[hbm, hbm],
        out_shape=[
            jax.ShapeDtypeStruct(params.shape, jnp.float32),
            jax.ShapeDtypeStruct(params.shape, jnp.bfloat16),
        ],
        scratch_shapes=[
            pltpu.VMEM((steps, unit_rows, width), jnp.float32),
            pltpu.VMEM((steps, unit_rows, width), jnp.bfloat16),
            pltpu.SemaphoreType.DMA((steps,)),
            pltpu.SemaphoreType.DMA((steps,)),
        ],
        input_output_aliases=aliases,
        cost_estimate=pl.CostEstimate(flops=4 * work * V, bytes_accessed=12 * work, transcendentals=0),
        compiler_params=pltpu.CompilerParams(vmem_limit_bytes=24 * 1024 * 1024),
    )(*operands)


def chunk_sizes(own):
    if own <= 4:
        return [own]
    return [own - 4, 4]


def swap(array, axis, distance):
    size = lax.axis_size(axis)
    return lax.ppermute(array, axis, [(i, i ^ distance) for i in range(size)])


def gram_of(rows_array, rows):
    blocks = rows_array.reshape(-1, rows, V)
    return jnp.einsum("mrv,mrw->mvw", blocks, blocks, preferred_element_type=jnp.float32)


def per_device(grads, params, table):
    local = grads[0]
    count, rows, width = local.shape
    replicas = lax.axis_size("dp")
    groups = lax.axis_size("shard")
    members = replicas // CORES
    own = -(-count // members)
    padded = members * own > count
    place = lax.axis_index("dp").astype(jnp.int32)
    core = place % CORES
    member = place // CORES
    if padded:
        filler = jnp.zeros((members * own - count, rows, width), local.dtype)
        local = jnp.concatenate([local, filler], axis=0)
    flat = local.reshape(members * own * rows, width)
    sizes = chunk_sizes(own)

    def rows_of(chip, offset, which, length):
        return lax.dynamic_slice_in_dim(flat, (chip * own + offset) * rows + which * length, length)

    def total_of(terms):
        terms = [term.astype(jnp.float32) for term in terms]
        while len(terms) > 1:
            terms = [sum(terms[i : i + 2][1:], terms[i]) for i in range(0, len(terms), 2)]
        return terms[0]

    def reduce_gram(gram, distance=1):
        while True:
            arrived = swap(gram, "shard", distance)
            distance *= 2
            if distance >= groups:
                return gram, arrived
            gram = gram + arrived

    def over_chips(array):
        return [swap(array, "dp", distance * CORES) for distance in range(1, members)]

    def over_cores(array):
        return [array, swap(array, "dp", 1)]

    def pieces_of(offset, size):
        share = size * rows // CORES
        return [
            rows_of((place ^ distance) // CORES, offset, (place ^ distance) % CORES, share)
            for distance in range(replicas)
        ]

    def exchange(pieces):
        return [swap(piece, "dp", d) if d else piece for d, piece in enumerate(pieces)]

    size = sizes[0]
    terms = exchange(pieces_of(0, size))
    seconds = []
    if len(sizes) > 1:
        pieces = pieces_of(size, sizes[1])
        terms[-1], *pieces = lax.optimization_barrier((terms[-1], *pieces))
        *seconds, late = exchange(pieces)

    first = total_of(terms).astype(jnp.bfloat16)
    whole = size // 2
    if size % 2:
        half = lax.dynamic_slice_in_dim(first, (1 - core) * whole * rows, rows // 2)
        gram = gram_of(half, rows // 2)
        if seconds:
            *seconds, gram = lax.optimization_barrier((*seconds, gram))
        gram = gram + swap(gram, "dp", 1)
        if whole:
            full = lax.dynamic_slice_in_dim(first, core * (rows // 2), whole * rows)
            gram = jnp.concatenate([gram_of(full, rows), gram], axis=0)
    else:
        gram = gram_of(first, rows)
    totals, qs = [first], []
    if seconds:
        gram = gram + swap(gram, "shard", 1)
        late, gram = lax.optimization_barrier((late, gram))
        gram = gram + swap(gram, "shard", 2)
        second = total_of([*seconds, late]).astype(jnp.bfloat16)
        totals.append(second)
        gram_second, gram = lax.optimization_barrier((gram_of(second, rows), gram))
        qs.append(newton_schulz(*reduce_gram(gram, 4)))
        pair = reduce_gram(gram_second)
        qs.append(newton_schulz(*pair, qs[0]))
    else:
        qs.append(newton_schulz(*reduce_gram(gram)))

    q = qs[-1]
    arrived_q = over_chips(q)
    arrived_rows = [over_chips(total) for total in totals]
    outputs = []
    for distance in range(members):
        if distance:
            q = arrived_q[distance - 1]
            if distance == 1:
                q, *outputs = lax.optimization_barrier((q, *outputs))
        pair_q = over_cores(q)
        for index, size in enumerate(sizes):
            rows_here = totals[index]
            if distance:
                tie = qs[-1] if index == len(sizes) - 1 else pair[0]
                rows_here = lax.optimization_barrier((arrived_rows[index][distance - 1], tie))[0]
            per_block = 2 if size % 2 else 1
            units = size * per_block // CORES
            outputs = apply_side(
                [
                    array.reshape(units, rows // per_block, width)
                    for array in over_cores(rows_here)
                ],
                pair_q,
                params,
                outputs,
                place.reshape(1),
                table,
                CORES * distance,
                qs[index - 1].shape[0] if index else 0,
                size,
                sum(sizes[:index]),
                own,
                padded,
            )
    new_params, update = outputs
    return (new_params, update)


def solution(mesh):
    return jax.shard_map(
        per_device,
        mesh=mesh,
        in_specs=(P("dp", None, "shard", None), P(None, "shard", None), P()),
        out_specs=(P(None, "shard", None), P(None, "shard", None)),
        check_vma=False,
    )
```

time: 132 us -> 105 us (0.80)
  local copies, waits for them, and re-layouts: 21.6 us -> 3.13 us
  waiting for transfers between devices: 39.3 us -> 52.5 us
  other arithmetic: 10.3 us -> 1.71 us
  Pallas kernels: 26.1 us -> 17.8 us
  starting transfers between devices: 32.3 us -> 27.5 us
    ppermute x37 -> x22, waiting for transfers between devices: 39.3 us -> 52.5 us  [swap(): return lax.ppermute(array, axis, [(i, i ^ distance) for i in range(size)])]
    unnamed x42 -> x6, local copies, waits for them, and re-layouts: 8.78 us -> 0.02 us
    pallas_call x6, Pallas kernels: 26.1 us -> 17.8 us  [the longest x4 10.6 us: apply_side(): pl.pallas_call(functools.partial(apply_kernel, layout), in_specs=in_specs...]
    ppermute x37 -> x22, starting transfers between devices: 32.3 us -> 27.5 us  [swap(): return lax.ppermute(array, axis, [(i, i ^ distance) for i in range(size)])]
    iota x12 -> x0, local copies, waits for them, and re-layouts: 3.6 us -> none  [the longest x8 2.65 us: per_device(): other = lax.broadcasted_iota(jnp.int32, shape, 1)]
    convert_element_type x6 -> x2, other arithmetic: 4.7 us -> 1.6 us  [the longest x1 1.36 us: per_device(): first = total_of(terms).astype(jnp.bfloat16)]
    concatenate x3 -> x0, other arithmetic: 3.07 us -> none  [per_device(): q_all = jnp.concatenate(spread(q), axis=0)]
    add x5 -> x0, local copies, waits for them, and re-layouts: 2.16 us -> none  [the longest x2 1.91 us: per_device(): block = ((member ^ distance) * own + offset + block).reshape(-1)]
  transfers between devices with their start and end apart: 37 -> 22, of which waited for: 12 -> 10; matrix products, arithmetic and copies ran while one was open for 17% -> 4% of each run, Pallas kernels for 17% -> 15%
where the time goes in v3:
time: 105 us
  waiting for transfers between devices  52.5 us (50%)
  starting transfers between devices  27.5 us (26%)
  Pallas kernels  17.8 us (17%)
  local copies, waits for them, and re-layouts  3.13 us (3%)
  other arithmetic  1.71 us (2%)
    ppermute x22, waiting for transfers between devices, swap(): return lax.ppermute(array, axis, [(i, i ^ distance) for i in range(size)])  52.5 us
    ppermute x22, starting transfers between devices, swap(): return lax.ppermute(array, axis, [(i, i ^ distance) for i in range(size)])  27.5 us
    pallas_call x4, Pallas kernels, apply_side(): pl.pallas_call(functools.partial(apply_kernel, layout), in_specs=in_specs...  10.6 us
    pallas_call x2, Pallas kernels, newton_schulz(): pl.pallas_call(newton_kernel, out_shape=jax.ShapeDtypeStruct((slots, V, V...  7.16 us
    dynamic_slice x2, local copies, waits for them, and re-layouts, rows_of(): lax.dynamic_slice_in_dim(flat, (chip * own + offset) * rows + which * len...  3.08 us
  transfers between devices with their start and end apart: 22, of which 10 were waited for; matrix products, arithmetic and copies ran while one was open for 4% of the time, Pallas kernels for 15%

profile of v3, /device:TPU:0, one launch (start us, length us, event | category | flops | bytes accessed | tf_op | source)
XLA Modules:
  0.0 104.5 jit_solution(17474408941181199162)
XLA Ops:
  0.7 1.5 %constant_dynamic-slice_fusion.2 = (bf16[2240,128]{1,0:T(8,128)(2,1)S(1)}, bf16[2240,128]{1,0:T(8,128)(2,1)S(1)}, bf16[2240,128]{1,0:T(8,128)(2,1)S(1)}) fusion(bf16[16128,128]{1,0:T(8,128)(2,1)} %bitcast.29, s32[]{:T(128)S(6)} %select_n.90, s32[]{:T(128)S(6)} %select_n.91, s32[]{:T(128)S(6)} %select_n.78), kind=kLoop, calls=%fused_computation.8 | loop fusion | bytes 3440652 | tf_op jit(solution)/shard_map/dynamic_slice | solution.py:214
  2.3 2.5 %collective-permute-start = (bf16[2240,128]{1,0:T(8,128)(2,1)S(1)}, bf16[2240,128]{1,0:T(8,128)(2,1)S(1)}, u32[]{:S(2)}, u32[]{:S(2)}) collective-permute-start(bf16[2240,128]{1,0:T(8,128)(2,1)S(1)} %get-tuple-element.52), channel_id=1, source_target_pairs={{0,24},{8,16},{16,8},{24,0},{1,25},{9,17},{17,9},{25,1},{2,26},{10... | collective-permute-start | bytes 1720328 | tf_op jit(solution)/shard_map/ppermute | solution.py:188
  5.5 1.6 %constant_dynamic-slice_fusion.3 = (bf16[1792,128]{1,0:T(8,128)(2,1)S(1)}, bf16[1792,128]{1,0:T(8,128)(2,1)S(1)}, bf16[1792,128]{1,0:T(8,128)(2,1)S(1)}, bf16[1792,128]{1,0:T(8,128)(2,1)S(1)}) fusion(bf16[16128,128]{1,0:T(8,128)(2,1)} %bitcast.30, s32[]{:T(128)S(6)} %select_n.88, s32[]{:T(128)S(6)} %select_n.87, s32[]{:T(128)S(6)} %select_n.84, s32[]{:T(128)S(6)} %select_n.81), kind=kLoop, calls=%fused_computation.9 | loop fusion | bytes 3670032 | tf_op jit(solution)/shard_map/dynamic_slice | solution.py:214
  7.0 11.1 %collective-permute-done = bf16[2240,128]{1,0:T(8,128)(2,1)S(1)} collective-permute-done((bf16[2240,128]{1,0:T(8,128)(2,1)S(1)}, bf16[2240,128]{1,0:T(8,128)(2,1)S(1)}, u32[]{:S(2)}, u32[]{:S(2)}) %collective-permute-start) | collective-permute-done | bytes 573472 | tf_op jit(solution)/shard_map/ppermute | solution.py:188
  18.1 0.8 collective-permute-start.1
  18.9 1.8 %collective-permute-start.2 = (bf16[1792,128]{1,0:T(8,128)(2,1)S(1)}, bf16[1792,128]{1,0:T(8,128)(2,1)S(1)}, u32[]{:S(2)}, u32[]{:S(2)}) collective-permute-start(bf16[1792,128]{1,0:T(8,128)(2,1)S(1)} %get-tuple-element.28), channel_id=1, source_target_pairs={{0,16},{8,24},{16,0},{24,8},{1,17},{9,25},{17,1},{25,9},{2,18},{10... | collective-permute-start | bytes 1376264 | tf_op jit(solution)/shard_map/ppermute | solution.py:188
  20.7 10.7 %collective-permute-done.4 = bf16[2240,128]{1,0:T(8,128)(2,1)S(1)} collective-permute-done((bf16[2240,128]{1,0:T(8,128)(2,1)S(1)}, bf16[2240,128]{1,0:T(8,128)(2,1)S(1)}, u32[]{:S(2)}, u32[]{:S(2)}) %collective-permute-start.4) | collective-permute-done | bytes 573472 | tf_op jit(solution)/shard_map/ppermute | solution.py:188
  31.4 1.4 %add_convert_fusion = bf16[2240,128]{1,0:T(8,128)(2,1)S(1)} fusion(bf16[2240,128]{1,0:T(8,128)(2,1)S(1)} %collective-permute-done, bf16[2240,128]{1,0:T(8,128)(2,1)S(1)} %collective-permute-done.4, bf16[2240,128]{1,0:T(8,128)(2,1)S(1)} %collective-permute-done.3, bf16[16128,128]{1,0:T(8,128)(2,1)} %bitcast.31, s32[]{:T(128)S(6)} %select_n.89), kind=kLoop, calls=%fused_computation | loop fusion | flops 2293760 | bytes 2867204 | tf_op jit(solution)/shard_map/convert_element_type | solution.py:254
  33.0 7.4 %collective-permute-done.2 = bf16[1792,128]{1,0:T(8,128)(2,1)S(1)} collective-permute-done((bf16[1792,128]{1,0:T(8,128)(2,1)S(1)}, bf16[1792,128]{1,0:T(8,128)(2,1)S(1)}, u32[]{:S(2)}, u32[]{:S(2)}) %collective-permute-start.2) | collective-permute-done | bytes 458784 | tf_op jit(solution)/shard_map/ppermute | solution.py:188
  40.7 2.5 %collective-permute-start.5 = (bf16[1792,128]{1,0:T(8,128)(2,1)S(1)}, bf16[1792,128]{1,0:T(8,128)(2,1)S(1)}, u32[]{:S(2)}, u32[]{:S(2)}) collective-permute-start(bf16[1792,128]{1,0:T(8,128)(2,1)S(1)} %get-tuple-element.33), channel_id=1, source_target_pairs={{0,24},{8,16},{16,8},{24,0},{1,25},{9,17},{17,9},{25,1},{2,26},{10... | collective-permute-start | bytes 1376264 | tf_op jit(solution)/shard_map/ppermute | solution.py:188
  43.3 1.6 %collective-permute-start.7 = (f32[3,128,128]{2,1,0:T(8,128)S(1)}, f32[3,128,128]{2,1,0:T(8,128)S(1)}, u32[]{:S(2)}, u32[]{:S(2)}) collective-permute-start(f32[3,128,128]{2,1,0:T(8,128)S(1)} %pad_maximum_fusion), channel_id=1, source_target_pairs={{0,1},{1,0},{2,3},{3,2},{4,5},{5,4},{6,7},{7,6},{8,9},{9,8},{10,11... | collective-permute-start | bytes 589832 | tf_op jit(solution)/shard_map/ppermute | solution.py:188
  44.8 0.7 collective-permute-start.20
  45.5 4.7 %collective-permute-done.7 = f32[3,128,128]{2,1,0:T(8,128)S(1)} collective-permute-done((f32[3,128,128]{2,1,0:T(8,128)S(1)}, f32[3,128,128]{2,1,0:T(8,128)S(1)}, u32[]{:S(2)}, u32[]{:S(2)}) %collective-permute-start.7) | collective-permute-done | bytes 196640 | tf_op jit(solution)/shard_map/ppermute | solution.py:188
  50.3 3.8 %collective-permute-done.5 = bf16[1792,128]{1,0:T(8,128)(2,1)S(1)} collective-permute-done((bf16[1792,128]{1,0:T(8,128)(2,1)S(1)}, bf16[1792,128]{1,0:T(8,128)(2,1)S(1)}, u32[]{:S(2)}, u32[]{:S(2)}) %collective-permute-start.5) | collective-permute-done | bytes 458784 | tf_op jit(solution)/shard_map/ppermute | solution.py:188
  54.1 1.6 %collective-permute-start.9 = (f32[3,128,128]{2,1,0:T(8,128)S(1)}, f32[3,128,128]{2,1,0:T(8,128)S(1)}, u32[]{:S(2)}, u32[]{:S(2)}) collective-permute-start(f32[3,128,128]{2,1,0:T(8,128)S(1)} %fusion.2), channel_id=1, source_target_pairs={{0,2},{1,3},{2,0},{3,1},{4,6},{5,7},{6,4},{7,5},{8,10},{9,11},{10,... | collective-permute-start | bytes 589832 | tf_op jit(solution)/shard_map/ppermute | solution.py:188
  56.3 5.2 %collective-permute-done.9 = f32[3,128,128]{2,1,0:T(8,128)S(1)} collective-permute-done((f32[3,128,128]{2,1,0:T(8,128)S(1)}, f32[3,128,128]{2,1,0:T(8,128)S(1)}, u32[]{:S(2)}, u32[]{:S(2)}) %collective-permute-start.9) | collective-permute-done | bytes 196640 | tf_op jit(solution)/shard_map/ppermute | solution.py:188
  61.5 1.7 %collective-permute-start.10 = (f32[2,128,128]{2,1,0:T(8,128)S(1)}, f32[2,128,128]{2,1,0:T(8,128)S(1)}, u32[]{:S(2)}, u32[]{:S(2)}) collective-permute-start(f32[2,128,128]{2,1,0:T(8,128)S(1)} %fusion.4), channel_id=1, source_target_pairs={{0,1},{1,0},{2,3},{3,2},{4,5},{5,4},{6,7},{7,6},{8,9},{9,8},{10,11... | collective-permute-start | bytes 393224 | tf_op jit(solution)/shard_map/ppermute | solution.py:188
  63.3 2.6 %collective-permute-start.13 = (f32[3,128,128]{2,1,0:T(8,128)S(1)}, f32[3,128,128]{2,1,0:T(8,128)S(1)}, u32[]{:S(2)}, u32[]{:S(2)}) collective-permute-start(f32[3,128,128]{2,1,0:T(8,128)S(1)} %add.155.gram_ref), channel_id=1, source_target_pairs={{0,4},{1,5},{2,6},{3,7},{4,0},{5,1},{6,2},{7,3},{8,12},{9,13},{10,... | collective-permute-start | bytes 589832 | tf_op jit(solution)/shard_map/ppermute | solution.py:188
  65.8 1.0 collective-permute-done.10
  66.9 1.9 %collective-permute-start.11 = (f32[2,128,128]{2,1,0:T(8,128)S(1)}, f32[2,128,128]{2,1,0:T(8,128)S(1)}, u32[]{:S(2)}, u32[]{:S(2)}) collective-permute-start(f32[2,128,128]{2,1,0:T(8,128)S(1)} %add.156), channel_id=1, source_target_pairs={{0,2},{1,3},{2,0},{3,1},{4,6},{5,7},{6,4},{7,5},{8,10},{9,11},{10,... | collective-permute-start | bytes 393224 | tf_op jit(solution)/shard_map/ppermute | solution.py:188
  68.7 1.7 %collective-permute-start.8 = (bf16[1792,128]{1,0:T(8,128)(2,1)S(1)}, bf16[1792,128]{1,0:T(8,128)(2,1)S(1)}, u32[]{:S(2)}, u32[]{:S(2)}) collective-permute-start(bf16[1792,128]{1,0:T(8,128)(2,1)S(1)} %add_convert_fusion.1), channel_id=1, source_target_pairs={{0,16},{8,24},{16,0},{24,8},{1,17},{9,25},{17,1},{25,9},{2,18},{10... | collective-permute-start | bytes 1376264 | tf_op jit(solution)/shard_map/ppermute | solution.py:188
  70.4 4.6 %collective-permute-done.11 = f32[2,128,128]{2,1,0:T(8,128)S(1)} collective-permute-done((f32[2,128,128]{2,1,0:T(8,128)S(1)}, f32[2,128,128]{2,1,0:T(8,128)S(1)}, u32[]{:S(2)}, u32[]{:S(2)}) %collective-permute-start.11) | collective-permute-done | bytes 131104 | tf_op jit(solution)/shard_map/ppermute | solution.py:188
  75.0 2.6 %collective-permute-start.12 = (f32[2,128,128]{2,1,0:T(8,128)S(1)}, f32[2,128,128]{2,1,0:T(8,128)S(1)}, u32[]{:S(2)}, u32[]{:S(2)}) collective-permute-start(f32[2,128,128]{2,1,0:T(8,128)S(1)} %add.157.gram_ref), channel_id=1, source_target_pairs={{0,4},{1,5},{2,6},{3,7},{4,0},{5,1},{6,2},{7,3},{8,12},{9,13},{10,... | collective-permute-start | bytes 393224 | tf_op jit(solution)/shard_map/ppermute | solution.py:188
  77.6 3.8 %shard_map.50.refs_0_ = f32[3,128,128]{2,1,0:T(8,128)S(1)} custom-call(f32[3,128,128]{2,1,0:T(8,128)S(1)} %add.155.gram_ref, f32[3,128,128]{2,1,0:T(8,128)S(1)} %collective-permute-done.13.arrived_ref), custom_call_target="tpu_custom_call" | custom-call | flops 1358954496 | bytes 589824 | tf_op jit(solution)/shard_map/pallas_call | solution.py:68
  81.4 3.4 %shard_map.51.refs_2_ = f32[5,128,128]{2,1,0:T(8,128)S(1)} custom-call(f32[2,128,128]{2,1,0:T(8,128)S(1)} %add.157.gram_ref, f32[2,128,128]{2,1,0:T(8,128)S(1)} %collective-permute-done.12.arrived_ref, f32[3,128,128]{2,1,0:T(8,128)S(1)} %shard_map.50.refs_0_), custom_call_target="tpu_custom_call" | custom-call | flops 905969664 | bytes 393216 | tf_op jit(solution)/shard_map/pallas_call | solution.py:68
  85.4 3.9 %collective-permute-start.15 = (f32[5,128,128]{2,1,0:T(8,128)S(1)}, f32[5,128,128]{2,1,0:T(8,128)S(1)}, u32[]{:S(2)}, u32[]{:S(2)}) collective-permute-start(f32[5,128,128]{2,1,0:T(8,128)S(1)} %shard_map.51.refs_2_), channel_id=1, source_target_pairs={{0,16},{8,24},{16,0},{24,8},{1,17},{9,25},{17,1},{25,9},{2,18},{10... | collective-permute-start | bytes 983048 | tf_op jit(solution)/shard_map/ppermute | solution.py:188
  89.8 2.8 %shard_map.52 = (f32[18,896,128]{2,1,0:T(8,128)}, bf16[18,896,128]{2,1,0:T(8,128)(2,1)}) custom-call(s32[1]{0:T(128)} %bitcast.place_ref, s32[18]{0:T(128)S(1)} %copy-done, bf16[5,448,128]{2,1,0:T(8,128)(2,1)S(1)} %bitcast.21, bf16[5,448,128]{2,1,0:T(8,128)(2,1)S(1)} %bitcast.22, f32[5,128,128]{2,1,0:T(8,128)S(1)} %shard_map.51.refs_2_, ...), custom_call_target="tpu_custom_call" | custom-call | flops 293601280 | bytes 6881280 | tf_op jit(solution)/shard_map/pallas_call | solution.py:160
  92.6 2.5 %shard_map.53 = (f32[18,896,128]{2,1,0:T(8,128)}, bf16[18,896,128]{2,1,0:T(8,128)(2,1)}) custom-call(s32[1]{0:T(128)} %bitcast.place_ref, s32[18]{0:T(128)S(1)} %copy-done, bf16[2,896,128]{2,1,0:T(8,128)(2,1)S(1)} %bitcast.20, bf16[2,896,128]{2,1,0:T(8,128)(2,1)S(1)} %bitcast.27, ...), custom_call_target="tpu_custom_call", output_to_operand_aliasing={{0}: (7, {}), {1}: (8, {})} | custom-call | flops 234881024 | bytes 5505024 | tf_op jit(solution)/shard_map/pallas_call | solution.py:160
  95.1 2.4 %collective-permute-done.15.refs_2_ = f32[5,128,128]{2,1,0:T(8,128)S(1)} collective-permute-done((f32[5,128,128]{2,1,0:T(8,128)S(1)}, f32[5,128,128]{2,1,0:T(8,128)S(1)}, u32[]{:S(2)}, u32[]{:S(2)}) %collective-permute-start.15) | collective-permute-done | bytes 327712 | tf_op jit(solution)/shard_map/ppermute | solution.py:188
  97.5 1.6 %collective-permute-done.19.refs_3_ = f32[5,128,128]{2,1,0:T(8,128)S(1)} collective-permute-done((f32[5,128,128]{2,1,0:T(8,128)S(1)}, f32[5,128,128]{2,1,0:T(8,128)S(1)}, u32[]{:S(2)}, u32[]{:S(2)}) %collective-permute-start.19) | collective-permute-done | bytes 327712 | tf_op jit(solution)/shard_map/ppermute | solution.py:188
  99.2 2.8 %shard_map.54 = (f32[18,896,128]{2,1,0:T(8,128)}, bf16[18,896,128]{2,1,0:T(8,128)(2,1)}) custom-call(s32[1]{0:T(128)} %bitcast.place_ref, s32[18]{0:T(128)S(1)} %copy-done, bf16[5,448,128]{2,1,0:T(8,128)(2,1)S(1)} %bitcast.23, bf16[5,448,128]{2,1,0:T(8,128)(2,1)S(1)} %bitcast.24, ...), custom_call_target="tpu_custom_call", output_to_operand_aliasing={{0}: (7, {}), {1}: (8, {})} | custom-call | flops 293601280 | bytes 6881280 | tf_op jit(solution)/shard_map/pallas_call | solution.py:160
  102.0 2.5 %shard_map.55 = (f32[18,896,128]{2,1,0:T(8,128)}, bf16[18,896,128]{2,1,0:T(8,128)(2,1)}) custom-call(s32[1]{0:T(128)} %bitcast.place_ref, s32[18]{0:T(128)S(1)} %copy-done, bf16[2,896,128]{2,1,0:T(8,128)(2,1)S(1)} %bitcast.25, bf16[2,896,128]{2,1,0:T(8,128)(2,1)S(1)} %bitcast.26, ...), custom_call_target="tpu_custom_call", output_to_operand_aliasing={{0}: (7, {}), {1}: (8, {})} | custom-call | flops 234881024 | bytes 5505024 | tf_op jit(solution)/shard_map/pallas_call | solution.py:160
  (39 shorter events, 3.2 us)
Async XLA Ops:
  2.3 15.8 %collective-permute-start = (bf16[2240,128]{1,0:T(8,128)(2,1)S(1)}, bf16[2240,128]{1,0:T(8,128)(2,1)S(1)}, u32[]{:S(2)}, u32[]{:S(2)}) collective-permute-start(bf16[2240,128]{1,0:T(8,128)(2,1)S(1)} %get-tuple-element.52), channel_id=1, source_target_pairs={{0,24},{8,16},{16,8},{24,0},{1,25},{9,17},{17,9},{25,1},{2,26},{10... | collective-permute-start | bytes 1720328 | tf_op jit(solution)/shard_map/ppermute | solution.py:188
  4.7 16.0 %collective-permute-start.3 = (bf16[2240,128]{1,0:T(8,128)(2,1)S(1)}, bf16[2240,128]{1,0:T(8,128)(2,1)S(1)}, u32[]{:S(2)}, u32[]{:S(2)}) collective-permute-start(bf16[2240,128]{1,0:T(8,128)(2,1)S(1)} %get-tuple-element.50), channel_id=1, source_target_pairs={{0,8},{8,0},{16,24},{24,16},{1,9},{9,1},{17,25},{25,17},{2,10},{10... | collective-permute-start | bytes 1720328 | tf_op jit(solution)/shard_map/ppermute | solution.py:188
  5.4 26.0 %collective-permute-start.4 = (bf16[2240,128]{1,0:T(8,128)(2,1)S(1)}, bf16[2240,128]{1,0:T(8,128)(2,1)S(1)}, u32[]{:S(2)}, u32[]{:S(2)}) collective-permute-start(bf16[2240,128]{1,0:T(8,128)(2,1)S(1)} %get-tuple-element.51), channel_id=1, source_target_pairs={{0,16},{8,24},{16,0},{24,8},{1,17},{9,25},{17,1},{25,9},{2,18},{10... | collective-permute-start | bytes 1720328 | tf_op jit(solution)/shard_map/ppermute | solution.py:188
  18.1 14.9 %collective-permute-start.1 = (bf16[1792,128]{1,0:T(8,128)(2,1)S(1)}, bf16[1792,128]{1,0:T(8,128)(2,1)S(1)}, u32[]{:S(2)}, u32[]{:S(2)}) collective-permute-start(bf16[1792,128]{1,0:T(8,128)(2,1)S(1)} %get-tuple-element.27), channel_id=1, source_target_pairs={{0,8},{8,0},{16,24},{24,16},{1,9},{9,1},{17,25},{25,17},{2,10},{10... | collective-permute-start | bytes 1376264 | tf_op jit(solution)/shard_map/ppermute | solution.py:188
  18.9 21.5 %collective-permute-start.2 = (bf16[1792,128]{1,0:T(8,128)(2,1)S(1)}, bf16[1792,128]{1,0:T(8,128)(2,1)S(1)}, u32[]{:S(2)}, u32[]{:S(2)}) collective-permute-start(bf16[1792,128]{1,0:T(8,128)(2,1)S(1)} %get-tuple-element.28), channel_id=1, source_target_pairs={{0,16},{8,24},{16,0},{24,8},{1,17},{9,25},{17,1},{25,9},{2,18},{10... | collective-permute-start | bytes 1376264 | tf_op jit(solution)/shard_map/ppermute | solution.py:188
  40.4 2.8 %collective-permute-start.6 = (f32[1,128,128]{2,1,0:T(8,128)S(1)}, f32[1,128,128]{2,1,0:T(8,128)S(1)}, u32[]{:S(2)}, u32[]{:S(2)}) collective-permute-start(f32[1,128,128]{2,1,0:T(8,128)S(1)} %convolution_bitcast_fusion), channel_id=1, source_target_pairs={{0,8},{8,0},{16,24},{24,16},{1,9},{9,1},{17,25},{25,17},{2,10},{10... | collective-permute-start | bytes 196616 | tf_op jit(solution)/shard_map/ppermute | solution.py:188
  40.4 49.4 %slice-start = ((s8[8257536]{0:T(1024)(128)(4,1)}), s8[4194304]{0:T(1024)(128)(4,1)S(1)}, s32[]{:S(2)}) async-start(s8[8257536]{0:T(1024)(128)(4,1)} %bitcast.17), calls=%async_computation | async-start | bytes 8388608
  40.7 13.3 %collective-permute-start.5 = (bf16[1792,128]{1,0:T(8,128)(2,1)S(1)}, bf16[1792,128]{1,0:T(8,128)(2,1)S(1)}, u32[]{:S(2)}, u32[]{:S(2)}) collective-permute-start(bf16[1792,128]{1,0:T(8,128)(2,1)S(1)} %get-tuple-element.33), channel_id=1, source_target_pairs={{0,24},{8,16},{16,8},{24,0},{1,25},{9,17},{17,9},{25,1},{2,26},{10... | collective-permute-start | bytes 1376264 | tf_op jit(solution)/shard_map/ppermute | solution.py:188
  43.3 7.0 %collective-permute-start.7 = (f32[3,128,128]{2,1,0:T(8,128)S(1)}, f32[3,128,128]{2,1,0:T(8,128)S(1)}, u32[]{:S(2)}, u32[]{:S(2)}) collective-permute-start(f32[3,128,128]{2,1,0:T(8,128)S(1)} %pad_maximum_fusion), channel_id=1, source_target_pairs={{0,1},{1,0},{2,3},{3,2},{4,5},{5,4},{6,7},{7,6},{8,9},{9,8},{10,11... | collective-permute-start | bytes 589832 | tf_op jit(solution)/shard_map/ppermute | solution.py:188
  44.8 40.5 %collective-permute-start.20 = (bf16[2240,128]{1,0:T(8,128)(2,1)S(1)}, bf16[2240,128]{1,0:T(8,128)(2,1)S(1)}, u32[]{:S(2)}, u32[]{:S(2)}) collective-permute-start(bf16[2240,128]{1,0:T(8,128)(2,1)S(1)} %add_convert_fusion), channel_id=1, source_target_pairs={{0,16},{8,24},{16,0},{24,8},{1,17},{9,25},{17,1},{25,9},{2,18},{10... | collective-permute-start | bytes 1720328 | tf_op jit(solution)/shard_map/ppermute | solution.py:188
  54.1 7.4 %collective-permute-start.9 = (f32[3,128,128]{2,1,0:T(8,128)S(1)}, f32[3,128,128]{2,1,0:T(8,128)S(1)}, u32[]{:S(2)}, u32[]{:S(2)}) collective-permute-start(f32[3,128,128]{2,1,0:T(8,128)S(1)} %fusion.2), channel_id=1, source_target_pairs={{0,2},{1,3},{2,0},{3,1},{4,6},{5,7},{6,4},{7,5},{8,10},{9,11},{10,... | collective-permute-start | bytes 589832 | tf_op jit(solution)/shard_map/ppermute | solution.py:188
  61.5 5.3 %collective-permute-start.10 = (f32[2,128,128]{2,1,0:T(8,128)S(1)}, f32[2,128,128]{2,1,0:T(8,128)S(1)}, u32[]{:S(2)}, u32[]{:S(2)}) collective-permute-start(f32[2,128,128]{2,1,0:T(8,128)S(1)} %fusion.4), channel_id=1, source_target_pairs={{0,1},{1,0},{2,3},{3,2},{4,5},{5,4},{6,7},{7,6},{8,9},{9,8},{10,11... | collective-permute-start | bytes 393224 | tf_op jit(solution)/shard_map/ppermute | solution.py:188
  63.3 14.3 %collective-permute-start.13 = (f32[3,128,128]{2,1,0:T(8,128)S(1)}, f32[3,128,128]{2,1,0:T(8,128)S(1)}, u32[]{:S(2)}, u32[]{:S(2)}) collective-permute-start(f32[3,128,128]{2,1,0:T(8,128)S(1)} %add.155.gram_ref), channel_id=1, source_target_pairs={{0,4},{1,5},{2,6},{3,7},{4,0},{5,1},{6,2},{7,3},{8,12},{9,13},{10,... | collective-permute-start | bytes 589832 | tf_op jit(solution)/shard_map/ppermute | solution.py:188
  66.9 8.1 %collective-permute-start.11 = (f32[2,128,128]{2,1,0:T(8,128)S(1)}, f32[2,128,128]{2,1,0:T(8,128)S(1)}, u32[]{:S(2)}, u32[]{:S(2)}) collective-permute-start(f32[2,128,128]{2,1,0:T(8,128)S(1)} %add.156), channel_id=1, source_target_pairs={{0,2},{1,3},{2,0},{3,1},{4,6},{5,7},{6,4},{7,5},{8,10},{9,11},{10,... | collective-permute-start | bytes 393224 | tf_op jit(solution)/shard_map/ppermute | solution.py:188
  68.7 20.5 %collective-permute-start.8 = (bf16[1792,128]{1,0:T(8,128)(2,1)S(1)}, bf16[1792,128]{1,0:T(8,128)(2,1)S(1)}, u32[]{:S(2)}, u32[]{:S(2)}) collective-permute-start(bf16[1792,128]{1,0:T(8,128)(2,1)S(1)} %add_convert_fusion.1), channel_id=1, source_target_pairs={{0,16},{8,24},{16,0},{24,8},{1,17},{9,25},{17,1},{25,9},{2,18},{10... | collective-permute-start | bytes 1376264 | tf_op jit(solution)/shard_map/ppermute | solution.py:188
  70.4 19.0 %collective-permute-start.18 = (bf16[2240,128]{1,0:T(8,128)(2,1)S(1)}, bf16[2240,128]{1,0:T(8,128)(2,1)S(1)}, u32[]{:S(2)}, u32[]{:S(2)}) collective-permute-start(bf16[2240,128]{1,0:T(8,128)(2,1)S(1)} %add_convert_fusion), channel_id=1, source_target_pairs={{0,8},{8,0},{16,24},{24,16},{1,9},{9,1},{17,25},{25,17},{2,10},{10... | collective-permute-start | bytes 1720328 | tf_op jit(solution)/shard_map/ppermute | solution.py:188
  75.0 14.8 %slice-start.1 = ((s8[8257536]{0:T(1024)(128)(4,1)}), s8[4063232]{0:T(1024)(128)(4,1)S(1)}, s32[]{:S(2)}) async-start(s8[8257536]{0:T(1024)(128)(4,1)} %bitcast.17), calls=%async_computation.1 | async-start | bytes 8126464
  75.0 14.7 %copy-start = (s32[18]{0:T(128)S(1)}, s32[18]{0:T(128)}, u32[]{:S(2)}) copy-start(s32[18]{0:T(128)} %table_ref.7) | copy-start | bytes 220
  75.0 6.4 %collective-permute-start.12 = (f32[2,128,128]{2,1,0:T(8,128)S(1)}, f32[2,128,128]{2,1,0:T(8,128)S(1)}, u32[]{:S(2)}, u32[]{:S(2)}) collective-permute-start(f32[2,128,128]{2,1,0:T(8,128)S(1)} %add.157.gram_ref), channel_id=1, source_target_pairs={{0,4},{1,5},{2,6},{3,7},{4,0},{5,1},{6,2},{7,3},{8,12},{9,13},{10,... | collective-permute-start | bytes 393224 | tf_op jit(solution)/shard_map/ppermute | solution.py:188
  77.6 15.0 %collective-permute-start.16 = (bf16[1792,128]{1,0:T(8,128)(2,1)S(1)}, bf16[1792,128]{1,0:T(8,128)(2,1)S(1)}, u32[]{:S(2)}, u32[]{:S(2)}) collective-permute-start(bf16[1792,128]{1,0:T(8,128)(2,1)S(1)} %add_convert_fusion.1), channel_id=1, source_target_pairs={{0,8},{8,0},{16,24},{24,16},{1,9},{9,1},{17,25},{25,17},{2,10},{10... | collective-permute-start | bytes 1376264 | tf_op jit(solution)/shard_map/ppermute | solution.py:188
  84.8 5.0 %collective-permute-start.17 = (f32[5,128,128]{2,1,0:T(8,128)S(1)}, f32[5,128,128]{2,1,0:T(8,128)S(1)}, u32[]{:S(2)}, u32[]{:S(2)}) collective-permute-start(f32[5,128,128]{2,1,0:T(8,128)S(1)} %shard_map.51.refs_2_), channel_id=1, source_target_pairs={{0,8},{8,0},{16,24},{24,16},{1,9},{9,1},{17,25},{25,17},{2,10},{10... | collective-permute-start | bytes 983048 | tf_op jit(solution)/shard_map/ppermute | solution.py:188
  85.4 12.2 %collective-permute-start.15 = (f32[5,128,128]{2,1,0:T(8,128)S(1)}, f32[5,128,128]{2,1,0:T(8,128)S(1)}, u32[]{:S(2)}, u32[]{:S(2)}) collective-permute-start(f32[5,128,128]{2,1,0:T(8,128)S(1)} %shard_map.51.refs_2_), channel_id=1, source_target_pairs={{0,16},{8,24},{16,0},{24,8},{1,17},{9,25},{17,1},{25,9},{2,18},{10... | collective-permute-start | bytes 983048 | tf_op jit(solution)/shard_map/ppermute | solution.py:188
  89.2 8.3 %collective-permute-start.21 = (bf16[2240,128]{1,0:T(8,128)(2,1)S(1)}, bf16[2240,128]{1,0:T(8,128)(2,1)S(1)}, u32[]{:S(2)}, u32[]{:S(2)}) collective-permute-start(bf16[2240,128]{1,0:T(8,128)(2,1)S(1)} %collective-permute-done.20), channel_id=1, source_target_pairs={{0,8},{8,0},{16,24},{24,16},{1,9},{9,1},{17,25},{25,17},{2,10},{10... | collective-permute-start | bytes 1720328 | tf_op jit(solution)/shard_map/ppermute | solution.py:188
  89.4 12.5 %collective-permute-start.14 = (bf16[1792,128]{1,0:T(8,128)(2,1)S(1)}, bf16[1792,128]{1,0:T(8,128)(2,1)S(1)}, u32[]{:S(2)}, u32[]{:S(2)}) collective-permute-start(bf16[1792,128]{1,0:T(8,128)(2,1)S(1)} %collective-permute-done.8), channel_id=1, source_target_pairs={{0,8},{8,0},{16,24},{24,16},{1,9},{9,1},{17,25},{25,17},{2,10},{10... | collective-permute-start | bytes 1376264 | tf_op jit(solution)/shard_map/ppermute | solution.py:188
  97.5 1.6 %collective-permute-start.19 = (f32[5,128,128]{2,1,0:T(8,128)S(1)}, f32[5,128,128]{2,1,0:T(8,128)S(1)}, u32[]{:S(2)}, u32[]{:S(2)}) collective-permute-start(f32[5,128,128]{2,1,0:T(8,128)S(1)} %collective-permute-done.15.refs_2_), channel_id=1, source_target_pairs={{0,8},{8,0},{16,24},{24,16},{1,9},{9,1},{17,25},{25,17},{2,10},{10... | collective-permute-start | bytes 983048 | tf_op jit(solution)/shard_map/ppermute | solution.py:188

commit v4 on v3

--- a/solution.py
+++ b/solution.py
@@ -26,12 +26,7 @@
     return jnp.dot(left, right, precision=HIGHEST, preferred_element_type=jnp.float32)
 
 
-def newton_kernel(gram_ref, arrived_ref, *refs):
-    *earlier, out_ref = refs
-    skip = 0
-    for ref in earlier:
-        out_ref[: ref.shape[0]] = ref[...]
-        skip = ref.shape[0]
+def newton_kernel(gram_ref, arrived_ref, out_ref):
     items = gram_ref.shape[0]
     rows = lax.broadcasted_iota(jnp.int32, (V, V), 0)
     columns = lax.broadcasted_iota(jnp.int32, (V, V), 1)
@@ -59,26 +54,25 @@
         if index < ITERS - 1:
             grams = [dot32(half, poly) for half, poly in zip(halves, polys)]
     for item in range(items):
-        out_ref[skip + item] = products[item] * scales[item]
-
-
-def newton_schulz(gram, arrived, *earlier):
+        out_ref[item] = products[item] * scales[item]
+
+
+def newton_schulz(gram, arrived):
     items = gram.shape[0]
-    slots = items + sum(q.shape[0] for q in earlier)
     return pl.pallas_call(
         newton_kernel,
-        out_shape=jax.ShapeDtypeStruct((slots, V, V), jnp.float32),
-        in_specs=[pl.BlockSpec(memory_space=pltpu.VMEM)] * (2 + len(earlier)),
+        out_shape=jax.ShapeDtypeStruct((items, V, V), jnp.float32),
+        in_specs=[pl.BlockSpec(memory_space=pltpu.VMEM)] * 2,
         out_specs=pl.BlockSpec(memory_space=pltpu.VMEM),
         cost_estimate=pl.CostEstimate(
             flops=items * 18 * 12 * V**3, bytes_accessed=items * V * V * 12, transcendentals=0
         ),
         compiler_params=pltpu.CompilerParams(vmem_limit_bytes=16 * 1024 * 1024),
-    )(gram, arrived, *earlier)
+    )(gram, arrived)
 
 
 def apply_kernel(layout, place_ref, table_ref, *refs):
-    count, first, base, size, offset, own, total, padded = layout
+    count, first, size, offset, own, total, padded = layout
     sources, qs = refs[:count], refs[count : 2 * count]
     params_ref = refs[2 * count]
     new_ref, update_ref, new_buf, update_buf, new_sems, update_sems = refs[-6:]
@@ -97,7 +91,7 @@
         slot = unit
         if per_block > 1:
             slot = jnp.where(block == whole, whole, block - holder * (whole + 1))
-        return index < total, head, pl.ds(start, unit_rows), base + slot
+        return index < total, head, pl.ds(start, unit_rows), slot
 
     items = [
         (index, unit, index * units + unit, locate(first + index, unit))
@@ -140,7 +134,7 @@
         pl.when(valid)(run) if padded else run()
 
 
-def apply_side(sources, qs, params, previous, place, table, first, base, size, offset, own, padded):
+def apply_side(sources, qs, params, previous, place, table, first, size, offset, own, padded):
     total, rows, width = params.shape
     count = len(sources)
     units, unit_rows = sources[0].shape[:2]
@@ -156,7 +150,7 @@
         operands.append(array)
         in_specs.append(hbm)
     work = steps * unit_rows * width
-    layout = (count, first, base, size, offset, own, total, padded)
+    layout = (count, first, size, offset, own, total, padded)
     return pl.pallas_call(
         functools.partial(apply_kernel, layout),
         in_specs=in_specs,
@@ -245,19 +239,20 @@
 
     size = sizes[0]
     terms = exchange(pieces_of(0, size))
-    seconds = []
     if len(sizes) > 1:
-        pieces = pieces_of(size, sizes[1])
-        terms[-1], *pieces = lax.optimization_barrier((terms[-1], *pieces))
-        *seconds, late = exchange(pieces)
+        offset, length = size, sizes[1] * rows
+        share = length // CORES
+        chunks = [rows_of(member ^ d, offset, 0, length) for d in range(members)]
+        to_core = rows_of(member, offset, 1 - core, share)
+        terms[-1], to_core, *chunks = lax.optimization_barrier((terms[-1], to_core, *chunks))
+        chunks = [swap(chunk, "dp", d * CORES) if d else chunk for d, chunk in enumerate(chunks)]
+        seconds = [rows_of(member, offset, core, share), swap(to_core, "dp", 1)]
 
     first = total_of(terms).astype(jnp.bfloat16)
     whole = size // 2
     if size % 2:
         half = lax.dynamic_slice_in_dim(first, (1 - core) * whole * rows, rows // 2)
         gram = gram_of(half, rows // 2)
-        if seconds:
-            *seconds, gram = lax.optimization_barrier((*seconds, gram))
         gram = gram + swap(gram, "dp", 1)
         if whole:
             full = lax.dynamic_slice_in_dim(first, core * (rows // 2), whole * rows)
@@ -265,48 +260,54 @@
     else:
         gram = gram_of(first, rows)
     totals, qs = [first], []
-    if seconds:
+    first_arrived = over_chips(first)
+    if len(sizes) > 1:
         gram = gram + swap(gram, "shard", 1)
-        late, gram = lax.optimization_barrier((late, gram))
         gram = gram + swap(gram, "shard", 2)
-        second = total_of([*seconds, late]).astype(jnp.bfloat16)
+        *arrived, gram = lax.optimization_barrier((*chunks[1:], gram))
+        for chunk in arrived:
+            seconds.append(lax.dynamic_slice_in_dim(chunk, core * share, share))
+            passed = lax.dynamic_slice_in_dim(chunk, (1 - core) * share, share)
+            seconds.append(swap(passed, "dp", 1))
+        second = total_of(seconds).astype(jnp.bfloat16)
         totals.append(second)
-        gram_second, gram = lax.optimization_barrier((gram_of(second, rows), gram))
-        qs.append(newton_schulz(*reduce_gram(gram, 4)))
-        pair = reduce_gram(gram_second)
-        qs.append(newton_schulz(*pair, qs[0]))
+        gram, arrived = reduce_gram(gram, 4)
+        gram_second = gram_of(second, rows)
+        gram_second = gram_second + swap(gram_second, "shard", 1)
+        arrived, gram_second = lax.optimization_barrier((arrived, gram_second))
+        qs.append(newton_schulz(gram, arrived))
+        gram_second = gram_second + swap(gram_second, "shard", 2)
+        *first_arrived, gram_second = lax.optimization_barrier((*first_arrived, gram_second))
+        qs.append(newton_schulz(*reduce_gram(gram_second, 4)))
     else:
         qs.append(newton_schulz(*reduce_gram(gram)))
 
-    q = qs[-1]
-    arrived_q = over_chips(q)
-    arrived_rows = [over_chips(total) for total in totals]
+    arrived_q = [over_chips(q) for q in qs]
+    arrived_rows = [first_arrived, *(over_chips(total) for total in totals[1:])]
     outputs = []
     for distance in range(members):
+        rows_here, q_here = totals, qs
         if distance:
-            q = arrived_q[distance - 1]
-            if distance == 1:
-                q, *outputs = lax.optimization_barrier((q, *outputs))
-        pair_q = over_cores(q)
+            rows_here = [arrived[distance - 1] for arrived in arrived_rows]
+            q_here = [arrived[distance - 1] for arrived in arrived_q]
+        if distance == 1:
+            rest = (rows_here[-1], *q_here, *outputs)
+            rows_here[-1], *rest = lax.optimization_barrier(rest)
+            q_here, outputs = rest[: len(qs)], rest[len(qs) :]
         for index, size in enumerate(sizes):
-            rows_here = totals[index]
-            if distance:
-                tie = qs[-1] if index == len(sizes) - 1 else pair[0]
-                rows_here = lax.optimization_barrier((arrived_rows[index][distance - 1], tie))[0]
             per_block = 2 if size % 2 else 1
             units = size * per_block // CORES
             outputs = apply_side(
                 [
                     array.reshape(units, rows // per_block, width)
-                    for array in over_cores(rows_here)
+                    for array in over_cores(rows_here[index])
                 ],
-                pair_q,
+                over_cores(q_here[index]),
                 params,
                 outputs,
                 place.reshape(1),
                 table,
                 CORES * distance,
-                qs[index - 1].shape[0] if index else 0,
                 size,
                 sum(sizes[:index]),
                 own,

time: 105 us -> 107 us (1.019)
  local copies, waits for them, and re-layouts: 3.13 us -> 9.01 us
  starting transfers between devices: 27.5 us -> 22.1 us
  other arithmetic: 1.71 us -> 3.03 us
    ppermute x22 -> x25, starting transfers between devices: 27.5 us -> 22.1 us  [swap(): return lax.ppermute(array, axis, [(i, i ^ distance) for i in range(size)])]
    unnamed x6 -> x8, local copies, waits for them, and re-layouts: 0.02 us -> 3.55 us
    dynamic_slice x2 -> x3, local copies, waits for them, and re-layouts: 3.08 us -> 5.39 us  [rows_of(): lax.dynamic_slice_in_dim(flat, (chip * own + offset) * rows + which * len...]
    convert_element_type x1, other arithmetic: 0.24 us -> 1.4 us  [per_device(): second = total_of(seconds).astype(jnp.bfloat16)]
    ppermute x22 -> x25, waiting for transfers between devices: 52.5 us -> 53.3 us  [swap(): return lax.ppermute(array, axis, [(i, i ^ distance) for i in range(size)])]
  transfers between devices with their start and end apart: 22 -> 25, of which waited for: 10 -> 10; matrix products, arithmetic and copies ran while one was open for 4% -> 5% of each run, Pallas kernels for 15% -> 14%
where the time goes in v4:
time: 107 us
  waiting for transfers between devices  53.3 us (50%)
  starting transfers between devices  22.1 us (21%)
  Pallas kernels  17.8 us (17%)
  local copies, waits for them, and re-layouts  9.01 us (8%)
  other arithmetic  3.03 us (3%)
    ppermute x25, waiting for transfers between devices, swap(): return lax.ppermute(array, axis, [(i, i ^ distance) for i in range(size)])  53.3 us
    ppermute x25, starting transfers between devices, swap(): return lax.ppermute(array, axis, [(i, i ^ distance) for i in range(size)])  22.1 us
    pallas_call x4, Pallas kernels, apply_side(): pl.pallas_call(functools.partial(apply_kernel, layout), in_specs=in_specs...  10.6 us
    pallas_call x2, Pallas kernels, newton_schulz(): pl.pallas_call(newton_kernel, out_shape=jax.ShapeDtypeStruct((items, V, V...  7.15 us
    dynamic_slice x3, local copies, waits for them, and re-layouts, rows_of(): lax.dynamic_slice_in_dim(flat, (chip * own + offset) * rows + which * len...  5.39 us
    unnamed x8, local copies, waits for them, and re-layouts  3.55 us
  transfers between devices with their start and end apart: 25, of which 10 were waited for; matrix products, arithmetic and copies ran while one was open for 5% of the time, Pallas kernels for 14%

profile of v4, /device:TPU:0, one launch (start us, length us, event | category | flops | bytes accessed | tf_op | source)
XLA Modules:
  0.0 107.1 jit_solution(3866440710877424551)
XLA Ops:
  0.7 2.3 %constant_dynamic-slice_fusion.2 = (bf16[2240,128]{1,0:T(8,128)(2,1)S(1)}, bf16[2240,128]{1,0:T(8,128)(2,1)S(1)}, bf16[2240,128]{1,0:T(8,128)(2,1)}) fusion(bf16[16128,128]{1,0:T(8,128)(2,1)} %bitcast.29, s32[]{:T(128)S(6)} %select_n.80, s32[]{:T(128)S(6)} %select_n.83, s32[]{:T(128)S(6)} %select_n.74), kind=kLoop, calls=%fused_computation.8 | loop fusion | bytes 3440652 | tf_op jit(solution)/shard_map/dynamic_slice | solution.py:208
  3.1 2.4 %collective-permute-start = (bf16[2240,128]{1,0:T(8,128)(2,1)}, bf16[2240,128]{1,0:T(8,128)(2,1)S(1)}, u32[]{:S(2)}, u32[]{:S(2)}) collective-permute-start(bf16[2240,128]{1,0:T(8,128)(2,1)} %get-tuple-element.44), channel_id=1, source_target_pairs={{0,24},{8,16},{16,8},{24,0},{1,25},{9,17},{17,9},{25,1},{2,26},{10... | collective-permute-start | bytes 1720328 | tf_op jit(solution)/shard_map/ppermute | solution.py:182
  6.2 1.8 %constant_dynamic-slice_fusion.4 = bf16[1792,128]{1,0:T(8,128)(2,1)} fusion(bf16[16128,128]{1,0:T(8,128)(2,1)} %bitcast.30, s32[]{:T(128)S(6)} %select_n.75), kind=kLoop, calls=%fused_computation.10 | loop fusion | bytes 917508 | tf_op jit(solution)/shard_map/dynamic_slice | solution.py:208
  8.0 1.2 %constant_dynamic-slice_fusion.3 = bf16[3584,128]{1,0:T(8,128)(2,1)S(1)} fusion(bf16[16128,128]{1,0:T(8,128)(2,1)} %bitcast.31, s32[]{:T(128)S(6)} %select_n.76), kind=kLoop, calls=%fused_computation.9 | loop fusion | bytes 1835012 | tf_op jit(solution)/shard_map/dynamic_slice | solution.py:208
  9.2 9.9 %collective-permute-done = bf16[2240,128]{1,0:T(8,128)(2,1)S(1)} collective-permute-done((bf16[2240,128]{1,0:T(8,128)(2,1)}, bf16[2240,128]{1,0:T(8,128)(2,1)S(1)}, u32[]{:S(2)}, u32[]{:S(2)}) %collective-permute-start) | collective-permute-done | bytes 573472 | tf_op jit(solution)/shard_map/ppermute | solution.py:182
  19.2 12.5 %collective-permute-done.4 = bf16[2240,128]{1,0:T(8,128)(2,1)} collective-permute-done((bf16[2240,128]{1,0:T(8,128)(2,1)S(1)}, bf16[2240,128]{1,0:T(8,128)(2,1)}, u32[]{:S(2)}, u32[]{:S(2)}) %collective-permute-start.4) | collective-permute-done | bytes 573472 | tf_op jit(solution)/shard_map/ppermute | solution.py:182
  31.6 1.5 %add_convert_fusion = bf16[2240,128]{1,0:T(8,128)(2,1)S(1)} fusion(bf16[2240,128]{1,0:T(8,128)(2,1)S(1)} %collective-permute-done, bf16[2240,128]{1,0:T(8,128)(2,1)} %collective-permute-done.4, bf16[2240,128]{1,0:T(8,128)(2,1)S(1)} %collective-permute-done.3, bf16[16128,128]{1,0:T(8,128)(2,1)} %bitcast.32, s32[]{:T(128)S(6)} %select_n.77), kind=kLoop, calls=%fused_computation | loop fusion | flops 2293760 | bytes 2867204 | tf_op jit(solution)/shard_map/convert_element_type | solution.py:251
  33.5 2.4 %collective-permute-start.2 = (bf16[3584,128]{1,0:T(8,128)(2,1)S(1)}, bf16[3584,128]{1,0:T(8,128)(2,1)S(1)}, u32[]{:S(2)}, u32[]{:S(2)}) collective-permute-start(bf16[3584,128]{1,0:T(8,128)(2,1)S(1)} %constant_dynamic-slice_fusion.3), channel_id=1, source_target_pairs={{0,16},{8,24},{16,0},{24,8},{1,17},{9,25},{17,1},{25,9},{2,18},{10... | collective-permute-start | bytes 2752520 | tf_op jit(solution)/shard_map/ppermute | solution.py:182
  36.3 1.6 %collective-permute-start.6 = (f32[3,128,128]{2,1,0:T(8,128)S(1)}, f32[3,128,128]{2,1,0:T(8,128)S(1)}, u32[]{:S(2)}, u32[]{:S(2)}) collective-permute-start(f32[3,128,128]{2,1,0:T(8,128)S(1)} %pad_maximum_fusion), channel_id=1, source_target_pairs={{0,1},{1,0},{2,3},{3,2},{4,5},{5,4},{6,7},{7,6},{8,9},{9,8},{10,11... | collective-permute-start | bytes 589832 | tf_op jit(solution)/shard_map/ppermute | solution.py:182
  37.8 5.5 %collective-permute-done.6 = f32[3,128,128]{2,1,0:T(8,128)S(1)} collective-permute-done((f32[3,128,128]{2,1,0:T(8,128)S(1)}, f32[3,128,128]{2,1,0:T(8,128)S(1)}, u32[]{:S(2)}, u32[]{:S(2)}) %collective-permute-start.6) | collective-permute-done | bytes 196640 | tf_op jit(solution)/shard_map/ppermute | solution.py:182
  43.3 1.6 %collective-permute-start.7 = (f32[3,128,128]{2,1,0:T(8,128)S(1)}, f32[3,128,128]{2,1,0:T(8,128)S(1)}, u32[]{:S(2)}, u32[]{:S(2)}) collective-permute-start(f32[3,128,128]{2,1,0:T(8,128)S(1)} %fusion.2), channel_id=1, source_target_pairs={{0,2},{1,3},{2,0},{3,1},{4,6},{5,7},{6,4},{7,5},{8,10},{9,11},{10,... | collective-permute-start | bytes 589832 | tf_op jit(solution)/shard_map/ppermute | solution.py:182
  45.0 4.5 %collective-permute-done.7 = f32[3,128,128]{2,1,0:T(8,128)S(1)} collective-permute-done((f32[3,128,128]{2,1,0:T(8,128)S(1)}, f32[3,128,128]{2,1,0:T(8,128)S(1)}, u32[]{:S(2)}, u32[]{:S(2)}) %collective-permute-start.7) | collective-permute-done | bytes 196640 | tf_op jit(solution)/shard_map/ppermute | solution.py:182
  49.6 7.3 %collective-permute-done.2 = bf16[3584,128]{1,0:T(8,128)(2,1)S(1)} collective-permute-done((bf16[3584,128]{1,0:T(8,128)(2,1)S(1)}, bf16[3584,128]{1,0:T(8,128)(2,1)S(1)}, u32[]{:S(2)}, u32[]{:S(2)}) %collective-permute-start.2) | collective-permute-done | bytes 917536 | tf_op jit(solution)/shard_map/ppermute | solution.py:182
  57.0 1.8 %collective-permute-start.13 = (bf16[2240,128]{1,0:T(8,128)(2,1)S(1)}, bf16[2240,128]{1,0:T(8,128)(2,1)S(1)}, u32[]{:S(2)}, u32[]{:S(2)}) collective-permute-start(bf16[2240,128]{1,0:T(8,128)(2,1)S(1)} %add_convert_fusion), channel_id=1, source_target_pairs={{0,16},{8,24},{16,0},{24,8},{1,17},{9,25},{17,1},{25,9},{2,18},{10... | collective-permute-start | bytes 1720328 | tf_op jit(solution)/shard_map/ppermute | solution.py:182
  58.8 2.6 %collective-permute-start.10 = (f32[3,128,128]{2,1,0:T(8,128)S(1)}, f32[3,128,128]{2,1,0:T(8,128)S(1)}, u32[]{:S(2)}, u32[]{:S(2)}) collective-permute-start(f32[3,128,128]{2,1,0:T(8,128)S(1)} %add.138.gram_ref), channel_id=1, source_target_pairs={{0,4},{1,5},{2,6},{3,7},{4,0},{5,1},{6,2},{7,3},{8,12},{9,13},{10,... | collective-permute-start | bytes 589832 | tf_op jit(solution)/shard_map/ppermute | solution.py:182
  61.4 1.4 %add_convert_fusion.1 = bf16[1792,128]{1,0:T(8,128)(2,1)S(1)} fusion(bf16[1792,128]{1,0:T(8,128)(2,1)S(1)} %collective-permute-done.8, bf16[1792,128]{1,0:T(8,128)(2,1)} %collective-permute-done.1, bf16[3584,128]{1,0:T(8,128)(2,1)S(1)} %collective-permute-done.2, s32[]{:T(128)S(6)} %select_n.86, bf16[16128,128]{1,0:T(8,128)(2,1)} %bitcast.33, s32[]{:T(128)S(6)} %select_n.71), kind=kLoop, calls=%fused_computation.2 | loop fusion | flops 1835008 | bytes 2293768 | tf_op jit(solution)/shard_map/convert_element_type | solution.py:272
  63.1 1.6 %collective-permute-start.11 = (f32[2,128,128]{2,1,0:T(8,128)S(1)}, f32[2,128,128]{2,1,0:T(8,128)S(1)}, u32[]{:S(2)}, u32[]{:S(2)}) collective-permute-start(f32[2,128,128]{2,1,0:T(8,128)S(1)} %fusion.4), channel_id=1, source_target_pairs={{0,1},{1,0},{2,3},{3,2},{4,5},{5,4},{6,7},{7,6},{8,9},{9,8},{10,11... | collective-permute-start | bytes 393224 | tf_op jit(solution)/shard_map/ppermute | solution.py:182
  64.7 3.8 %collective-permute-done.11 = f32[2,128,128]{2,1,0:T(8,128)S(1)} collective-permute-done((f32[2,128,128]{2,1,0:T(8,128)S(1)}, f32[2,128,128]{2,1,0:T(8,128)S(1)}, u32[]{:S(2)}, u32[]{:S(2)}) %collective-permute-start.11) | collective-permute-done | bytes 131104 | tf_op jit(solution)/shard_map/ppermute | solution.py:182
  68.5 2.4 %collective-permute-done.10.arrived_ref = f32[3,128,128]{2,1,0:T(8,128)S(1)} collective-permute-done((f32[3,128,128]{2,1,0:T(8,128)S(1)}, f32[3,128,128]{2,1,0:T(8,128)S(1)}, u32[]{:S(2)}, u32[]{:S(2)}) %collective-permute-start.10) | collective-permute-done | bytes 196640 | tf_op jit(solution)/shard_map/ppermute | solution.py:182
  70.8 0.7 collective-permute-start.14
  72.0 3.8 %collective-permute-done.14 = f32[2,128,128]{2,1,0:T(8,128)S(1)} collective-permute-done((f32[2,128,128]{2,1,0:T(8,128)S(1)}, f32[2,128,128]{2,1,0:T(8,128)S(1)}, u32[]{:S(2)}, u32[]{:S(2)}) %collective-permute-start.14) | collective-permute-done | bytes 131104 | tf_op jit(solution)/shard_map/ppermute | solution.py:182
  75.9 2.8 %collective-permute-start.15 = (f32[2,128,128]{2,1,0:T(8,128)S(1)}, f32[2,128,128]{2,1,0:T(8,128)S(1)}, u32[]{:S(2)}, u32[]{:S(2)}) collective-permute-start(f32[2,128,128]{2,1,0:T(8,128)S(1)} %add.144.gram_ref), channel_id=1, source_target_pairs={{0,4},{1,5},{2,6},{3,7},{4,0},{5,1},{6,2},{7,3},{8,12},{9,13},{10,... | collective-permute-start | bytes 393224 | tf_op jit(solution)/shard_map/ppermute | solution.py:182
  78.7 3.8 %shard_map.50.refs_2_ = f32[3,128,128]{2,1,0:T(8,128)S(1)} custom-call(f32[3,128,128]{2,1,0:T(8,128)S(1)} %add.138.gram_ref, f32[3,128,128]{2,1,0:T(8,128)S(1)} %collective-permute-done.10.arrived_ref), custom_call_target="tpu_custom_call" | custom-call | flops 1358954496 | bytes 589824 | tf_op jit(solution)/shard_map/pallas_call | solution.py:62
  82.6 2.1 %collective-permute-done.15.arrived_ref = f32[2,128,128]{2,1,0:T(8,128)S(1)} collective-permute-done((f32[2,128,128]{2,1,0:T(8,128)S(1)}, f32[2,128,128]{2,1,0:T(8,128)S(1)}, u32[]{:S(2)}, u32[]{:S(2)}) %collective-permute-start.15) | collective-permute-done | bytes 131104 | tf_op jit(solution)/shard_map/ppermute | solution.py:182
  85.2 3.4 %shard_map.51.refs_2_ = f32[2,128,128]{2,1,0:T(8,128)S(1)} custom-call(f32[2,128,128]{2,1,0:T(8,128)S(1)} %add.144.gram_ref, f32[2,128,128]{2,1,0:T(8,128)S(1)} %collective-permute-done.15.arrived_ref), custom_call_target="tpu_custom_call" | custom-call | flops 905969664 | bytes 393216 | tf_op jit(solution)/shard_map/pallas_call | solution.py:62
  89.2 1.5 %collective-permute-start.16 = (f32[2,128,128]{2,1,0:T(8,128)S(1)}, f32[2,128,128]{2,1,0:T(8,128)S(1)}, u32[]{:S(2)}, u32[]{:S(2)}) collective-permute-start(f32[2,128,128]{2,1,0:T(8,128)S(1)} %shard_map.51.refs_2_), channel_id=1, source_target_pairs={{0,16},{8,24},{16,0},{24,8},{1,17},{9,25},{17,1},{25,9},{2,18},{10... | collective-permute-start | bytes 393224 | tf_op jit(solution)/shard_map/ppermute | solution.py:182
  90.7 3.3 %copy-done = f32[18,896,128]{2,1,0:T(8,128)S(1)} copy-done((f32[18,896,128]{2,1,0:T(8,128)S(1)}, f32[18,896,128]{2,1,0:T(8,128)}, u32[]{:S(2)}) %copy-start) | copy-done | bytes 8257560
  94.0 2.8 %shard_map.52 = (f32[18,896,128]{2,1,0:T(8,128)}, bf16[18,896,128]{2,1,0:T(8,128)(2,1)}) custom-call(s32[1]{0:T(128)} %bitcast.place_ref, s32[18]{0:T(128)S(1)} %copy-done.1, bf16[5,448,128]{2,1,0:T(8,128)(2,1)S(1)} %bitcast.21, bf16[5,448,128]{2,1,0:T(8,128)(2,1)S(1)} %bitcast.22, f32[3,128,128]{2,1,0:T(8,128)S(1)} %shard_map.50.refs_2_, ...), custom_call_target="tpu_custom_call" | custom-call | flops 293601280 | bytes 6881280 | tf_op jit(solution)/shard_map/pallas_call | solution.py:154
  97.0 2.5 %shard_map.53 = (f32[18,896,128]{2,1,0:T(8,128)}, bf16[18,896,128]{2,1,0:T(8,128)(2,1)}) custom-call(s32[1]{0:T(128)} %bitcast.place_ref, s32[18]{0:T(128)S(1)} %copy-done.1, bf16[2,896,128]{2,1,0:T(8,128)(2,1)S(1)} %bitcast.20, bf16[2,896,128]{2,1,0:T(8,128)(2,1)S(1)} %bitcast.26, ...), custom_call_target="tpu_custom_call", output_to_operand_aliasing={{0}: (7, {}), {1}: (8, {})} | custom-call | flops 234881024 | bytes 5505024 | tf_op jit(solution)/shard_map/pallas_call | solution.py:154
  100.3 1.5 %collective-permute-done.24.refs_3_ = f32[3,128,128]{2,1,0:T(8,128)S(1)} collective-permute-done((f32[3,128,128]{2,1,0:T(8,128)S(1)}, f32[3,128,128]{2,1,0:T(8,128)S(1)}, u32[]{:S(2)}, u32[]{:S(2)}) %collective-permute-start.24) | collective-permute-done | bytes 196640 | tf_op jit(solution)/shard_map/ppermute | solution.py:182
  101.8 2.8 %shard_map.54 = (f32[18,896,128]{2,1,0:T(8,128)}, bf16[18,896,128]{2,1,0:T(8,128)(2,1)}) custom-call(s32[1]{0:T(128)} %bitcast.place_ref, s32[18]{0:T(128)S(1)} %copy-done.1, bf16[5,448,128]{2,1,0:T(8,128)(2,1)S(1)} %bitcast.23, bf16[5,448,128]{2,1,0:T(8,128)(2,1)S(1)} %bitcast.24, ...), custom_call_target="tpu_custom_call", output_to_operand_aliasing={{0}: (7, {}), {1}: (8, {})} | custom-call | flops 293601280 | bytes 6881280 | tf_op jit(solution)/shard_map/pallas_call | solution.py:154
  104.6 2.6 %shard_map.55 = (f32[18,896,128]{2,1,0:T(8,128)}, bf16[18,896,128]{2,1,0:T(8,128)(2,1)}) custom-call(s32[1]{0:T(128)} %bitcast.place_ref, s32[18]{0:T(128)S(1)} %copy-done.1, bf16[2,896,128]{2,1,0:T(8,128)(2,1)S(1)} %bitcast.25, bf16[2,896,128]{2,1,0:T(8,128)(2,1)S(1)} %bitcast.27, ...), custom_call_target="tpu_custom_call", output_to_operand_aliasing={{0}: (7, {}), {1}: (8, {})} | custom-call | flops 234881024 | bytes 5505024 | tf_op jit(solution)/shard_map/pallas_call | solution.py:154
  (49 shorter events, 4.4 us)
Async XLA Ops:
  3.1 16.1 %collective-permute-start = (bf16[2240,128]{1,0:T(8,128)(2,1)}, bf16[2240,128]{1,0:T(8,128)(2,1)S(1)}, u32[]{:S(2)}, u32[]{:S(2)}) collective-permute-start(bf16[2240,128]{1,0:T(8,128)(2,1)} %get-tuple-element.44), channel_id=1, source_target_pairs={{0,24},{8,16},{16,8},{24,0},{1,25},{9,17},{17,9},{25,1},{2,26},{10... | collective-permute-start | bytes 1720328 | tf_op jit(solution)/shard_map/ppermute | solution.py:182
  5.5 13.7 %collective-permute-start.3 = (bf16[2240,128]{1,0:T(8,128)(2,1)S(1)}, bf16[2240,128]{1,0:T(8,128)(2,1)S(1)}, u32[]{:S(2)}, u32[]{:S(2)}) collective-permute-start(bf16[2240,128]{1,0:T(8,128)(2,1)S(1)} %get-tuple-element.42), channel_id=1, source_target_pairs={{0,8},{8,0},{16,24},{24,16},{1,9},{9,1},{17,25},{25,17},{2,10},{10... | collective-permute-start | bytes 1720328 | tf_op jit(solution)/shard_map/ppermute | solution.py:182
  6.2 25.5 %collective-permute-start.4 = (bf16[2240,128]{1,0:T(8,128)(2,1)S(1)}, bf16[2240,128]{1,0:T(8,128)(2,1)}, u32[]{:S(2)}, u32[]{:S(2)}) collective-permute-start(bf16[2240,128]{1,0:T(8,128)(2,1)S(1)} %get-tuple-element.43), channel_id=1, source_target_pairs={{0,16},{8,24},{16,0},{24,8},{1,17},{9,25},{17,1},{25,9},{2,18},{10... | collective-permute-start | bytes 1720328 | tf_op jit(solution)/shard_map/ppermute | solution.py:182
  33.4 2.8 %collective-permute-start.5 = (f32[1,128,128]{2,1,0:T(8,128)S(1)}, f32[1,128,128]{2,1,0:T(8,128)S(1)}, u32[]{:S(2)}, u32[]{:S(2)}) collective-permute-start(f32[1,128,128]{2,1,0:T(8,128)S(1)} %convolution_bitcast_fusion), channel_id=1, source_target_pairs={{0,8},{8,0},{16,24},{24,16},{1,9},{9,1},{17,25},{25,17},{2,10},{10... | collective-permute-start | bytes 196616 | tf_op jit(solution)/shard_map/ppermute | solution.py:182
  33.5 23.3 %collective-permute-start.2 = (bf16[3584,128]{1,0:T(8,128)(2,1)S(1)}, bf16[3584,128]{1,0:T(8,128)(2,1)S(1)}, u32[]{:S(2)}, u32[]{:S(2)}) collective-permute-start(bf16[3584,128]{1,0:T(8,128)(2,1)S(1)} %constant_dynamic-slice_fusion.3), channel_id=1, source_target_pairs={{0,16},{8,24},{16,0},{24,8},{1,17},{9,25},{17,1},{25,9},{2,18},{10... | collective-permute-start | bytes 2752520 | tf_op jit(solution)/shard_map/ppermute | solution.py:182
  36.3 7.0 %collective-permute-start.6 = (f32[3,128,128]{2,1,0:T(8,128)S(1)}, f32[3,128,128]{2,1,0:T(8,128)S(1)}, u32[]{:S(2)}, u32[]{:S(2)}) collective-permute-start(f32[3,128,128]{2,1,0:T(8,128)S(1)} %pad_maximum_fusion), channel_id=1, source_target_pairs={{0,1},{1,0},{2,3},{3,2},{4,5},{5,4},{6,7},{7,6},{8,9},{9,8},{10,11... | collective-permute-start | bytes 589832 | tf_op jit(solution)/shard_map/ppermute | solution.py:182
  43.3 6.2 %collective-permute-start.7 = (f32[3,128,128]{2,1,0:T(8,128)S(1)}, f32[3,128,128]{2,1,0:T(8,128)S(1)}, u32[]{:S(2)}, u32[]{:S(2)}) collective-permute-start(f32[3,128,128]{2,1,0:T(8,128)S(1)} %fusion.2), channel_id=1, source_target_pairs={{0,2},{1,3},{2,0},{3,1},{4,6},{5,7},{6,4},{7,5},{8,10},{9,11},{10,... | collective-permute-start | bytes 589832 | tf_op jit(solution)/shard_map/ppermute | solution.py:182
  45.0 16.4 %collective-permute-start.1 = (bf16[1792,128]{1,0:T(8,128)(2,1)}, bf16[1792,128]{1,0:T(8,128)(2,1)}, u32[]{:S(2)}, u32[]{:S(2)}) collective-permute-start(bf16[1792,128]{1,0:T(8,128)(2,1)} %constant_dynamic-slice_fusion.4), channel_id=1, source_target_pairs={{0,8},{8,0},{16,24},{24,16},{1,9},{9,1},{17,25},{25,17},{2,10},{10... | collective-permute-start | bytes 1376264 | tf_op jit(solution)/shard_map/ppermute | solution.py:182
  56.9 4.5 %collective-permute-start.8 = (bf16[1792,128]{1,0:T(8,128)(2,1)S(1)}, bf16[1792,128]{1,0:T(8,128)(2,1)S(1)}, u32[]{:S(2)}, u32[]{:S(2)}) collective-permute-start(bf16[1792,128]{1,0:T(8,128)(2,1)S(1)} %constant_dynamic-slice_fusion.6), channel_id=1, source_target_pairs={{0,8},{8,0},{16,24},{24,16},{1,9},{9,1},{17,25},{25,17},{2,10},{10... | collective-permute-start | bytes 1376264 | tf_op jit(solution)/shard_map/ppermute | solution.py:182
  57.0 18.9 %collective-permute-start.13 = (bf16[2240,128]{1,0:T(8,128)(2,1)S(1)}, bf16[2240,128]{1,0:T(8,128)(2,1)S(1)}, u32[]{:S(2)}, u32[]{:S(2)}) collective-permute-start(bf16[2240,128]{1,0:T(8,128)(2,1)S(1)} %add_convert_fusion), channel_id=1, source_target_pairs={{0,16},{8,24},{16,0},{24,8},{1,17},{9,25},{17,1},{25,9},{2,18},{10... | collective-permute-start | bytes 1720328 | tf_op jit(solution)/shard_map/ppermute | solution.py:182
  58.8 12.1 %collective-permute-start.10 = (f32[3,128,128]{2,1,0:T(8,128)S(1)}, f32[3,128,128]{2,1,0:T(8,128)S(1)}, u32[]{:S(2)}, u32[]{:S(2)}) collective-permute-start(f32[3,128,128]{2,1,0:T(8,128)S(1)} %add.138.gram_ref), channel_id=1, source_target_pairs={{0,4},{1,5},{2,6},{3,7},{4,0},{5,1},{6,2},{7,3},{8,12},{9,13},{10,... | collective-permute-start | bytes 589832 | tf_op jit(solution)/shard_map/ppermute | solution.py:182
  63.1 5.3 %collective-permute-start.11 = (f32[2,128,128]{2,1,0:T(8,128)S(1)}, f32[2,128,128]{2,1,0:T(8,128)S(1)}, u32[]{:S(2)}, u32[]{:S(2)}) collective-permute-start(f32[2,128,128]{2,1,0:T(8,128)S(1)} %fusion.4), channel_id=1, source_target_pairs={{0,1},{1,0},{2,3},{3,2},{4,5},{5,4},{6,7},{7,6},{8,9},{9,8},{10,11... | collective-permute-start | bytes 393224 | tf_op jit(solution)/shard_map/ppermute | solution.py:182
  64.7 23.9 %collective-permute-start.19 = (bf16[2240,128]{1,0:T(8,128)(2,1)S(1)}, bf16[2240,128]{1,0:T(8,128)(2,1)S(1)}, u32[]{:S(2)}, u32[]{:S(2)}) collective-permute-start(bf16[2240,128]{1,0:T(8,128)(2,1)S(1)} %add_convert_fusion), channel_id=1, source_target_pairs={{0,8},{8,0},{16,24},{24,16},{1,9},{9,1},{17,25},{25,17},{2,10},{10... | collective-permute-start | bytes 1720328 | tf_op jit(solution)/shard_map/ppermute | solution.py:182
  70.8 5.0 %collective-permute-start.14 = (f32[2,128,128]{2,1,0:T(8,128)S(1)}, f32[2,128,128]{2,1,0:T(8,128)S(1)}, u32[]{:S(2)}, u32[]{:S(2)}) collective-permute-start(f32[2,128,128]{2,1,0:T(8,128)S(1)} %add.143), channel_id=1, source_target_pairs={{0,2},{1,3},{2,0},{3,1},{4,6},{5,7},{6,4},{7,5},{8,10},{9,11},{10,... | collective-permute-start | bytes 393224 | tf_op jit(solution)/shard_map/ppermute | solution.py:182
  71.5 17.6 %collective-permute-start.17 = (bf16[1792,128]{1,0:T(8,128)(2,1)S(1)}, bf16[1792,128]{1,0:T(8,128)(2,1)S(1)}, u32[]{:S(2)}, u32[]{:S(2)}) collective-permute-start(bf16[1792,128]{1,0:T(8,128)(2,1)S(1)} %add_convert_fusion.1), channel_id=1, source_target_pairs={{0,8},{8,0},{16,24},{24,16},{1,9},{9,1},{17,25},{25,17},{2,10},{10... | collective-permute-start | bytes 1376264 | tf_op jit(solution)/shard_map/ppermute | solution.py:182
  71.5 28.1 %collective-permute-start.9 = (bf16[1792,128]{1,0:T(8,128)(2,1)S(1)}, bf16[1792,128]{1,0:T(8,128)(2,1)S(1)}, u32[]{:S(2)}, u32[]{:S(2)}) collective-permute-start(bf16[1792,128]{1,0:T(8,128)(2,1)S(1)} %add_convert_fusion.1), channel_id=1, source_target_pairs={{0,16},{8,24},{16,0},{24,8},{1,17},{9,25},{17,1},{25,9},{2,18},{10... | collective-permute-start | bytes 1376264 | tf_op jit(solution)/shard_map/ppermute | solution.py:182
  75.8 14.9 %copy-start.1 = (s32[18]{0:T(128)S(1)}, s32[18]{0:T(128)}, u32[]{:S(2)}) copy-start(s32[18]{0:T(128)} %table_ref.7) | copy-start | bytes 220
  75.9 8.8 %collective-permute-start.15 = (f32[2,128,128]{2,1,0:T(8,128)S(1)}, f32[2,128,128]{2,1,0:T(8,128)S(1)}, u32[]{:S(2)}, u32[]{:S(2)}) collective-permute-start(f32[2,128,128]{2,1,0:T(8,128)S(1)} %add.144.gram_ref), channel_id=1, source_target_pairs={{0,4},{1,5},{2,6},{3,7},{4,0},{5,1},{6,2},{7,3},{8,12},{9,13},{10,... | collective-permute-start | bytes 393224 | tf_op jit(solution)/shard_map/ppermute | solution.py:182
  78.7 18.1 %slice-start = ((s8[8257536]{0:T(1024)(128)(4,1)}), s8[4194304]{0:T(1024)(128)(4,1)S(1)}, s32[]{:S(2)}) async-start(s8[8257536]{0:T(1024)(128)(4,1)} %bitcast.17), calls=%async_computation | async-start | bytes 8388608
  82.5 6.2 %collective-permute-start.20 = (f32[3,128,128]{2,1,0:T(8,128)S(1)}, f32[3,128,128]{2,1,0:T(8,128)S(1)}, u32[]{:S(2)}, u32[]{:S(2)}) collective-permute-start(f32[3,128,128]{2,1,0:T(8,128)S(1)} %shard_map.50.refs_2_), channel_id=1, source_target_pairs={{0,8},{8,0},{16,24},{24,16},{1,9},{9,1},{17,25},{25,17},{2,10},{10... | collective-permute-start | bytes 589832 | tf_op jit(solution)/shard_map/ppermute | solution.py:182
  84.7 14.9 %collective-permute-start.12 = (f32[3,128,128]{2,1,0:T(8,128)S(1)}, f32[3,128,128]{2,1,0:T(8,128)S(1)}, u32[]{:S(2)}, u32[]{:S(2)}) collective-permute-start(f32[3,128,128]{2,1,0:T(8,128)S(1)} %shard_map.50.refs_2_), channel_id=1, source_target_pairs={{0,16},{8,24},{16,0},{24,8},{1,17},{9,25},{17,1},{25,9},{2,18},{10... | collective-permute-start | bytes 589832 | tf_op jit(solution)/shard_map/ppermute | solution.py:182
  88.6 8.2 %collective-permute-start.18 = (f32[2,128,128]{2,1,0:T(8,128)S(1)}, f32[2,128,128]{2,1,0:T(8,128)S(1)}, u32[]{:S(2)}, u32[]{:S(2)}) collective-permute-start(f32[2,128,128]{2,1,0:T(8,128)S(1)} %shard_map.51.refs_2_), channel_id=1, source_target_pairs={{0,8},{8,0},{16,24},{24,16},{1,9},{9,1},{17,25},{25,17},{2,10},{10... | collective-permute-start | bytes 393224 | tf_op jit(solution)/shard_map/ppermute | solution.py:182
  88.7 13.1 %collective-permute-start.23 = (bf16[2240,128]{1,0:T(8,128)(2,1)S(1)}, bf16[2240,128]{1,0:T(8,128)(2,1)S(1)}, u32[]{:S(2)}, u32[]{:S(2)}) collective-permute-start(bf16[2240,128]{1,0:T(8,128)(2,1)S(1)} %collective-permute-done.13), channel_id=1, source_target_pairs={{0,8},{8,0},{16,24},{24,16},{1,9},{9,1},{17,25},{25,17},{2,10},{10... | collective-permute-start | bytes 1720328 | tf_op jit(solution)/shard_map/ppermute | solution.py:182
  89.2 10.4 %collective-permute-start.16 = (f32[2,128,128]{2,1,0:T(8,128)S(1)}, f32[2,128,128]{2,1,0:T(8,128)S(1)}, u32[]{:S(2)}, u32[]{:S(2)}) collective-permute-start(f32[2,128,128]{2,1,0:T(8,128)S(1)} %shard_map.51.refs_2_), channel_id=1, source_target_pairs={{0,16},{8,24},{16,0},{24,8},{1,17},{9,25},{17,1},{25,9},{2,18},{10... | collective-permute-start | bytes 393224 | tf_op jit(solution)/shard_map/ppermute | solution.py:182
  90.7 3.3 %copy-start = (f32[18,896,128]{2,1,0:T(8,128)S(1)}, f32[18,896,128]{2,1,0:T(8,128)}, u32[]{:S(2)}) copy-start(f32[18,896,128]{2,1,0:T(8,128)} %refs_4_.7) | copy-start | bytes 24772612
  94.0 3.0 %slice-start.1 = ((s8[8257536]{0:T(1024)(128)(4,1)}), s8[4063232]{0:T(1024)(128)(4,1)S(1)}, s32[]{:S(2)}) async-start(s8[8257536]{0:T(1024)(128)(4,1)} %bitcast.17), calls=%async_computation.1 | async-start | bytes 8126464
  99.6 5.0 %collective-permute-start.21 = (bf16[1792,128]{1,0:T(8,128)(2,1)S(1)}, bf16[1792,128]{1,0:T(8,128)(2,1)S(1)}, u32[]{:S(2)}, u32[]{:S(2)}) collective-permute-start(bf16[1792,128]{1,0:T(8,128)(2,1)S(1)} %collective-permute-done.9), channel_id=1, source_target_pairs={{0,8},{8,0},{16,24},{24,16},{1,9},{9,1},{17,25},{25,17},{2,10},{10... | collective-permute-start | bytes 1376264 | tf_op jit(solution)/shard_map/ppermute | solution.py:182
  99.7 2.1 %collective-permute-start.24 = (f32[3,128,128]{2,1,0:T(8,128)S(1)}, f32[3,128,128]{2,1,0:T(8,128)S(1)}, u32[]{:S(2)}, u32[]{:S(2)}) collective-permute-start(f32[3,128,128]{2,1,0:T(8,128)S(1)} %collective-permute-done.12.refs_2_), channel_id=1, source_target_pairs={{0,8},{8,0},{16,24},{24,16},{1,9},{9,1},{17,25},{25,17},{2,10},{10... | collective-permute-start | bytes 589832 | tf_op jit(solution)/shard_map/ppermute | solution.py:182
  100.2 4.4 %collective-permute-start.22 = (f32[2,128,128]{2,1,0:T(8,128)S(1)}, f32[2,128,128]{2,1,0:T(8,128)S(1)}, u32[]{:S(2)}, u32[]{:S(2)}) collective-permute-start(f32[2,128,128]{2,1,0:T(8,128)S(1)} %collective-permute-done.16.refs_2_), channel_id=1, source_target_pairs={{0,8},{8,0},{16,24},{24,16},{1,9},{9,1},{17,25},{25,17},{2,10},{10... | collective-permute-start | bytes 393224 | tf_op jit(solution)/shard_map/ppermute | solution.py:182

commit v5 on v3

--- a/solution.py
+++ b/solution.py
@@ -256,8 +256,6 @@
     if size % 2:
         half = lax.dynamic_slice_in_dim(first, (1 - core) * whole * rows, rows // 2)
         gram = gram_of(half, rows // 2)
-        if seconds:
-            *seconds, gram = lax.optimization_barrier((*seconds, gram))
         gram = gram + swap(gram, "dp", 1)
         if whole:
             full = lax.dynamic_slice_in_dim(first, core * (rows // 2), whole * rows)
@@ -266,6 +264,7 @@
         gram = gram_of(first, rows)
     totals, qs = [first], []
     if seconds:
+        *seconds, gram = lax.optimization_barrier((*seconds, gram))
         gram = gram + swap(gram, "shard", 1)
         late, gram = lax.optimization_barrier((late, gram))
         gram = gram + swap(gram, "shard", 2)

time: 105 us -> 99.8 us (0.950)
  starting transfers between devices: 27.5 us -> 23.3 us
    ppermute x22, starting transfers between devices: 27.5 us -> 23.3 us  [swap(): return lax.ppermute(array, axis, [(i, i ^ distance) for i in range(size)])]
  transfers between devices with their start and end apart: 22 -> 22, of which waited for: 10 -> 11; matrix products, arithmetic and copies ran while one was open for 4% -> 4% of each run, Pallas kernels for 15% -> 15%
where the time goes in v5:
time: 99.8 us; the launch traced here: 99.6 us
  waiting for transfers between devices  51.8 us (52%)
  starting transfers between devices  23.3 us (23%)
  Pallas kernels  17.8 us (18%)
  local copies, waits for them, and re-layouts  3.13 us (3%)
  other arithmetic  1.7 us (2%)
    ppermute x22, waiting for transfers between devices, swap(): return lax.ppermute(array, axis, [(i, i ^ distance) for i in range(size)])  51.8 us
    ppermute x22, starting transfers between devices, swap(): return lax.ppermute(array, axis, [(i, i ^ distance) for i in range(size)])  23.3 us
    pallas_call x4, Pallas kernels, apply_side(): pl.pallas_call(functools.partial(apply_kernel, layout), in_specs=in_specs...  10.6 us
    pallas_call x2, Pallas kernels, newton_schulz(): pl.pallas_call(newton_kernel, out_shape=jax.ShapeDtypeStruct((slots, V, V...  7.15 us
    dynamic_slice x2, local copies, waits for them, and re-layouts, rows_of(): lax.dynamic_slice_in_dim(flat, (chip * own + offset) * rows + which * len...  3.08 us
  transfers between devices with their start and end apart: 22, of which 11 were waited for; matrix products, arithmetic and copies ran while one was open for 4% of the time, Pallas kernels for 15%

profile of v5, /device:TPU:0, one launch (start us, length us, event | category | flops | bytes accessed | tf_op | source)
XLA Modules:
  0.0 99.6 jit_solution(11837109835206646787)
XLA Ops:
  0.7 1.5 %constant_dynamic-slice_fusion.2 = (bf16[2240,128]{1,0:T(8,128)(2,1)S(1)}, bf16[2240,128]{1,0:T(8,128)(2,1)S(1)}, bf16[2240,128]{1,0:T(8,128)(2,1)S(1)}) fusion(bf16[16128,128]{1,0:T(8,128)(2,1)} %bitcast.29, s32[]{:T(128)S(6)} %select_n.90, s32[]{:T(128)S(6)} %select_n.91, s32[]{:T(128)S(6)} %select_n.78), kind=kLoop, calls=%fused_computation.8 | loop fusion | bytes 3440652 | tf_op jit(solution)/shard_map/dynamic_slice | solution.py:214
  2.3 2.5 %collective-permute-start = (bf16[2240,128]{1,0:T(8,128)(2,1)S(1)}, bf16[2240,128]{1,0:T(8,128)(2,1)S(1)}, u32[]{:S(2)}, u32[]{:S(2)}) collective-permute-start(bf16[2240,128]{1,0:T(8,128)(2,1)S(1)} %get-tuple-element.52), channel_id=1, source_target_pairs={{0,24},{8,16},{16,8},{24,0},{1,25},{9,17},{17,9},{25,1},{2,26},{10... | collective-permute-start | bytes 1720328 | tf_op jit(solution)/shard_map/ppermute | solution.py:188
  5.5 1.6 %constant_dynamic-slice_fusion.3 = (bf16[1792,128]{1,0:T(8,128)(2,1)S(1)}, bf16[1792,128]{1,0:T(8,128)(2,1)S(1)}, bf16[1792,128]{1,0:T(8,128)(2,1)S(1)}, bf16[1792,128]{1,0:T(8,128)(2,1)S(1)}) fusion(bf16[16128,128]{1,0:T(8,128)(2,1)} %bitcast.30, s32[]{:T(128)S(6)} %select_n.88, s32[]{:T(128)S(6)} %select_n.87, s32[]{:T(128)S(6)} %select_n.84, s32[]{:T(128)S(6)} %select_n.81), kind=kLoop, calls=%fused_computation.9 | loop fusion | bytes 3670032 | tf_op jit(solution)/shard_map/dynamic_slice | solution.py:214
  7.0 11.1 %collective-permute-done = bf16[2240,128]{1,0:T(8,128)(2,1)S(1)} collective-permute-done((bf16[2240,128]{1,0:T(8,128)(2,1)S(1)}, bf16[2240,128]{1,0:T(8,128)(2,1)S(1)}, u32[]{:S(2)}, u32[]{:S(2)}) %collective-permute-start) | collective-permute-done | bytes 573472 | tf_op jit(solution)/shard_map/ppermute | solution.py:188
  18.1 0.8 collective-permute-start.1
  18.9 1.8 %collective-permute-start.2 = (bf16[1792,128]{1,0:T(8,128)(2,1)S(1)}, bf16[1792,128]{1,0:T(8,128)(2,1)S(1)}, u32[]{:S(2)}, u32[]{:S(2)}) collective-permute-start(bf16[1792,128]{1,0:T(8,128)(2,1)S(1)} %get-tuple-element.28), channel_id=1, source_target_pairs={{0,16},{8,24},{16,0},{24,8},{1,17},{9,25},{17,1},{25,9},{2,18},{10... | collective-permute-start | bytes 1376264 | tf_op jit(solution)/shard_map/ppermute | solution.py:188
  20.7 10.7 %collective-permute-done.4 = bf16[2240,128]{1,0:T(8,128)(2,1)S(1)} collective-permute-done((bf16[2240,128]{1,0:T(8,128)(2,1)S(1)}, bf16[2240,128]{1,0:T(8,128)(2,1)S(1)}, u32[]{:S(2)}, u32[]{:S(2)}) %collective-permute-start.4) | collective-permute-done | bytes 573472 | tf_op jit(solution)/shard_map/ppermute | solution.py:188
  31.4 1.4 %add_convert_fusion = bf16[2240,128]{1,0:T(8,128)(2,1)S(1)} fusion(bf16[2240,128]{1,0:T(8,128)(2,1)S(1)} %collective-permute-done, bf16[2240,128]{1,0:T(8,128)(2,1)S(1)} %collective-permute-done.4, bf16[2240,128]{1,0:T(8,128)(2,1)S(1)} %collective-permute-done.3, bf16[16128,128]{1,0:T(8,128)(2,1)} %bitcast.31, s32[]{:T(128)S(6)} %select_n.89), kind=kLoop, calls=%fused_computation | loop fusion | flops 2293760 | bytes 2867204 | tf_op jit(solution)/shard_map/convert_element_type | solution.py:254
  33.1 1.6 %collective-permute-start.6 = (bf16[1792,128]{1,0:T(8,128)(2,1)S(1)}, bf16[1792,128]{1,0:T(8,128)(2,1)S(1)}, u32[]{:S(2)}, u32[]{:S(2)}) collective-permute-start(bf16[1792,128]{1,0:T(8,128)(2,1)S(1)} %get-tuple-element.33), channel_id=1, source_target_pairs={{0,24},{8,16},{16,8},{24,0},{1,25},{9,17},{17,9},{25,1},{2,26},{10... | collective-permute-start | bytes 1376264 | tf_op jit(solution)/shard_map/ppermute | solution.py:188
  35.1 6.1 %collective-permute-done.2 = bf16[1792,128]{1,0:T(8,128)(2,1)S(1)} collective-permute-done((bf16[1792,128]{1,0:T(8,128)(2,1)S(1)}, bf16[1792,128]{1,0:T(8,128)(2,1)S(1)}, u32[]{:S(2)}, u32[]{:S(2)}) %collective-permute-start.2) | collective-permute-done | bytes 458784 | tf_op jit(solution)/shard_map/ppermute | solution.py:188
  41.2 1.5 %collective-permute-start.7 = (f32[3,128,128]{2,1,0:T(8,128)S(1)}, f32[3,128,128]{2,1,0:T(8,128)S(1)}, u32[]{:S(2)}, u32[]{:S(2)}) collective-permute-start(f32[3,128,128]{2,1,0:T(8,128)S(1)} %pad_maximum_fusion), channel_id=1, source_target_pairs={{0,1},{1,0},{2,3},{3,2},{4,5},{5,4},{6,7},{7,6},{8,9},{9,8},{10,11... | collective-permute-start | bytes 589832 | tf_op jit(solution)/shard_map/ppermute | solution.py:188
  42.7 1.5 %collective-permute-start.20 = (bf16[2240,128]{1,0:T(8,128)(2,1)S(1)}, bf16[2240,128]{1,0:T(8,128)(2,1)S(1)}, u32[]{:S(2)}, u32[]{:S(2)}) collective-permute-start(bf16[2240,128]{1,0:T(8,128)(2,1)S(1)} %add_convert_fusion), channel_id=1, source_target_pairs={{0,16},{8,24},{16,0},{24,8},{1,17},{9,25},{17,1},{25,9},{2,18},{10... | collective-permute-start | bytes 1720328 | tf_op jit(solution)/shard_map/ppermute | solution.py:188
  44.2 3.6 %collective-permute-done.7 = f32[3,128,128]{2,1,0:T(8,128)S(1)} collective-permute-done((f32[3,128,128]{2,1,0:T(8,128)S(1)}, f32[3,128,128]{2,1,0:T(8,128)S(1)}, u32[]{:S(2)}, u32[]{:S(2)}) %collective-permute-start.7) | collective-permute-done | bytes 196640 | tf_op jit(solution)/shard_map/ppermute | solution.py:188
  47.8 2.3 %collective-permute-done.6 = bf16[1792,128]{1,0:T(8,128)(2,1)S(1)} collective-permute-done((bf16[1792,128]{1,0:T(8,128)(2,1)S(1)}, bf16[1792,128]{1,0:T(8,128)(2,1)S(1)}, u32[]{:S(2)}, u32[]{:S(2)}) %collective-permute-start.6) | collective-permute-done | bytes 458784 | tf_op jit(solution)/shard_map/ppermute | solution.py:188
  50.1 2.5 %collective-permute-start.9 = (f32[3,128,128]{2,1,0:T(8,128)S(1)}, f32[3,128,128]{2,1,0:T(8,128)S(1)}, u32[]{:S(2)}, u32[]{:S(2)}) collective-permute-start(f32[3,128,128]{2,1,0:T(8,128)S(1)} %add.152), channel_id=1, source_target_pairs={{0,2},{1,3},{2,0},{3,1},{4,6},{5,7},{6,4},{7,5},{8,10},{9,11},{10,... | collective-permute-start | bytes 589832 | tf_op jit(solution)/shard_map/ppermute | solution.py:188
  53.1 4.6 %collective-permute-done.9 = f32[3,128,128]{2,1,0:T(8,128)S(1)} collective-permute-done((f32[3,128,128]{2,1,0:T(8,128)S(1)}, f32[3,128,128]{2,1,0:T(8,128)S(1)}, u32[]{:S(2)}, u32[]{:S(2)}) %collective-permute-start.9) | collective-permute-done | bytes 196640 | tf_op jit(solution)/shard_map/ppermute | solution.py:188
  57.7 1.7 %collective-permute-start.10 = (f32[2,128,128]{2,1,0:T(8,128)S(1)}, f32[2,128,128]{2,1,0:T(8,128)S(1)}, u32[]{:S(2)}, u32[]{:S(2)}) collective-permute-start(f32[2,128,128]{2,1,0:T(8,128)S(1)} %fusion.3), channel_id=1, source_target_pairs={{0,1},{1,0},{2,3},{3,2},{4,5},{5,4},{6,7},{7,6},{8,9},{9,8},{10,11... | collective-permute-start | bytes 393224 | tf_op jit(solution)/shard_map/ppermute | solution.py:188
  59.4 2.6 %collective-permute-start.13 = (f32[3,128,128]{2,1,0:T(8,128)S(1)}, f32[3,128,128]{2,1,0:T(8,128)S(1)}, u32[]{:S(2)}, u32[]{:S(2)}) collective-permute-start(f32[3,128,128]{2,1,0:T(8,128)S(1)} %add.155.gram_ref), channel_id=1, source_target_pairs={{0,4},{1,5},{2,6},{3,7},{4,0},{5,1},{6,2},{7,3},{8,12},{9,13},{10,... | collective-permute-start | bytes 589832 | tf_op jit(solution)/shard_map/ppermute | solution.py:188
  62.0 0.8 collective-permute-done.10
  62.8 1.8 %collective-permute-start.11 = (f32[2,128,128]{2,1,0:T(8,128)S(1)}, f32[2,128,128]{2,1,0:T(8,128)S(1)}, u32[]{:S(2)}, u32[]{:S(2)}) collective-permute-start(f32[2,128,128]{2,1,0:T(8,128)S(1)} %add.156), channel_id=1, source_target_pairs={{0,2},{1,3},{2,0},{3,1},{4,6},{5,7},{6,4},{7,5},{8,10},{9,11},{10,... | collective-permute-start | bytes 393224 | tf_op jit(solution)/shard_map/ppermute | solution.py:188
  64.6 1.6 %collective-permute-start.8 = (bf16[1792,128]{1,0:T(8,128)(2,1)S(1)}, bf16[1792,128]{1,0:T(8,128)(2,1)S(1)}, u32[]{:S(2)}, u32[]{:S(2)}) collective-permute-start(bf16[1792,128]{1,0:T(8,128)(2,1)S(1)} %add_convert_fusion.1), channel_id=1, source_target_pairs={{0,16},{8,24},{16,0},{24,8},{1,17},{9,25},{17,1},{25,9},{2,18},{10... | collective-permute-start | bytes 1376264 | tf_op jit(solution)/shard_map/ppermute | solution.py:188
  66.2 6.0 %collective-permute-done.11 = f32[2,128,128]{2,1,0:T(8,128)S(1)} collective-permute-done((f32[2,128,128]{2,1,0:T(8,128)S(1)}, f32[2,128,128]{2,1,0:T(8,128)S(1)}, u32[]{:S(2)}, u32[]{:S(2)}) %collective-permute-start.11) | collective-permute-done | bytes 131104 | tf_op jit(solution)/shard_map/ppermute | solution.py:188
  72.8 3.8 %shard_map.50.refs_0_ = f32[3,128,128]{2,1,0:T(8,128)S(1)} custom-call(f32[3,128,128]{2,1,0:T(8,128)S(1)} %add.155.gram_ref, f32[3,128,128]{2,1,0:T(8,128)S(1)} %collective-permute-done.13.arrived_ref), custom_call_target="tpu_custom_call" | custom-call | flops 1358954496 | bytes 589824 | tf_op jit(solution)/shard_map/pallas_call | solution.py:68
  76.6 2.4 %collective-permute-done.12.arrived_ref = f32[2,128,128]{2,1,0:T(8,128)S(1)} collective-permute-done((f32[2,128,128]{2,1,0:T(8,128)S(1)}, f32[2,128,128]{2,1,0:T(8,128)S(1)}, u32[]{:S(2)}, u32[]{:S(2)}) %collective-permute-start.12) | collective-permute-done | bytes 131104 | tf_op jit(solution)/shard_map/ppermute | solution.py:188
  79.0 3.4 %shard_map.51.refs_2_ = f32[5,128,128]{2,1,0:T(8,128)S(1)} custom-call(f32[2,128,128]{2,1,0:T(8,128)S(1)} %add.157.gram_ref, f32[2,128,128]{2,1,0:T(8,128)S(1)} %collective-permute-done.12.arrived_ref, f32[3,128,128]{2,1,0:T(8,128)S(1)} %shard_map.50.refs_0_), custom_call_target="tpu_custom_call" | custom-call | flops 905969664 | bytes 393216 | tf_op jit(solution)/shard_map/pallas_call | solution.py:68
  82.5 1.6 %collective-permute-start.15 = (f32[5,128,128]{2,1,0:T(8,128)S(1)}, f32[5,128,128]{2,1,0:T(8,128)S(1)}, u32[]{:S(2)}, u32[]{:S(2)}) collective-permute-start(f32[5,128,128]{2,1,0:T(8,128)S(1)} %shard_map.51.refs_2_), channel_id=1, source_target_pairs={{0,16},{8,24},{16,0},{24,8},{1,17},{9,25},{17,1},{25,9},{2,18},{10... | collective-permute-start | bytes 983048 | tf_op jit(solution)/shard_map/ppermute | solution.py:188
  84.7 2.8 %shard_map.52 = (f32[18,896,128]{2,1,0:T(8,128)}, bf16[18,896,128]{2,1,0:T(8,128)(2,1)}) custom-call(s32[1]{0:T(128)} %bitcast.place_ref, s32[18]{0:T(128)S(1)} %copy-done, bf16[5,448,128]{2,1,0:T(8,128)(2,1)S(1)} %bitcast.21, bf16[5,448,128]{2,1,0:T(8,128)(2,1)S(1)} %bitcast.22, f32[5,128,128]{2,1,0:T(8,128)S(1)} %shard_map.51.refs_2_, ...), custom_call_target="tpu_custom_call" | custom-call | flops 293601280 | bytes 6881280 | tf_op jit(solution)/shard_map/pallas_call | solution.py:160
  87.5 2.5 %shard_map.53 = (f32[18,896,128]{2,1,0:T(8,128)}, bf16[18,896,128]{2,1,0:T(8,128)(2,1)}) custom-call(s32[1]{0:T(128)} %bitcast.place_ref, s32[18]{0:T(128)S(1)} %copy-done, bf16[2,896,128]{2,1,0:T(8,128)(2,1)S(1)} %bitcast.20, bf16[2,896,128]{2,1,0:T(8,128)(2,1)S(1)} %bitcast.27, ...), custom_call_target="tpu_custom_call", output_to_operand_aliasing={{0}: (7, {}), {1}: (8, {})} | custom-call | flops 234881024 | bytes 5505024 | tf_op jit(solution)/shard_map/pallas_call | solution.py:160
  90.0 2.6 %collective-permute-done.15.refs_2_ = f32[5,128,128]{2,1,0:T(8,128)S(1)} collective-permute-done((f32[5,128,128]{2,1,0:T(8,128)S(1)}, f32[5,128,128]{2,1,0:T(8,128)S(1)}, u32[]{:S(2)}, u32[]{:S(2)}) %collective-permute-start.15) | collective-permute-done | bytes 327712 | tf_op jit(solution)/shard_map/ppermute | solution.py:188
  92.6 1.6 %collective-permute-done.19.refs_3_ = f32[5,128,128]{2,1,0:T(8,128)S(1)} collective-permute-done((f32[5,128,128]{2,1,0:T(8,128)S(1)}, f32[5,128,128]{2,1,0:T(8,128)S(1)}, u32[]{:S(2)}, u32[]{:S(2)}) %collective-permute-start.19) | collective-permute-done | bytes 327712 | tf_op jit(solution)/shard_map/ppermute | solution.py:188
  94.2 2.8 %shard_map.54 = (f32[18,896,128]{2,1,0:T(8,128)}, bf16[18,896,128]{2,1,0:T(8,128)(2,1)}) custom-call(s32[1]{0:T(128)} %bitcast.place_ref, s32[18]{0:T(128)S(1)} %copy-done, bf16[5,448,128]{2,1,0:T(8,128)(2,1)S(1)} %bitcast.23, bf16[5,448,128]{2,1,0:T(8,128)(2,1)S(1)} %bitcast.24, ...), custom_call_target="tpu_custom_call", output_to_operand_aliasing={{0}: (7, {}), {1}: (8, {})} | custom-call | flops 293601280 | bytes 6881280 | tf_op jit(solution)/shard_map/pallas_call | solution.py:160
  97.0 2.5 %shard_map.55 = (f32[18,896,128]{2,1,0:T(8,128)}, bf16[18,896,128]{2,1,0:T(8,128)(2,1)}) custom-call(s32[1]{0:T(128)} %bitcast.place_ref, s32[18]{0:T(128)S(1)} %copy-done, bf16[2,896,128]{2,1,0:T(8,128)(2,1)S(1)} %bitcast.25, bf16[2,896,128]{2,1,0:T(8,128)(2,1)S(1)} %bitcast.26, ...), custom_call_target="tpu_custom_call", output_to_operand_aliasing={{0}: (7, {}), {1}: (8, {})} | custom-call | flops 234881024 | bytes 5505024 | tf_op jit(solution)/shard_map/pallas_call | solution.py:160
  (39 shorter events, 3.2 us)
Async XLA Ops:
  2.3 15.8 %collective-permute-start = (bf16[2240,128]{1,0:T(8,128)(2,1)S(1)}, bf16[2240,128]{1,0:T(8,128)(2,1)S(1)}, u32[]{:S(2)}, u32[]{:S(2)}) collective-permute-start(bf16[2240,128]{1,0:T(8,128)(2,1)S(1)} %get-tuple-element.52), channel_id=1, source_target_pairs={{0,24},{8,16},{16,8},{24,0},{1,25},{9,17},{17,9},{25,1},{2,26},{10... | collective-permute-start | bytes 1720328 | tf_op jit(solution)/shard_map/ppermute | solution.py:188
  4.7 16.0 %collective-permute-start.3 = (bf16[2240,128]{1,0:T(8,128)(2,1)S(1)}, bf16[2240,128]{1,0:T(8,128)(2,1)S(1)}, u32[]{:S(2)}, u32[]{:S(2)}) collective-permute-start(bf16[2240,128]{1,0:T(8,128)(2,1)S(1)} %get-tuple-element.50), channel_id=1, source_target_pairs={{0,8},{8,0},{16,24},{24,16},{1,9},{9,1},{17,25},{25,17},{2,10},{10... | collective-permute-start | bytes 1720328 | tf_op jit(solution)/shard_map/ppermute | solution.py:188
  5.4 26.0 %collective-permute-start.4 = (bf16[2240,128]{1,0:T(8,128)(2,1)S(1)}, bf16[2240,128]{1,0:T(8,128)(2,1)S(1)}, u32[]{:S(2)}, u32[]{:S(2)}) collective-permute-start(bf16[2240,128]{1,0:T(8,128)(2,1)S(1)} %get-tuple-element.51), channel_id=1, source_target_pairs={{0,16},{8,24},{16,0},{24,8},{1,17},{9,25},{17,1},{25,9},{2,18},{10... | collective-permute-start | bytes 1720328 | tf_op jit(solution)/shard_map/ppermute | solution.py:188
  18.1 17.0 %collective-permute-start.1 = (bf16[1792,128]{1,0:T(8,128)(2,1)S(1)}, bf16[1792,128]{1,0:T(8,128)(2,1)S(1)}, u32[]{:S(2)}, u32[]{:S(2)}) collective-permute-start(bf16[1792,128]{1,0:T(8,128)(2,1)S(1)} %get-tuple-element.27), channel_id=1, source_target_pairs={{0,8},{8,0},{16,24},{24,16},{1,9},{9,1},{17,25},{25,17},{2,10},{10... | collective-permute-start | bytes 1376264 | tf_op jit(solution)/shard_map/ppermute | solution.py:188
  18.9 22.3 %collective-permute-start.2 = (bf16[1792,128]{1,0:T(8,128)(2,1)S(1)}, bf16[1792,128]{1,0:T(8,128)(2,1)S(1)}, u32[]{:S(2)}, u32[]{:S(2)}) collective-permute-start(bf16[1792,128]{1,0:T(8,128)(2,1)S(1)} %get-tuple-element.28), channel_id=1, source_target_pairs={{0,16},{8,24},{16,0},{24,8},{1,17},{9,25},{17,1},{25,9},{2,18},{10... | collective-permute-start | bytes 1376264 | tf_op jit(solution)/shard_map/ppermute | solution.py:188
  33.0 2.0 %collective-permute-start.5 = (f32[1,128,128]{2,1,0:T(8,128)S(1)}, f32[1,128,128]{2,1,0:T(8,128)S(1)}, u32[]{:S(2)}, u32[]{:S(2)}) collective-permute-start(f32[1,128,128]{2,1,0:T(8,128)S(1)} %convolution_bitcast_fusion), channel_id=1, source_target_pairs={{0,8},{8,0},{16,24},{24,16},{1,9},{9,1},{17,25},{25,17},{2,10},{10... | collective-permute-start | bytes 196616 | tf_op jit(solution)/shard_map/ppermute | solution.py:188
  33.1 16.9 %collective-permute-start.6 = (bf16[1792,128]{1,0:T(8,128)(2,1)S(1)}, bf16[1792,128]{1,0:T(8,128)(2,1)S(1)}, u32[]{:S(2)}, u32[]{:S(2)}) collective-permute-start(bf16[1792,128]{1,0:T(8,128)(2,1)S(1)} %get-tuple-element.33), channel_id=1, source_target_pairs={{0,24},{8,16},{16,8},{24,0},{1,25},{9,17},{17,9},{25,1},{2,26},{10... | collective-permute-start | bytes 1376264 | tf_op jit(solution)/shard_map/ppermute | solution.py:188
  34.7 49.9 %slice-start = ((s8[8257536]{0:T(1024)(128)(4,1)}), s8[4194304]{0:T(1024)(128)(4,1)S(1)}, s32[]{:S(2)}) async-start(s8[8257536]{0:T(1024)(128)(4,1)} %bitcast.17), calls=%async_computation | async-start | bytes 8388608
  41.2 6.5 %collective-permute-start.7 = (f32[3,128,128]{2,1,0:T(8,128)S(1)}, f32[3,128,128]{2,1,0:T(8,128)S(1)}, u32[]{:S(2)}, u32[]{:S(2)}) collective-permute-start(f32[3,128,128]{2,1,0:T(8,128)S(1)} %pad_maximum_fusion), channel_id=1, source_target_pairs={{0,1},{1,0},{2,3},{3,2},{4,5},{5,4},{6,7},{7,6},{8,9},{9,8},{10,11... | collective-permute-start | bytes 589832 | tf_op jit(solution)/shard_map/ppermute | solution.py:188
  42.7 39.7 %collective-permute-start.20 = (bf16[2240,128]{1,0:T(8,128)(2,1)S(1)}, bf16[2240,128]{1,0:T(8,128)(2,1)S(1)}, u32[]{:S(2)}, u32[]{:S(2)}) collective-permute-start(bf16[2240,128]{1,0:T(8,128)(2,1)S(1)} %add_convert_fusion), channel_id=1, source_target_pairs={{0,16},{8,24},{16,0},{24,8},{1,17},{9,25},{17,1},{25,9},{2,18},{10... | collective-permute-start | bytes 1720328 | tf_op jit(solution)/shard_map/ppermute | solution.py:188
  50.1 7.6 %collective-permute-start.9 = (f32[3,128,128]{2,1,0:T(8,128)S(1)}, f32[3,128,128]{2,1,0:T(8,128)S(1)}, u32[]{:S(2)}, u32[]{:S(2)}) collective-permute-start(f32[3,128,128]{2,1,0:T(8,128)S(1)} %add.152), channel_id=1, source_target_pairs={{0,2},{1,3},{2,0},{3,1},{4,6},{5,7},{6,4},{7,5},{8,10},{9,11},{10,... | collective-permute-start | bytes 589832 | tf_op jit(solution)/shard_map/ppermute | solution.py:188
  57.7 5.1 %collective-permute-start.10 = (f32[2,128,128]{2,1,0:T(8,128)S(1)}, f32[2,128,128]{2,1,0:T(8,128)S(1)}, u32[]{:S(2)}, u32[]{:S(2)}) collective-permute-start(f32[2,128,128]{2,1,0:T(8,128)S(1)} %fusion.3), channel_id=1, source_target_pairs={{0,1},{1,0},{2,3},{3,2},{4,5},{5,4},{6,7},{7,6},{8,9},{9,8},{10,11... | collective-permute-start | bytes 393224 | tf_op jit(solution)/shard_map/ppermute | solution.py:188
  59.4 13.3 %collective-permute-start.13 = (f32[3,128,128]{2,1,0:T(8,128)S(1)}, f32[3,128,128]{2,1,0:T(8,128)S(1)}, u32[]{:S(2)}, u32[]{:S(2)}) collective-permute-start(f32[3,128,128]{2,1,0:T(8,128)S(1)} %add.155.gram_ref), channel_id=1, source_target_pairs={{0,4},{1,5},{2,6},{3,7},{4,0},{5,1},{6,2},{7,3},{8,12},{9,13},{10,... | collective-permute-start | bytes 589832 | tf_op jit(solution)/shard_map/ppermute | solution.py:188
  62.8 9.4 %collective-permute-start.11 = (f32[2,128,128]{2,1,0:T(8,128)S(1)}, f32[2,128,128]{2,1,0:T(8,128)S(1)}, u32[]{:S(2)}, u32[]{:S(2)}) collective-permute-start(f32[2,128,128]{2,1,0:T(8,128)S(1)} %add.156), channel_id=1, source_target_pairs={{0,2},{1,3},{2,0},{3,1},{4,6},{5,7},{6,4},{7,5},{8,10},{9,11},{10,... | collective-permute-start | bytes 393224 | tf_op jit(solution)/shard_map/ppermute | solution.py:188
  64.6 19.6 %collective-permute-start.8 = (bf16[1792,128]{1,0:T(8,128)(2,1)S(1)}, bf16[1792,128]{1,0:T(8,128)(2,1)S(1)}, u32[]{:S(2)}, u32[]{:S(2)}) collective-permute-start(bf16[1792,128]{1,0:T(8,128)(2,1)S(1)} %add_convert_fusion.1), channel_id=1, source_target_pairs={{0,16},{8,24},{16,0},{24,8},{1,17},{9,25},{17,1},{25,9},{2,18},{10... | collective-permute-start | bytes 1376264 | tf_op jit(solution)/shard_map/ppermute | solution.py:188
  66.2 18.1 %collective-permute-start.18 = (bf16[2240,128]{1,0:T(8,128)(2,1)S(1)}, bf16[2240,128]{1,0:T(8,128)(2,1)S(1)}, u32[]{:S(2)}, u32[]{:S(2)}) collective-permute-start(bf16[2240,128]{1,0:T(8,128)(2,1)S(1)} %add_convert_fusion), channel_id=1, source_target_pairs={{0,8},{8,0},{16,24},{24,16},{1,9},{9,1},{17,25},{25,17},{2,10},{10... | collective-permute-start | bytes 1720328 | tf_op jit(solution)/shard_map/ppermute | solution.py:188
  72.2 12.4 %slice-start.1 = ((s8[8257536]{0:T(1024)(128)(4,1)}), s8[4063232]{0:T(1024)(128)(4,1)S(1)}, s32[]{:S(2)}) async-start(s8[8257536]{0:T(1024)(128)(4,1)} %bitcast.17), calls=%async_computation.1 | async-start | bytes 8126464
  72.2 12.4 %copy-start = (s32[18]{0:T(128)S(1)}, s32[18]{0:T(128)}, u32[]{:S(2)}) copy-start(s32[18]{0:T(128)} %table_ref.7) | copy-start | bytes 220
  72.3 6.8 %collective-permute-start.12 = (f32[2,128,128]{2,1,0:T(8,128)S(1)}, f32[2,128,128]{2,1,0:T(8,128)S(1)}, u32[]{:S(2)}, u32[]{:S(2)}) collective-permute-start(f32[2,128,128]{2,1,0:T(8,128)S(1)} %add.157.gram_ref), channel_id=1, source_target_pairs={{0,4},{1,5},{2,6},{3,7},{4,0},{5,1},{6,2},{7,3},{8,12},{9,13},{10,... | collective-permute-start | bytes 393224 | tf_op jit(solution)/shard_map/ppermute | solution.py:188
  72.8 14.7 %collective-permute-start.16 = (bf16[1792,128]{1,0:T(8,128)(2,1)S(1)}, bf16[1792,128]{1,0:T(8,128)(2,1)S(1)}, u32[]{:S(2)}, u32[]{:S(2)}) collective-permute-start(bf16[1792,128]{1,0:T(8,128)(2,1)S(1)} %add_convert_fusion.1), channel_id=1, source_target_pairs={{0,8},{8,0},{16,24},{24,16},{1,9},{9,1},{17,25},{25,17},{2,10},{10... | collective-permute-start | bytes 1376264 | tf_op jit(solution)/shard_map/ppermute | solution.py:188
  82.4 2.3 %collective-permute-start.17 = (f32[5,128,128]{2,1,0:T(8,128)S(1)}, f32[5,128,128]{2,1,0:T(8,128)S(1)}, u32[]{:S(2)}, u32[]{:S(2)}) collective-permute-start(f32[5,128,128]{2,1,0:T(8,128)S(1)} %shard_map.51.refs_2_), channel_id=1, source_target_pairs={{0,8},{8,0},{16,24},{24,16},{1,9},{9,1},{17,25},{25,17},{2,10},{10... | collective-permute-start | bytes 983048 | tf_op jit(solution)/shard_map/ppermute | solution.py:188
  82.5 10.1 %collective-permute-start.15 = (f32[5,128,128]{2,1,0:T(8,128)S(1)}, f32[5,128,128]{2,1,0:T(8,128)S(1)}, u32[]{:S(2)}, u32[]{:S(2)}) collective-permute-start(f32[5,128,128]{2,1,0:T(8,128)S(1)} %shard_map.51.refs_2_), channel_id=1, source_target_pairs={{0,16},{8,24},{16,0},{24,8},{1,17},{9,25},{17,1},{25,9},{2,18},{10... | collective-permute-start | bytes 983048 | tf_op jit(solution)/shard_map/ppermute | solution.py:188
  84.1 8.5 %collective-permute-start.21 = (bf16[2240,128]{1,0:T(8,128)(2,1)S(1)}, bf16[2240,128]{1,0:T(8,128)(2,1)S(1)}, u32[]{:S(2)}, u32[]{:S(2)}) collective-permute-start(bf16[2240,128]{1,0:T(8,128)(2,1)S(1)} %collective-permute-done.20), channel_id=1, source_target_pairs={{0,8},{8,0},{16,24},{24,16},{1,9},{9,1},{17,25},{25,17},{2,10},{10... | collective-permute-start | bytes 1720328 | tf_op jit(solution)/shard_map/ppermute | solution.py:188
  84.3 12.7 %collective-permute-start.14 = (bf16[1792,128]{1,0:T(8,128)(2,1)S(1)}, bf16[1792,128]{1,0:T(8,128)(2,1)S(1)}, u32[]{:S(2)}, u32[]{:S(2)}) collective-permute-start(bf16[1792,128]{1,0:T(8,128)(2,1)S(1)} %collective-permute-done.8), channel_id=1, source_target_pairs={{0,8},{8,0},{16,24},{24,16},{1,9},{9,1},{17,25},{25,17},{2,10},{10... | collective-permute-start | bytes 1376264 | tf_op jit(solution)/shard_map/ppermute | solution.py:188
  92.6 1.6 %collective-permute-start.19 = (f32[5,128,128]{2,1,0:T(8,128)S(1)}, f32[5,128,128]{2,1,0:T(8,128)S(1)}, u32[]{:S(2)}, u32[]{:S(2)}) collective-permute-start(f32[5,128,128]{2,1,0:T(8,128)S(1)} %collective-permute-done.15.refs_2_), channel_id=1, source_target_pairs={{0,8},{8,0},{16,24},{24,16},{1,9},{9,1},{17,25},{25,17},{2,10},{10... | collective-permute-start | bytes 983048 | tf_op jit(solution)/shard_map/ppermute | solution.py:188

commit v6 on v5

--- a/solution.py
+++ b/solution.py
@@ -78,14 +78,20 @@
 
 
 def apply_kernel(layout, place_ref, table_ref, *refs):
-    count, first, base, size, offset, own, total, padded = layout
-    sources, qs = refs[:count], refs[count : 2 * count]
-    params_ref = refs[2 * count]
-    new_ref, update_ref, new_buf, update_buf, new_sems, update_sems = refs[-6:]
+    count, kinds, first, bases, size, offset, own, total, padded = layout
+    sources, refs = refs[:count], refs[count:]
+    new_ref, update_ref, new_buf, update_buf, q_buf, new_sems, update_sems = refs[-7:]
+    qs, params_ref = refs[: kinds * count], refs[kinds * count]
     per_block = 2 if size % 2 else 1
     units, unit_rows = sources[0].shape[:2]
     whole = size // 2
-    place = place_ref[0]
+    kept_base, other_base, half = bases
+    place, side = place_ref[0], place_ref[1]
+    for index in range(count):
+        skip = 0
+        for q_ref in qs[index * kinds : (index + 1) * kinds]:
+            q_buf[index, pl.ds(skip, q_ref.shape[0])] = q_ref[...]
+            skip += q_ref.shape[0]
 
     def locate(source, unit):
         holder = (place ^ source) & (CORES - 1)
@@ -94,10 +100,16 @@
         index = ((place ^ source) >> (CORES - 1)) * own + offset + block
         head = table_ref[jnp.minimum(index, total - 1) if padded else index]
         start = pl.multiple_of((within & (per_block - 1)) * unit_rows, unit_rows)
-        slot = unit
-        if per_block > 1:
-            slot = jnp.where(block == whole, whole, block - holder * (whole + 1))
-        return index < total, head, pl.ds(start, unit_rows), base + slot
+        number = block - holder * (size - whole)
+        slot = kept_base + number
+        if half:
+            mine = (number >= side * half) & (number < (side + 1) * half)
+            slot = jnp.where(
+                mine, slot - side * half, other_base + number - (1 - side) * half
+            )
+        if size % 2:
+            slot = jnp.where(block == whole, kept_base - 1, slot)
+        return index < total, head, pl.ds(start, unit_rows), slot
 
     items = [
         (index, unit, index * units + unit, locate(first + index, unit))
@@ -106,7 +118,7 @@
     ]
 
     def compute(index, unit, item, head, span, slot):
-        q = qs[index][slot]
+        q = q_buf[index, slot]
         high = q.astype(jnp.bfloat16)
         low = (q - high.astype(jnp.float32)).astype(jnp.bfloat16)
         rows = sources[index][unit]
@@ -140,7 +152,7 @@
         pl.when(valid)(run) if padded else run()
 
 
-def apply_side(sources, qs, params, previous, place, table, first, base, size, offset, own, padded):
+def apply_side(sources, qs, params, previous, place, table, first, bases, size, offset, own, padded):
     total, rows, width = params.shape
     count = len(sources)
     units, unit_rows = sources[0].shape[:2]
@@ -149,14 +161,14 @@
     hbm = pl.BlockSpec(memory_space=pltpu.HBM)
     smem = pl.BlockSpec(memory_space=pltpu.SMEM)
     operands = [place, table, *sources, *qs, params]
-    in_specs = [smem, smem] + [vmem] * (2 * count + 1)
+    in_specs = [smem, smem] + [vmem] * (count + len(qs) + 1)
     aliases = {}
     for index, array in enumerate(previous):
         aliases[len(operands)] = index
         operands.append(array)
         in_specs.append(hbm)
     work = steps * unit_rows * width
-    layout = (count, first, base, size, offset, own, total, padded)
+    layout = (count, len(qs) // count, first, bases, size, offset, own, total, padded)
     return pl.pallas_call(
         functools.partial(apply_kernel, layout),
         in_specs=in_specs,
@@ -168,6 +180,7 @@
         scratch_shapes=[
             pltpu.VMEM((steps, unit_rows, width), jnp.float32),
             pltpu.VMEM((steps, unit_rows, width), jnp.bfloat16),
+            pltpu.VMEM((count, sum(q.shape[0] for q in qs) // count, V, V), jnp.float32),
             pltpu.SemaphoreType.DMA((steps,)),
             pltpu.SemaphoreType.DMA((steps,)),
         ],
@@ -204,6 +217,7 @@
     place = lax.axis_index("dp").astype(jnp.int32)
     core = place % CORES
     member = place // CORES
+    side = lax.axis_index("shard").astype(jnp.int32) % 2
     if padded:
         filler = jnp.zeros((members * own - count, rows, width), local.dtype)
         local = jnp.concatenate([local, filler], axis=0)
@@ -219,13 +233,26 @@
             terms = [sum(terms[i : i + 2][1:], terms[i]) for i in range(0, len(terms), 2)]
         return terms[0]
 
-    def reduce_gram(gram, distance=1):
+    def reduce_gram(gram, distance):
         while True:
             arrived = swap(gram, "shard", distance)
             distance *= 2
             if distance >= groups:
                 return gram, arrived
             gram = gram + arrived
+
+    def first_stage(middle, whole):
+        count_whole = whole.shape[0]
+        if count_whole == 0 or count_whole % 2:
+            gram = jnp.concatenate([*middle, whole], axis=0)
+            return gram + swap(gram, "shard", 1)
+        half = count_whole // 2
+        keep = lax.dynamic_slice_in_dim(whole, side * half, half)
+        send = lax.dynamic_slice_in_dim(whole, (1 - side) * half, half)
+        if middle:
+            keep = jnp.concatenate([*middle, keep], axis=0)
+            send = jnp.concatenate([*middle, send], axis=0)
+        return keep + swap(send, "shard", 1)
 
     def over_chips(array):
         return [swap(array, "dp", distance * CORES) for distance in range(1, members)]
@@ -253,40 +280,54 @@
 
     first = total_of(terms).astype(jnp.bfloat16)
     whole = size // 2
+    middle = []
+    full = first
     if size % 2:
         half = lax.dynamic_slice_in_dim(first, (1 - core) * whole * rows, rows // 2)
         gram = gram_of(half, rows // 2)
-        gram = gram + swap(gram, "dp", 1)
-        if whole:
-            full = lax.dynamic_slice_in_dim(first, core * (rows // 2), whole * rows)
-            gram = jnp.concatenate([gram_of(full, rows), gram], axis=0)
-    else:
-        gram = gram_of(first, rows)
+        middle = [gram + swap(gram, "dp", 1)]
+        full = lax.dynamic_slice_in_dim(first, core * (rows // 2), whole * rows)
+    grams = gram_of(full, rows) if whole else jnp.zeros((0, V, V), jnp.float32)
     totals, qs = [first], []
     if seconds:
-        *seconds, gram = lax.optimization_barrier((*seconds, gram))
-        gram = gram + swap(gram, "shard", 1)
+        *seconds, grams, middle = lax.optimization_barrier((*seconds, grams, middle))
+        gram = first_stage(middle, grams)
         late, gram = lax.optimization_barrier((late, gram))
         gram = gram + swap(gram, "shard", 2)
         second = total_of([*seconds, late]).astype(jnp.bfloat16)
         totals.append(second)
         gram_second, gram = lax.optimization_barrier((gram_of(second, rows), gram))
         qs.append(newton_schulz(*reduce_gram(gram, 4)))
-        pair = reduce_gram(gram_second)
+        pair = reduce_gram(first_stage([], gram_second), 2)
         qs.append(newton_schulz(*pair, qs[0]))
     else:
-        qs.append(newton_schulz(*reduce_gram(gram)))
-
+        qs.append(newton_schulz(*reduce_gram(first_stage(middle, grams), 2)))
+
+    halves = [0 if (size // 2) % 2 else size // 4 for size in sizes]
+    odd = sizes[0] % 2
+    kept_bases, other_bases = [odd], [qs[-1].shape[0]]
+    for size, half in zip(sizes, halves):
+        kept_bases.append(kept_bases[-1] + (half or size // 2))
+        other_bases.append(other_bases[-1] + half)
+    shared = kept_bases[0] if halves[0] else kept_bases[1]
+
+    def both_sides(q):
+        if not any(halves):
+            return [q]
+        return [q, swap(q[shared:], "shard", 1)]
+
+    scalars = jnp.stack([place, side])
     q = qs[-1]
     arrived_q = over_chips(q)
     arrived_rows = [over_chips(total) for total in totals]
     outputs = []
+    waiting = None
     for distance in range(members):
         if distance:
-            q = arrived_q[distance - 1]
-            if distance == 1:
-                q, *outputs = lax.optimization_barrier((q, *outputs))
-        pair_q = over_cores(q)
+            q = waiting if waiting is not None else arrived_q[distance - 1]
+            waiting = None
+        kinds = [over_cores(array) for array in both_sides(q)]
+        pair_q = [kind[which] for which in range(CORES) for kind in kinds]
         for index, size in enumerate(sizes):
             rows_here = totals[index]
             if distance:
@@ -302,15 +343,17 @@
                 pair_q,
                 params,
                 outputs,
-                place.reshape(1),
+                scalars,
                 table,
                 CORES * distance,
-                qs[index - 1].shape[0] if index else 0,
+                (kept_bases[index], other_bases[index], halves[index]),
                 size,
                 sum(sizes[:index]),
                 own,
                 padded,
             )
+            if distance == 0 and index == 0:
+                waiting, *outputs = lax.optimization_barrier((arrived_q[0], *outputs))
     new_params, update = outputs
     return (new_params, update)
 

time: 99.8 us -> 107 us (1.072)
  waiting for transfers between devices: 51.8 us -> 56.2 us
  starting transfers between devices: 23.3 us -> 25.2 us
    ppermute x22 -> x26, waiting for transfers between devices: 51.8 us -> 56.2 us  [swap(): return lax.ppermute(array, axis, [(i, i ^ distance) for i in range(size)])]
    ppermute x22 -> x26, starting transfers between devices: 23.3 us -> 25.2 us  [swap(): return lax.ppermute(array, axis, [(i, i ^ distance) for i in range(size)])]
  transfers between devices with their start and end apart: 22 -> 26, of which waited for: 11 -> 11; matrix products, arithmetic and copies ran while one was open for 4% -> 3% of each run, Pallas kernels for 15% -> 14%
where the time goes in v6:
time: 107 us; the launch traced here: 106 us
  waiting for transfers between devices  56.2 us (53%)
  starting transfers between devices  25.2 us (24%)
  Pallas kernels  17.5 us (16%)
  local copies, waits for them, and re-layouts  3.17 us (3%)
  other arithmetic  1.9 us (2%)
    ppermute x26, waiting for transfers between devices, swap(): return lax.ppermute(array, axis, [(i, i ^ distance) for i in range(size)])  56.2 us
    ppermute x26, starting transfers between devices, swap(): return lax.ppermute(array, axis, [(i, i ^ distance) for i in range(size)])  25.2 us
    pallas_call x4, Pallas kernels, apply_side(): pl.pallas_call(functools.partial(apply_kernel, layout), in_specs=in_specs...  10.8 us
    pallas_call x2, Pallas kernels, newton_schulz(): pl.pallas_call(newton_kernel, out_shape=jax.ShapeDtypeStruct((slots, V, V...  6.67 us
    dynamic_slice x2, local copies, waits for them, and re-layouts, rows_of(): lax.dynamic_slice_in_dim(flat, (chip * own + offset) * rows + which * len...  3.08 us
  transfers between devices with their start and end apart: 26, of which 11 were waited for; matrix products, arithmetic and copies ran while one was open for 3% of the time, Pallas kernels for 14%

profile of v6, /device:TPU:0, one launch (start us, length us, event | category | flops | bytes accessed | tf_op | source)
XLA Modules:
  0.0 105.9 jit_solution(1919029515040718610)
XLA Ops:
  0.7 1.5 %constant_dynamic-slice_fusion.5 = (bf16[2240,128]{1,0:T(8,128)(2,1)S(1)}, bf16[2240,128]{1,0:T(8,128)(2,1)S(1)}, bf16[2240,128]{1,0:T(8,128)(2,1)S(1)}) fusion(bf16[16128,128]{1,0:T(8,128)(2,1)} %bitcast.30, s32[]{:T(128)S(6)} %select_n.103, s32[]{:T(128)S(6)} %select_n.104, s32[]{:T(128)S(6)} %select_n.91), kind=kLoop, calls=%fused_computation.14 | loop fusion | bytes 3440652 | tf_op jit(solution)/shard_map/dynamic_slice | solution.py:228
  2.3 2.5 %collective-permute-start = (bf16[2240,128]{1,0:T(8,128)(2,1)S(1)}, bf16[2240,128]{1,0:T(8,128)(2,1)S(1)}, u32[]{:S(2)}, u32[]{:S(2)}) collective-permute-start(bf16[2240,128]{1,0:T(8,128)(2,1)S(1)} %get-tuple-element.54), channel_id=1, source_target_pairs={{0,24},{8,16},{16,8},{24,0},{1,25},{9,17},{17,9},{25,1},{2,26},{10... | collective-permute-start | bytes 1720328 | tf_op jit(solution)/shard_map/ppermute | solution.py:201
  4.7 0.7 collective-permute-start.3
  5.5 1.6 %constant_dynamic-slice_fusion.6 = (bf16[1792,128]{1,0:T(8,128)(2,1)S(1)}, bf16[1792,128]{1,0:T(8,128)(2,1)S(1)}, bf16[1792,128]{1,0:T(8,128)(2,1)S(1)}, bf16[1792,128]{1,0:T(8,128)(2,1)S(1)}) fusion(bf16[16128,128]{1,0:T(8,128)(2,1)} %bitcast.31, s32[]{:T(128)S(6)} %select_n.101, s32[]{:T(128)S(6)} %select_n.100, s32[]{:T(128)S(6)} %select_n.97, ...), kind=kLoop, calls=%fused_computation.15 | loop fusion | bytes 3670032 | tf_op jit(solution)/shard_map/dynamic_slice | solution.py:228
  7.0 11.1 %collective-permute-done = bf16[2240,128]{1,0:T(8,128)(2,1)S(1)} collective-permute-done((bf16[2240,128]{1,0:T(8,128)(2,1)S(1)}, bf16[2240,128]{1,0:T(8,128)(2,1)S(1)}, u32[]{:S(2)}, u32[]{:S(2)}) %collective-permute-start) | collective-permute-done | bytes 573472 | tf_op jit(solution)/shard_map/ppermute | solution.py:201
  18.1 12.5 %collective-permute-done.4 = bf16[2240,128]{1,0:T(8,128)(2,1)S(1)} collective-permute-done((bf16[2240,128]{1,0:T(8,128)(2,1)S(1)}, bf16[2240,128]{1,0:T(8,128)(2,1)S(1)}, u32[]{:S(2)}, u32[]{:S(2)}) %collective-permute-start.4) | collective-permute-done | bytes 573472 | tf_op jit(solution)/shard_map/ppermute | solution.py:201
  30.6 1.5 %add_convert_fusion = bf16[2240,128]{1,0:T(8,128)(2,1)S(1)} fusion(bf16[2240,128]{1,0:T(8,128)(2,1)S(1)} %collective-permute-done, bf16[2240,128]{1,0:T(8,128)(2,1)S(1)} %collective-permute-done.4, bf16[2240,128]{1,0:T(8,128)(2,1)S(1)} %collective-permute-done.3, bf16[16128,128]{1,0:T(8,128)(2,1)} %bitcast.32, s32[]{:T(128)S(6)} %select_n.102), kind=kLoop, calls=%fused_computation | loop fusion | flops 2293760 | bytes 2867204 | tf_op jit(solution)/shard_map/convert_element_type | solution.py:281
  32.9 2.3 %collective-permute-start.2 = (bf16[1792,128]{1,0:T(8,128)(2,1)S(1)}, bf16[1792,128]{1,0:T(8,128)(2,1)S(1)}, u32[]{:S(2)}, u32[]{:S(2)}) collective-permute-start(bf16[1792,128]{1,0:T(8,128)(2,1)S(1)} %get-tuple-element.29), channel_id=1, source_target_pairs={{0,16},{8,24},{16,0},{24,8},{1,17},{9,25},{17,1},{25,9},{2,18},{10... | collective-permute-start | bytes 1376264 | tf_op jit(solution)/shard_map/ppermute | solution.py:201
  35.7 10.8 %collective-permute-done.2 = bf16[1792,128]{1,0:T(8,128)(2,1)S(1)} collective-permute-done((bf16[1792,128]{1,0:T(8,128)(2,1)S(1)}, bf16[1792,128]{1,0:T(8,128)(2,1)S(1)}, u32[]{:S(2)}, u32[]{:S(2)}) %collective-permute-start.2) | collective-permute-done | bytes 458784 | tf_op jit(solution)/shard_map/ppermute | solution.py:201
  46.5 2.1 %collective-permute-start.7 = (f32[2,128,128]{2,1,0:T(8,128)S(1)}, f32[2,128,128]{2,1,0:T(8,128)S(1)}, u32[]{:S(2)}, u32[]{:S(2)}) collective-permute-start(f32[2,128,128]{2,1,0:T(8,128)S(1)} %pad_maximum_fusion), channel_id=1, source_target_pairs={{0,1},{1,0},{2,3},{3,2},{4,5},{5,4},{6,7},{7,6},{8,9},{9,8},{10,11... | collective-permute-start | bytes 393224 | tf_op jit(solution)/shard_map/ppermute | solution.py:201
  48.6 1.5 %collective-permute-start.23 = (bf16[2240,128]{1,0:T(8,128)(2,1)S(1)}, bf16[2240,128]{1,0:T(8,128)(2,1)S(1)}, u32[]{:S(2)}, u32[]{:S(2)}) collective-permute-start(bf16[2240,128]{1,0:T(8,128)(2,1)S(1)} %add_convert_fusion), channel_id=1, source_target_pairs={{0,16},{8,24},{16,0},{24,8},{1,17},{9,25},{17,1},{25,9},{2,18},{10... | collective-permute-start | bytes 1720328 | tf_op jit(solution)/shard_map/ppermute | solution.py:201
  50.1 1.4 %collective-permute-done.7 = f32[2,128,128]{2,1,0:T(8,128)S(1)} collective-permute-done((f32[2,128,128]{2,1,0:T(8,128)S(1)}, f32[2,128,128]{2,1,0:T(8,128)S(1)}, u32[]{:S(2)}, u32[]{:S(2)}) %collective-permute-start.7) | collective-permute-done | bytes 131104 | tf_op jit(solution)/shard_map/ppermute | solution.py:201
  51.6 4.3 %collective-permute-done.6 = bf16[1792,128]{1,0:T(8,128)(2,1)S(1)} collective-permute-done((bf16[1792,128]{1,0:T(8,128)(2,1)S(1)}, bf16[1792,128]{1,0:T(8,128)(2,1)S(1)}, u32[]{:S(2)}, u32[]{:S(2)}) %collective-permute-start.6) | collective-permute-done | bytes 458784 | tf_op jit(solution)/shard_map/ppermute | solution.py:201
  55.9 1.6 %collective-permute-start.9 = (f32[2,128,128]{2,1,0:T(8,128)S(1)}, f32[2,128,128]{2,1,0:T(8,128)S(1)}, u32[]{:S(2)}, u32[]{:S(2)}) collective-permute-start(f32[2,128,128]{2,1,0:T(8,128)S(1)} %fusion), channel_id=1, source_target_pairs={{0,2},{1,3},{2,0},{3,1},{4,6},{5,7},{6,4},{7,5},{8,10},{9,11},{10,... | collective-permute-start | bytes 393224 | tf_op jit(solution)/shard_map/ppermute | solution.py:201
  58.1 3.9 %collective-permute-done.9 = f32[2,128,128]{2,1,0:T(8,128)S(1)} collective-permute-done((f32[2,128,128]{2,1,0:T(8,128)S(1)}, f32[2,128,128]{2,1,0:T(8,128)S(1)}, u32[]{:S(2)}, u32[]{:S(2)}) %collective-permute-start.9) | collective-permute-done | bytes 131104 | tf_op jit(solution)/shard_map/ppermute | solution.py:201
  62.0 1.7 %collective-permute-start.10 = (f32[1,128,128]{2,1,0:T(8,128)S(1)}, f32[1,128,128]{2,1,0:T(8,128)S(1)}, u32[]{:S(2)}, u32[]{:S(2)}) collective-permute-start(f32[1,128,128]{2,1,0:T(8,128)S(1)} %constant_dynamic-slice_fusion), channel_id=1, source_target_pairs={{0,1},{1,0},{2,3},{3,2},{4,5},{5,4},{6,7},{7,6},{8,9},{9,8},{10,11... | collective-permute-start | bytes 196616 | tf_op jit(solution)/shard_map/ppermute | solution.py:201
  63.7 0.8 collective-permute-start.8
  64.5 2.6 %collective-permute-start.13 = (f32[2,128,128]{2,1,0:T(8,128)S(1)}, f32[2,128,128]{2,1,0:T(8,128)S(1)}, u32[]{:S(2)}, u32[]{:S(2)}) collective-permute-start(f32[2,128,128]{2,1,0:T(8,128)S(1)} %add.170.gram_ref), channel_id=1, source_target_pairs={{0,4},{1,5},{2,6},{3,7},{4,0},{5,1},{6,2},{7,3},{8,12},{9,13},{10,... | collective-permute-start | bytes 393224 | tf_op jit(solution)/shard_map/ppermute | solution.py:201
  67.1 1.6 %collective-permute-start.11 = (f32[1,128,128]{2,1,0:T(8,128)S(1)}, f32[1,128,128]{2,1,0:T(8,128)S(1)}, u32[]{:S(2)}, u32[]{:S(2)}) collective-permute-start(f32[1,128,128]{2,1,0:T(8,128)S(1)} %dynamic-slice_add_fusion), channel_id=1, source_target_pairs={{0,2},{1,3},{2,0},{3,1},{4,6},{5,7},{6,4},{7,5},{8,10},{9,11},{10,... | collective-permute-start | bytes 196616 | tf_op jit(solution)/shard_map/ppermute | solution.py:201
  68.7 3.3 %collective-permute-done.11 = f32[1,128,128]{2,1,0:T(8,128)S(1)} collective-permute-done((f32[1,128,128]{2,1,0:T(8,128)S(1)}, f32[1,128,128]{2,1,0:T(8,128)S(1)}, u32[]{:S(2)}, u32[]{:S(2)}) %collective-permute-start.11) | collective-permute-done | bytes 65568 | tf_op jit(solution)/shard_map/ppermute | solution.py:201
  72.0 1.8 %collective-permute-start.12 = (f32[1,128,128]{2,1,0:T(8,128)S(1)}, f32[1,128,128]{2,1,0:T(8,128)S(1)}, u32[]{:S(2)}, u32[]{:S(2)}) collective-permute-start(f32[1,128,128]{2,1,0:T(8,128)S(1)} %add.172.gram_ref), channel_id=1, source_target_pairs={{0,4},{1,5},{2,6},{3,7},{4,0},{5,1},{6,2},{7,3},{8,12},{9,13},{10,... | collective-permute-start | bytes 196616 | tf_op jit(solution)/shard_map/ppermute | solution.py:201
  73.8 3.4 %shard_map.50.refs_0_ = f32[2,128,128]{2,1,0:T(8,128)S(1)} custom-call(f32[2,128,128]{2,1,0:T(8,128)S(1)} %add.170.gram_ref, f32[2,128,128]{2,1,0:T(8,128)S(1)} %collective-permute-done.13.arrived_ref), custom_call_target="tpu_custom_call" | custom-call | flops 905969664 | bytes 393216 | tf_op jit(solution)/shard_map/pallas_call | solution.py:68
  77.3 3.3 %shard_map.51.refs_2_ = f32[3,128,128]{2,1,0:T(8,128)S(1)} custom-call(f32[1,128,128]{2,1,0:T(8,128)S(1)} %add.172.gram_ref, f32[1,128,128]{2,1,0:T(8,128)S(1)} %collective-permute-done.12.arrived_ref, f32[2,128,128]{2,1,0:T(8,128)S(1)} %shard_map.50.refs_0_), custom_call_target="tpu_custom_call" | custom-call | flops 452984832 | bytes 196608 | tf_op jit(solution)/shard_map/pallas_call | solution.py:68
  81.2 2.4 %collective-permute-start.17 = (f32[2,128,128]{2,1,0:T(8,128)S(1)}, f32[2,128,128]{2,1,0:T(8,128)S(1)}, u32[]{:S(2)}, u32[]{:S(2)}) collective-permute-start(f32[2,128,128]{2,1,0:T(8,128)S(1)} %slice.8), channel_id=1, source_target_pairs={{0,1},{1,0},{2,3},{3,2},{4,5},{5,4},{6,7},{7,6},{8,9},{9,8},{10,11... | collective-permute-start | bytes 393224 | tf_op jit(solution)/shard_map/ppermute | solution.py:201
  83.6 3.7 %collective-permute-done.17.refs_3_ = f32[2,128,128]{2,1,0:T(8,128)S(1)} collective-permute-done((f32[2,128,128]{2,1,0:T(8,128)S(1)}, f32[2,128,128]{2,1,0:T(8,128)S(1)}, u32[]{:S(2)}, u32[]{:S(2)}) %collective-permute-start.17) | collective-permute-done | bytes 131104 | tf_op jit(solution)/shard_map/ppermute | solution.py:201
  87.9 1.4 %collective-permute-done.19.refs_5_ = f32[2,128,128]{2,1,0:T(8,128)S(1)} collective-permute-done((f32[2,128,128]{2,1,0:T(8,128)S(1)}, f32[2,128,128]{2,1,0:T(8,128)S(1)}, u32[]{:S(2)}, u32[]{:S(2)}) %collective-permute-start.19) | collective-permute-done | bytes 131104 | tf_op jit(solution)/shard_map/ppermute | solution.py:201
  89.3 2.8 %shard_map.52 = (f32[18,896,128]{2,1,0:T(8,128)}, bf16[18,896,128]{2,1,0:T(8,128)(2,1)}) custom-call(s32[2]{0:T(128)S(1)} %pad_add_fusion.place_ref, s32[18]{0:T(128)S(1)} %copy-done, bf16[5,448,128]{2,1,0:T(8,128)(2,1)S(1)} %bitcast.22, bf16[5,448,128]{2,1,0:T(8,128)(2,1)S(1)} %bitcast.23, f32[3,128,128]{2,1,0:T(8,128)S(1)} %shard_map.51.refs_2_, ...), custom_call_target="tpu_custom_call" | custom-call | flops 293601280 | bytes 6881280 | tf_op jit(solution)/shard_map/pallas_call | solution.py:172
  92.2 1.8 %collective-permute-start.20 = (f32[2,128,128]{2,1,0:T(8,128)S(1)}, f32[2,128,128]{2,1,0:T(8,128)S(1)}, u32[]{:S(2)}, u32[]{:S(2)}) collective-permute-start(f32[2,128,128]{2,1,0:T(8,128)S(1)} %slice.7), channel_id=1, source_target_pairs={{0,1},{1,0},{2,3},{3,2},{4,5},{5,4},{6,7},{7,6},{8,9},{9,8},{10,11... | collective-permute-start | bytes 393224 | tf_op jit(solution)/shard_map/ppermute | solution.py:201
  94.0 3.8 %collective-permute-done.20.refs_3_ = f32[2,128,128]{2,1,0:T(8,128)S(1)} collective-permute-done((f32[2,128,128]{2,1,0:T(8,128)S(1)}, f32[2,128,128]{2,1,0:T(8,128)S(1)}, u32[]{:S(2)}, u32[]{:S(2)}) %collective-permute-start.20) | collective-permute-done | bytes 131104 | tf_op jit(solution)/shard_map/ppermute | solution.py:201
  97.8 2.6 %shard_map.53 = (f32[18,896,128]{2,1,0:T(8,128)}, bf16[18,896,128]{2,1,0:T(8,128)(2,1)}) custom-call(s32[2]{0:T(128)S(1)} %pad_add_fusion.place_ref, s32[18]{0:T(128)S(1)} %copy-done, bf16[2,896,128]{2,1,0:T(8,128)(2,1)S(1)} %bitcast.21, bf16[2,896,128]{2,1,0:T(8,128)(2,1)S(1)} %bitcast.28, ...), custom_call_target="tpu_custom_call", output_to_operand_aliasing={{0}: (9, {}), {1}: (10, {})} | custom-call | flops 234881024 | bytes 5505024 | tf_op jit(solution)/shard_map/pallas_call | solution.py:172
  100.4 2.8 %shard_map.54 = (f32[18,896,128]{2,1,0:T(8,128)}, bf16[18,896,128]{2,1,0:T(8,128)(2,1)}) custom-call(s32[2]{0:T(128)S(1)} %pad_add_fusion.place_ref, s32[18]{0:T(128)S(1)} %copy-done, bf16[5,448,128]{2,1,0:T(8,128)(2,1)S(1)} %bitcast.24, bf16[5,448,128]{2,1,0:T(8,128)(2,1)S(1)} %bitcast.25, ...), custom_call_target="tpu_custom_call", output_to_operand_aliasing={{0}: (9, {}), {1}: (10, {})} | custom-call | flops 293601280 | bytes 6881280 | tf_op jit(solution)/shard_map/pallas_call | solution.py:172
  103.3 2.6 %shard_map.55 = (f32[18,896,128]{2,1,0:T(8,128)}, bf16[18,896,128]{2,1,0:T(8,128)(2,1)}) custom-call(s32[2]{0:T(128)S(1)} %pad_add_fusion.place_ref, s32[18]{0:T(128)S(1)} %copy-done, bf16[2,896,128]{2,1,0:T(8,128)(2,1)S(1)} %bitcast.26, bf16[2,896,128]{2,1,0:T(8,128)(2,1)S(1)} %bitcast.27, ...), custom_call_target="tpu_custom_call", output_to_operand_aliasing={{0}: (9, {}), {1}: (10, {})} | custom-call | flops 234881024 | bytes 5505024 | tf_op jit(solution)/shard_map/pallas_call | solution.py:172
  (52 shorter events, 3.3 us)
Async XLA Ops:
  2.3 15.8 %collective-permute-start = (bf16[2240,128]{1,0:T(8,128)(2,1)S(1)}, bf16[2240,128]{1,0:T(8,128)(2,1)S(1)}, u32[]{:S(2)}, u32[]{:S(2)}) collective-permute-start(bf16[2240,128]{1,0:T(8,128)(2,1)S(1)} %get-tuple-element.54), channel_id=1, source_target_pairs={{0,24},{8,16},{16,8},{24,0},{1,25},{9,17},{17,9},{25,1},{2,26},{10... | collective-permute-start | bytes 1720328 | tf_op jit(solution)/shard_map/ppermute | solution.py:201
  4.7 13.4 %collective-permute-start.3 = (bf16[2240,128]{1,0:T(8,128)(2,1)S(1)}, bf16[2240,128]{1,0:T(8,128)(2,1)S(1)}, u32[]{:S(2)}, u32[]{:S(2)}) collective-permute-start(bf16[2240,128]{1,0:T(8,128)(2,1)S(1)} %get-tuple-element.52), channel_id=1, source_target_pairs={{0,8},{8,0},{16,24},{24,16},{1,9},{9,1},{17,25},{25,17},{2,10},{10... | collective-permute-start | bytes 1720328 | tf_op jit(solution)/shard_map/ppermute | solution.py:201
  5.4 25.1 %collective-permute-start.4 = (bf16[2240,128]{1,0:T(8,128)(2,1)S(1)}, bf16[2240,128]{1,0:T(8,128)(2,1)S(1)}, u32[]{:S(2)}, u32[]{:S(2)}) collective-permute-start(bf16[2240,128]{1,0:T(8,128)(2,1)S(1)} %get-tuple-element.53), channel_id=1, source_target_pairs={{0,16},{8,24},{16,0},{24,8},{1,17},{9,25},{17,1},{25,9},{2,18},{10... | collective-permute-start | bytes 1720328 | tf_op jit(solution)/shard_map/ppermute | solution.py:201
  30.6 58.7 %slice-start = ((s8[8257536]{0:T(1024)(128)(4,1)}), s8[4194304]{0:T(1024)(128)(4,1)S(1)}, s32[]{:S(2)}) async-start(s8[8257536]{0:T(1024)(128)(4,1)} %bitcast.18), calls=%async_computation | async-start | bytes 8388608
  32.3 3.3 %collective-permute-start.5 = (f32[1,128,128]{2,1,0:T(8,128)S(1)}, f32[1,128,128]{2,1,0:T(8,128)S(1)}, u32[]{:S(2)}, u32[]{:S(2)}) collective-permute-start(f32[1,128,128]{2,1,0:T(8,128)S(1)} %convolution_bitcast_fusion), channel_id=1, source_target_pairs={{0,8},{8,0},{16,24},{24,16},{1,9},{9,1},{17,25},{25,17},{2,10},{10... | collective-permute-start | bytes 196616 | tf_op jit(solution)/shard_map/ppermute | solution.py:201
  32.4 3.3 %collective-permute-start.1 = (bf16[1792,128]{1,0:T(8,128)(2,1)S(1)}, bf16[1792,128]{1,0:T(8,128)(2,1)S(1)}, u32[]{:S(2)}, u32[]{:S(2)}) collective-permute-start(bf16[1792,128]{1,0:T(8,128)(2,1)S(1)} %get-tuple-element.28), channel_id=1, source_target_pairs={{0,8},{8,0},{16,24},{24,16},{1,9},{9,1},{17,25},{25,17},{2,10},{10... | collective-permute-start | bytes 1376264 | tf_op jit(solution)/shard_map/ppermute | solution.py:201
  32.9 13.6 %collective-permute-start.2 = (bf16[1792,128]{1,0:T(8,128)(2,1)S(1)}, bf16[1792,128]{1,0:T(8,128)(2,1)S(1)}, u32[]{:S(2)}, u32[]{:S(2)}) collective-permute-start(bf16[1792,128]{1,0:T(8,128)(2,1)S(1)} %get-tuple-element.29), channel_id=1, source_target_pairs={{0,16},{8,24},{16,0},{24,8},{1,17},{9,25},{17,1},{25,9},{2,18},{10... | collective-permute-start | bytes 1376264 | tf_op jit(solution)/shard_map/ppermute | solution.py:201
  35.6 20.3 %collective-permute-start.6 = (bf16[1792,128]{1,0:T(8,128)(2,1)S(1)}, bf16[1792,128]{1,0:T(8,128)(2,1)S(1)}, u32[]{:S(2)}, u32[]{:S(2)}) collective-permute-start(bf16[1792,128]{1,0:T(8,128)(2,1)S(1)} %get-tuple-element.34), channel_id=1, source_target_pairs={{0,24},{8,16},{16,8},{24,0},{1,25},{9,17},{17,9},{25,1},{2,26},{10... | collective-permute-start | bytes 1376264 | tf_op jit(solution)/shard_map/ppermute | solution.py:201
  46.5 5.1 %collective-permute-start.7 = (f32[2,128,128]{2,1,0:T(8,128)S(1)}, f32[2,128,128]{2,1,0:T(8,128)S(1)}, u32[]{:S(2)}, u32[]{:S(2)}) collective-permute-start(f32[2,128,128]{2,1,0:T(8,128)S(1)} %pad_maximum_fusion), channel_id=1, source_target_pairs={{0,1},{1,0},{2,3},{3,2},{4,5},{5,4},{6,7},{7,6},{8,9},{9,8},{10,11... | collective-permute-start | bytes 393224 | tf_op jit(solution)/shard_map/ppermute | solution.py:201
  48.6 32.0 %collective-permute-start.23 = (bf16[2240,128]{1,0:T(8,128)(2,1)S(1)}, bf16[2240,128]{1,0:T(8,128)(2,1)S(1)}, u32[]{:S(2)}, u32[]{:S(2)}) collective-permute-start(bf16[2240,128]{1,0:T(8,128)(2,1)S(1)} %add_convert_fusion), channel_id=1, source_target_pairs={{0,16},{8,24},{16,0},{24,8},{1,17},{9,25},{17,1},{25,9},{2,18},{10... | collective-permute-start | bytes 1720328 | tf_op jit(solution)/shard_map/ppermute | solution.py:201
  51.6 37.7 %slice-start.1 = ((s8[8257536]{0:T(1024)(128)(4,1)}), s8[4063232]{0:T(1024)(128)(4,1)S(1)}, s32[]{:S(2)}) async-start(s8[8257536]{0:T(1024)(128)(4,1)} %bitcast.18), calls=%async_computation.1 | async-start | bytes 8126464
  55.9 6.0 %collective-permute-start.9 = (f32[2,128,128]{2,1,0:T(8,128)S(1)}, f32[2,128,128]{2,1,0:T(8,128)S(1)}, u32[]{:S(2)}, u32[]{:S(2)}) collective-permute-start(f32[2,128,128]{2,1,0:T(8,128)S(1)} %fusion), channel_id=1, source_target_pairs={{0,2},{1,3},{2,0},{3,1},{4,6},{5,7},{6,4},{7,5},{8,10},{9,11},{10,... | collective-permute-start | bytes 393224 | tf_op jit(solution)/shard_map/ppermute | solution.py:201
  57.7 31.6 %copy-start = (s32[18]{0:T(128)S(1)}, s32[18]{0:T(128)}, u32[]{:S(2)}) copy-start(s32[18]{0:T(128)} %table_ref.7) | copy-start | bytes 220
  62.0 5.1 %collective-permute-start.10 = (f32[1,128,128]{2,1,0:T(8,128)S(1)}, f32[1,128,128]{2,1,0:T(8,128)S(1)}, u32[]{:S(2)}, u32[]{:S(2)}) collective-permute-start(f32[1,128,128]{2,1,0:T(8,128)S(1)} %constant_dynamic-slice_fusion), channel_id=1, source_target_pairs={{0,1},{1,0},{2,3},{3,2},{4,5},{5,4},{6,7},{7,6},{8,9},{9,8},{10,11... | collective-permute-start | bytes 196616 | tf_op jit(solution)/shard_map/ppermute | solution.py:201
  63.7 19.9 %collective-permute-start.16 = (bf16[2240,128]{1,0:T(8,128)(2,1)S(1)}, bf16[2240,128]{1,0:T(8,128)(2,1)S(1)}, u32[]{:S(2)}, u32[]{:S(2)}) collective-permute-start(bf16[2240,128]{1,0:T(8,128)(2,1)S(1)} %add_convert_fusion), channel_id=1, source_target_pairs={{0,8},{8,0},{16,24},{24,16},{1,9},{9,1},{17,25},{25,17},{2,10},{10... | collective-permute-start | bytes 1720328 | tf_op jit(solution)/shard_map/ppermute | solution.py:201
  63.7 19.9 %collective-permute-start.8 = (bf16[1792,128]{1,0:T(8,128)(2,1)S(1)}, bf16[1792,128]{1,0:T(8,128)(2,1)S(1)}, u32[]{:S(2)}, u32[]{:S(2)}) collective-permute-start(bf16[1792,128]{1,0:T(8,128)(2,1)S(1)} %add_convert_fusion.1), channel_id=1, source_target_pairs={{0,16},{8,24},{16,0},{24,8},{1,17},{9,25},{17,1},{25,9},{2,18},{10... | collective-permute-start | bytes 1376264 | tf_op jit(solution)/shard_map/ppermute | solution.py:201
  64.5 9.3 %collective-permute-start.13 = (f32[2,128,128]{2,1,0:T(8,128)S(1)}, f32[2,128,128]{2,1,0:T(8,128)S(1)}, u32[]{:S(2)}, u32[]{:S(2)}) collective-permute-start(f32[2,128,128]{2,1,0:T(8,128)S(1)} %add.170.gram_ref), channel_id=1, source_target_pairs={{0,4},{1,5},{2,6},{3,7},{4,0},{5,1},{6,2},{7,3},{8,12},{9,13},{10,... | collective-permute-start | bytes 393224 | tf_op jit(solution)/shard_map/ppermute | solution.py:201
  67.1 4.9 %collective-permute-start.11 = (f32[1,128,128]{2,1,0:T(8,128)S(1)}, f32[1,128,128]{2,1,0:T(8,128)S(1)}, u32[]{:S(2)}, u32[]{:S(2)}) collective-permute-start(f32[1,128,128]{2,1,0:T(8,128)S(1)} %dynamic-slice_add_fusion), channel_id=1, source_target_pairs={{0,2},{1,3},{2,0},{3,1},{4,6},{5,7},{6,4},{7,5},{8,10},{9,11},{10,... | collective-permute-start | bytes 196616 | tf_op jit(solution)/shard_map/ppermute | solution.py:201
  72.0 5.3 %collective-permute-start.12 = (f32[1,128,128]{2,1,0:T(8,128)S(1)}, f32[1,128,128]{2,1,0:T(8,128)S(1)}, u32[]{:S(2)}, u32[]{:S(2)}) collective-permute-start(f32[1,128,128]{2,1,0:T(8,128)S(1)} %add.172.gram_ref), channel_id=1, source_target_pairs={{0,4},{1,5},{2,6},{3,7},{4,0},{5,1},{6,2},{7,3},{8,12},{9,13},{10,... | collective-permute-start | bytes 196616 | tf_op jit(solution)/shard_map/ppermute | solution.py:201
  80.6 6.7 %collective-permute-start.18 = (f32[3,128,128]{2,1,0:T(8,128)S(1)}, f32[3,128,128]{2,1,0:T(8,128)S(1)}, u32[]{:S(2)}, u32[]{:S(2)}) collective-permute-start(f32[3,128,128]{2,1,0:T(8,128)S(1)} %shard_map.51.refs_2_), channel_id=1, source_target_pairs={{0,8},{8,0},{16,24},{24,16},{1,9},{9,1},{17,25},{25,17},{2,10},{10... | collective-permute-start | bytes 589832 | tf_op jit(solution)/shard_map/ppermute | solution.py:201
  80.7 19.7 %collective-permute-start.24 = (bf16[2240,128]{1,0:T(8,128)(2,1)S(1)}, bf16[2240,128]{1,0:T(8,128)(2,1)S(1)}, u32[]{:S(2)}, u32[]{:S(2)}) collective-permute-start(bf16[2240,128]{1,0:T(8,128)(2,1)S(1)} %collective-permute-done.23), channel_id=1, source_target_pairs={{0,8},{8,0},{16,24},{24,16},{1,9},{9,1},{17,25},{25,17},{2,10},{10... | collective-permute-start | bytes 1720328 | tf_op jit(solution)/shard_map/ppermute | solution.py:201
  81.2 6.1 %collective-permute-start.17 = (f32[2,128,128]{2,1,0:T(8,128)S(1)}, f32[2,128,128]{2,1,0:T(8,128)S(1)}, u32[]{:S(2)}, u32[]{:S(2)}) collective-permute-start(f32[2,128,128]{2,1,0:T(8,128)S(1)} %slice.8), channel_id=1, source_target_pairs={{0,1},{1,0},{2,3},{3,2},{4,5},{5,4},{6,7},{7,6},{8,9},{9,8},{10,11... | collective-permute-start | bytes 393224 | tf_op jit(solution)/shard_map/ppermute | solution.py:201
  83.5 14.2 %collective-permute-start.25 = (bf16[1792,128]{1,0:T(8,128)(2,1)S(1)}, bf16[1792,128]{1,0:T(8,128)(2,1)S(1)}, u32[]{:S(2)}, u32[]{:S(2)}) collective-permute-start(bf16[1792,128]{1,0:T(8,128)(2,1)S(1)} %add_convert_fusion.1), channel_id=1, source_target_pairs={{0,8},{8,0},{16,24},{24,16},{1,9},{9,1},{17,25},{25,17},{2,10},{10... | collective-permute-start | bytes 1376264 | tf_op jit(solution)/shard_map/ppermute | solution.py:201
  83.6 8.6 %collective-permute-start.15 = (f32[3,128,128]{2,1,0:T(8,128)S(1)}, f32[3,128,128]{2,1,0:T(8,128)S(1)}, u32[]{:S(2)}, u32[]{:S(2)}) collective-permute-start(f32[3,128,128]{2,1,0:T(8,128)S(1)} %shard_map.51.refs_2_), channel_id=1, source_target_pairs={{0,16},{8,24},{16,0},{24,8},{1,17},{9,25},{17,1},{25,9},{2,18},{10... | collective-permute-start | bytes 589832 | tf_op jit(solution)/shard_map/ppermute | solution.py:201
  87.3 15.9 %collective-permute-start.14 = (bf16[1792,128]{1,0:T(8,128)(2,1)S(1)}, bf16[1792,128]{1,0:T(8,128)(2,1)S(1)}, u32[]{:S(2)}, u32[]{:S(2)}) collective-permute-start(bf16[1792,128]{1,0:T(8,128)(2,1)S(1)} %collective-permute-done.8), channel_id=1, source_target_pairs={{0,8},{8,0},{16,24},{24,16},{1,9},{9,1},{17,25},{25,17},{2,10},{10... | collective-permute-start | bytes 1376264 | tf_op jit(solution)/shard_map/ppermute | solution.py:201
  87.3 2.0 %collective-permute-start.19 = (f32[2,128,128]{2,1,0:T(8,128)S(1)}, f32[2,128,128]{2,1,0:T(8,128)S(1)}, u32[]{:S(2)}, u32[]{:S(2)}) collective-permute-start(f32[2,128,128]{2,1,0:T(8,128)S(1)} %collective-permute-done.17.refs_3_), channel_id=1, source_target_pairs={{0,8},{8,0},{16,24},{24,16},{1,9},{9,1},{17,25},{25,17},{2,10},{10... | collective-permute-start | bytes 393224 | tf_op jit(solution)/shard_map/ppermute | solution.py:201
  92.2 5.6 %collective-permute-start.20 = (f32[2,128,128]{2,1,0:T(8,128)S(1)}, f32[2,128,128]{2,1,0:T(8,128)S(1)}, u32[]{:S(2)}, u32[]{:S(2)}) collective-permute-start(f32[2,128,128]{2,1,0:T(8,128)S(1)} %slice.7), channel_id=1, source_target_pairs={{0,1},{1,0},{2,3},{3,2},{4,5},{5,4},{6,7},{7,6},{8,9},{9,8},{10,11... | collective-permute-start | bytes 393224 | tf_op jit(solution)/shard_map/ppermute | solution.py:201
  94.0 6.4 %collective-permute-start.21 = (f32[3,128,128]{2,1,0:T(8,128)S(1)}, f32[3,128,128]{2,1,0:T(8,128)S(1)}, u32[]{:S(2)}, u32[]{:S(2)}) collective-permute-start(f32[3,128,128]{2,1,0:T(8,128)S(1)} %collective-permute-done.15.refs_2_), channel_id=1, source_target_pairs={{0,8},{8,0},{16,24},{24,16},{1,9},{9,1},{17,25},{25,17},{2,10},{10... | collective-permute-start | bytes 589832 | tf_op jit(solution)/shard_map/ppermute | solution.py:201
  97.8 2.6 %collective-permute-start.22 = (f32[2,128,128]{2,1,0:T(8,128)S(1)}, f32[2,128,128]{2,1,0:T(8,128)S(1)}, u32[]{:S(2)}, u32[]{:S(2)}) collective-permute-start(f32[2,128,128]{2,1,0:T(8,128)S(1)} %collective-permute-done.20.refs_3_), channel_id=1, source_target_pairs={{0,8},{8,0},{16,24},{24,16},{1,9},{9,1},{17,25},{25,17},{2,10},{10... | collective-permute-start | bytes 393224 | tf_op jit(solution)/shard_map/ppermute | solution.py:201

commit v7 on v5

--- a/solution.py
+++ b/solution.py
@@ -273,25 +273,20 @@
         gram_second, gram = lax.optimization_barrier((gram_of(second, rows), gram))
         qs.append(newton_schulz(*reduce_gram(gram, 4)))
         pair = reduce_gram(gram_second)
-        qs.append(newton_schulz(*pair, qs[0]))
+        qs.append(newton_schulz(*pair))
     else:
         qs.append(newton_schulz(*reduce_gram(gram)))
 
-    q = qs[-1]
-    arrived_q = over_chips(q)
+    arrived_q = [over_chips(q) for q in qs]
     arrived_rows = [over_chips(total) for total in totals]
     outputs = []
     for distance in range(members):
-        if distance:
-            q = arrived_q[distance - 1]
-            if distance == 1:
-                q, *outputs = lax.optimization_barrier((q, *outputs))
-        pair_q = over_cores(q)
         for index, size in enumerate(sizes):
-            rows_here = totals[index]
+            rows_here, q = totals[index], qs[index]
             if distance:
                 tie = qs[-1] if index == len(sizes) - 1 else pair[0]
                 rows_here = lax.optimization_barrier((arrived_rows[index][distance - 1], tie))[0]
+                q = arrived_q[index][distance - 1]
             per_block = 2 if size % 2 else 1
             units = size * per_block // CORES
             outputs = apply_side(
@@ -299,18 +294,21 @@
                     array.reshape(units, rows // per_block, width)
                     for array in over_cores(rows_here)
                 ],
-                pair_q,
+                over_cores(q),
                 params,
                 outputs,
                 place.reshape(1),
                 table,
                 CORES * distance,
-                qs[index - 1].shape[0] if index else 0,
+                0,
                 size,
                 sum(sizes[:index]),
                 own,
                 padded,
             )
+            if distance == 0:
+                first_q, *outputs = lax.optimization_barrier((arrived_q[index][0], *outputs))
+                arrived_q[index][0] = first_q
     new_params, update = outputs
     return (new_params, update)
 

time: 99.8 us -> 100 us (level)
  starting transfers between devices: 23.3 us -> 27.6 us
  waiting for transfers between devices: 51.8 us -> 48 us
    ppermute x22 -> x25, starting transfers between devices: 23.3 us -> 27.6 us  [swap(): return lax.ppermute(array, axis, [(i, i ^ distance) for i in range(size)])]
    ppermute x22 -> x25, waiting for transfers between devices: 51.8 us -> 48 us  [swap(): return lax.ppermute(array, axis, [(i, i ^ distance) for i in range(size)])]
  transfers between devices with their start and end apart: 22 -> 25, of which waited for: 11 -> 10; matrix products, arithmetic and copies ran while one was open for 4% -> 4% of each run, Pallas kernels for 15% -> 15%
where the time goes in v7:
time: 100 us
  waiting for transfers between devices  48 us (48%)
  starting transfers between devices  27.6 us (28%)
  Pallas kernels  17.8 us (18%)
  local copies, waits for them, and re-layouts  3.13 us (3%)
  other arithmetic  1.71 us (2%)
    ppermute x25, waiting for transfers between devices, swap(): return lax.ppermute(array, axis, [(i, i ^ distance) for i in range(size)])  48 us
    ppermute x25, starting transfers between devices, swap(): return lax.ppermute(array, axis, [(i, i ^ distance) for i in range(size)])  27.6 us
    pallas_call x4, Pallas kernels, apply_side(): pl.pallas_call(functools.partial(apply_kernel, layout), in_specs=in_specs...  10.6 us
    pallas_call x2, Pallas kernels, newton_schulz(): pl.pallas_call(newton_kernel, out_shape=jax.ShapeDtypeStruct((slots, V, V...  7.14 us
    dynamic_slice x2, local copies, waits for them, and re-layouts, rows_of(): lax.dynamic_slice_in_dim(flat, (chip * own + offset) * rows + which * len...  3.08 us
  transfers between devices with their start and end apart: 25, of which 10 were waited for; matrix products, arithmetic and copies ran while one was open for 4% of the time, Pallas kernels for 15%

profile of v7, /device:TPU:0, one launch (start us, length us, event | category | flops | bytes accessed | tf_op | source)
XLA Modules:
  0.0 100.1 jit_solution(5371079642430883145)
XLA Ops:
  0.7 1.5 %constant_dynamic-slice_fusion.2 = (bf16[2240,128]{1,0:T(8,128)(2,1)S(1)}, bf16[2240,128]{1,0:T(8,128)(2,1)S(1)}, bf16[2240,128]{1,0:T(8,128)(2,1)S(1)}) fusion(bf16[16128,128]{1,0:T(8,128)(2,1)} %bitcast.29, s32[]{:T(128)S(6)} %select_n.90, s32[]{:T(128)S(6)} %select_n.91, s32[]{:T(128)S(6)} %select_n.78), kind=kLoop, calls=%fused_computation.8 | loop fusion | bytes 3440652 | tf_op jit(solution)/shard_map/dynamic_slice | solution.py:214
  2.3 2.5 %collective-permute-start = (bf16[2240,128]{1,0:T(8,128)(2,1)S(1)}, bf16[2240,128]{1,0:T(8,128)(2,1)S(1)}, u32[]{:S(2)}, u32[]{:S(2)}) collective-permute-start(bf16[2240,128]{1,0:T(8,128)(2,1)S(1)} %get-tuple-element.58), channel_id=1, source_target_pairs={{0,24},{8,16},{16,8},{24,0},{1,25},{9,17},{17,9},{25,1},{2,26},{10... | collective-permute-start | bytes 1720328 | tf_op jit(solution)/shard_map/ppermute | solution.py:188
  5.5 1.6 %constant_dynamic-slice_fusion.3 = (bf16[1792,128]{1,0:T(8,128)(2,1)S(1)}, bf16[1792,128]{1,0:T(8,128)(2,1)S(1)}, bf16[1792,128]{1,0:T(8,128)(2,1)S(1)}, bf16[1792,128]{1,0:T(8,128)(2,1)S(1)}) fusion(bf16[16128,128]{1,0:T(8,128)(2,1)} %bitcast.30, s32[]{:T(128)S(6)} %select_n.88, s32[]{:T(128)S(6)} %select_n.87, s32[]{:T(128)S(6)} %select_n.84, s32[]{:T(128)S(6)} %select_n.81), kind=kLoop, calls=%fused_computation.9 | loop fusion | bytes 3670032 | tf_op jit(solution)/shard_map/dynamic_slice | solution.py:214
  7.0 11.1 %collective-permute-done = bf16[2240,128]{1,0:T(8,128)(2,1)S(1)} collective-permute-done((bf16[2240,128]{1,0:T(8,128)(2,1)S(1)}, bf16[2240,128]{1,0:T(8,128)(2,1)S(1)}, u32[]{:S(2)}, u32[]{:S(2)}) %collective-permute-start) | collective-permute-done | bytes 573472 | tf_op jit(solution)/shard_map/ppermute | solution.py:188
  18.1 0.8 collective-permute-start.1
  18.9 1.8 %collective-permute-start.2 = (bf16[1792,128]{1,0:T(8,128)(2,1)S(1)}, bf16[1792,128]{1,0:T(8,128)(2,1)S(1)}, u32[]{:S(2)}, u32[]{:S(2)}) collective-permute-start(bf16[1792,128]{1,0:T(8,128)(2,1)S(1)} %get-tuple-element.31), channel_id=1, source_target_pairs={{0,16},{8,24},{16,0},{24,8},{1,17},{9,25},{17,1},{25,9},{2,18},{10... | collective-permute-start | bytes 1376264 | tf_op jit(solution)/shard_map/ppermute | solution.py:188
  20.7 10.7 %collective-permute-done.4 = bf16[2240,128]{1,0:T(8,128)(2,1)S(1)} collective-permute-done((bf16[2240,128]{1,0:T(8,128)(2,1)S(1)}, bf16[2240,128]{1,0:T(8,128)(2,1)S(1)}, u32[]{:S(2)}, u32[]{:S(2)}) %collective-permute-start.4) | collective-permute-done | bytes 573472 | tf_op jit(solution)/shard_map/ppermute | solution.py:188
  31.4 1.4 %add_convert_fusion = bf16[2240,128]{1,0:T(8,128)(2,1)S(1)} fusion(bf16[2240,128]{1,0:T(8,128)(2,1)S(1)} %collective-permute-done, bf16[2240,128]{1,0:T(8,128)(2,1)S(1)} %collective-permute-done.4, bf16[2240,128]{1,0:T(8,128)(2,1)S(1)} %collective-permute-done.3, bf16[16128,128]{1,0:T(8,128)(2,1)} %bitcast.31, s32[]{:T(128)S(6)} %select_n.89), kind=kLoop, calls=%fused_computation | loop fusion | flops 2293760 | bytes 2867204 | tf_op jit(solution)/shard_map/convert_element_type | solution.py:254
  33.1 1.6 %collective-permute-start.6 = (bf16[1792,128]{1,0:T(8,128)(2,1)S(1)}, bf16[1792,128]{1,0:T(8,128)(2,1)S(1)}, u32[]{:S(2)}, u32[]{:S(2)}) collective-permute-start(bf16[1792,128]{1,0:T(8,128)(2,1)S(1)} %get-tuple-element.36), channel_id=1, source_target_pairs={{0,24},{8,16},{16,8},{24,0},{1,25},{9,17},{17,9},{25,1},{2,26},{10... | collective-permute-start | bytes 1376264 | tf_op jit(solution)/shard_map/ppermute | solution.py:188
  35.1 6.1 %collective-permute-done.2 = bf16[1792,128]{1,0:T(8,128)(2,1)S(1)} collective-permute-done((bf16[1792,128]{1,0:T(8,128)(2,1)S(1)}, bf16[1792,128]{1,0:T(8,128)(2,1)S(1)}, u32[]{:S(2)}, u32[]{:S(2)}) %collective-permute-start.2) | collective-permute-done | bytes 458784 | tf_op jit(solution)/shard_map/ppermute | solution.py:188
  41.2 1.5 %collective-permute-start.7 = (f32[3,128,128]{2,1,0:T(8,128)S(1)}, f32[3,128,128]{2,1,0:T(8,128)S(1)}, u32[]{:S(2)}, u32[]{:S(2)}) collective-permute-start(f32[3,128,128]{2,1,0:T(8,128)S(1)} %pad_maximum_fusion), channel_id=1, source_target_pairs={{0,1},{1,0},{2,3},{3,2},{4,5},{5,4},{6,7},{7,6},{8,9},{9,8},{10,11... | collective-permute-start | bytes 589832 | tf_op jit(solution)/shard_map/ppermute | solution.py:188
  42.7 1.5 %collective-permute-start.22 = (bf16[2240,128]{1,0:T(8,128)(2,1)S(1)}, bf16[2240,128]{1,0:T(8,128)(2,1)S(1)}, u32[]{:S(2)}, u32[]{:S(2)}) collective-permute-start(bf16[2240,128]{1,0:T(8,128)(2,1)S(1)} %add_convert_fusion), channel_id=1, source_target_pairs={{0,16},{8,24},{16,0},{24,8},{1,17},{9,25},{17,1},{25,9},{2,18},{10... | collective-permute-start | bytes 1720328 | tf_op jit(solution)/shard_map/ppermute | solution.py:188
  44.2 3.6 %collective-permute-done.7 = f32[3,128,128]{2,1,0:T(8,128)S(1)} collective-permute-done((f32[3,128,128]{2,1,0:T(8,128)S(1)}, f32[3,128,128]{2,1,0:T(8,128)S(1)}, u32[]{:S(2)}, u32[]{:S(2)}) %collective-permute-start.7) | collective-permute-done | bytes 196640 | tf_op jit(solution)/shard_map/ppermute | solution.py:188
  47.8 2.3 %collective-permute-done.6 = bf16[1792,128]{1,0:T(8,128)(2,1)S(1)} collective-permute-done((bf16[1792,128]{1,0:T(8,128)(2,1)S(1)}, bf16[1792,128]{1,0:T(8,128)(2,1)S(1)}, u32[]{:S(2)}, u32[]{:S(2)}) %collective-permute-start.6) | collective-permute-done | bytes 458784 | tf_op jit(solution)/shard_map/ppermute | solution.py:188
  50.1 2.5 %collective-permute-start.9 = (f32[3,128,128]{2,1,0:T(8,128)S(1)}, f32[3,128,128]{2,1,0:T(8,128)S(1)}, u32[]{:S(2)}, u32[]{:S(2)}) collective-permute-start(f32[3,128,128]{2,1,0:T(8,128)S(1)} %add.152), channel_id=1, source_target_pairs={{0,2},{1,3},{2,0},{3,1},{4,6},{5,7},{6,4},{7,5},{8,10},{9,11},{10,... | collective-permute-start | bytes 589832 | tf_op jit(solution)/shard_map/ppermute | solution.py:188
  52.8 1.6 %collective-permute-start.8 = (bf16[1792,128]{1,0:T(8,128)(2,1)S(1)}, bf16[1792,128]{1,0:T(8,128)(2,1)S(1)}, u32[]{:S(2)}, u32[]{:S(2)}) collective-permute-start(bf16[1792,128]{1,0:T(8,128)(2,1)S(1)} %add_convert_fusion.1), channel_id=1, source_target_pairs={{0,16},{8,24},{16,0},{24,8},{1,17},{9,25},{17,1},{25,9},{2,18},{10... | collective-permute-start | bytes 1376264 | tf_op jit(solution)/shard_map/ppermute | solution.py:188
  54.7 3.0 %collective-permute-done.9 = f32[3,128,128]{2,1,0:T(8,128)S(1)} collective-permute-done((f32[3,128,128]{2,1,0:T(8,128)S(1)}, f32[3,128,128]{2,1,0:T(8,128)S(1)}, u32[]{:S(2)}, u32[]{:S(2)}) %collective-permute-start.9) | collective-permute-done | bytes 196640 | tf_op jit(solution)/shard_map/ppermute | solution.py:188
  57.7 1.7 %collective-permute-start.10 = (f32[2,128,128]{2,1,0:T(8,128)S(1)}, f32[2,128,128]{2,1,0:T(8,128)S(1)}, u32[]{:S(2)}, u32[]{:S(2)}) collective-permute-start(f32[2,128,128]{2,1,0:T(8,128)S(1)} %fusion.3), channel_id=1, source_target_pairs={{0,1},{1,0},{2,3},{3,2},{4,5},{5,4},{6,7},{7,6},{8,9},{9,8},{10,11... | collective-permute-start | bytes 393224 | tf_op jit(solution)/shard_map/ppermute | solution.py:188
  59.4 2.6 %collective-permute-start.17 = (f32[3,128,128]{2,1,0:T(8,128)S(1)}, f32[3,128,128]{2,1,0:T(8,128)S(1)}, u32[]{:S(2)}, u32[]{:S(2)}) collective-permute-start(f32[3,128,128]{2,1,0:T(8,128)S(1)} %add.155.gram_ref), channel_id=1, source_target_pairs={{0,4},{1,5},{2,6},{3,7},{4,0},{5,1},{6,2},{7,3},{8,12},{9,13},{10,... | collective-permute-start | bytes 589832 | tf_op jit(solution)/shard_map/ppermute | solution.py:188
  62.8 1.8 %collective-permute-start.11 = (f32[2,128,128]{2,1,0:T(8,128)S(1)}, f32[2,128,128]{2,1,0:T(8,128)S(1)}, u32[]{:S(2)}, u32[]{:S(2)}) collective-permute-start(f32[2,128,128]{2,1,0:T(8,128)S(1)} %add.156), channel_id=1, source_target_pairs={{0,2},{1,3},{2,0},{3,1},{4,6},{5,7},{6,4},{7,5},{8,10},{9,11},{10,... | collective-permute-start | bytes 393224 | tf_op jit(solution)/shard_map/ppermute | solution.py:188
  64.6 6.2 %collective-permute-done.11 = f32[2,128,128]{2,1,0:T(8,128)S(1)} collective-permute-done((f32[2,128,128]{2,1,0:T(8,128)S(1)}, f32[2,128,128]{2,1,0:T(8,128)S(1)}, u32[]{:S(2)}, u32[]{:S(2)}) %collective-permute-start.11) | collective-permute-done | bytes 131104 | tf_op jit(solution)/shard_map/ppermute | solution.py:188
  70.9 1.9 %collective-permute-start.12 = (f32[2,128,128]{2,1,0:T(8,128)S(1)}, f32[2,128,128]{2,1,0:T(8,128)S(1)}, u32[]{:S(2)}, u32[]{:S(2)}) collective-permute-start(f32[2,128,128]{2,1,0:T(8,128)S(1)} %add.157.gram_ref), channel_id=1, source_target_pairs={{0,4},{1,5},{2,6},{3,7},{4,0},{5,1},{6,2},{7,3},{8,12},{9,13},{10,... | collective-permute-start | bytes 393224 | tf_op jit(solution)/shard_map/ppermute | solution.py:188
  73.0 3.8 %shard_map.51.refs_2_ = f32[3,128,128]{2,1,0:T(8,128)S(1)} custom-call(f32[3,128,128]{2,1,0:T(8,128)S(1)} %add.155.gram_ref, f32[3,128,128]{2,1,0:T(8,128)S(1)} %collective-permute-done.17.arrived_ref), custom_call_target="tpu_custom_call" | custom-call | flops 1358954496 | bytes 589824 | tf_op jit(solution)/shard_map/pallas_call | solution.py:68
  77.2 3.4 %collective-permute-done.12.arrived_ref = f32[2,128,128]{2,1,0:T(8,128)S(1)} collective-permute-done((f32[2,128,128]{2,1,0:T(8,128)S(1)}, f32[2,128,128]{2,1,0:T(8,128)S(1)}, u32[]{:S(2)}, u32[]{:S(2)}) %collective-permute-start.12) | collective-permute-done | bytes 131104 | tf_op jit(solution)/shard_map/ppermute | solution.py:188
  80.6 1.6 %collective-permute-start.18 = (f32[3,128,128]{2,1,0:T(8,128)S(1)}, f32[3,128,128]{2,1,0:T(8,128)S(1)}, u32[]{:S(2)}, u32[]{:S(2)}) collective-permute-start(f32[3,128,128]{2,1,0:T(8,128)S(1)} %shard_map.51.refs_2_), channel_id=1, source_target_pairs={{0,16},{8,24},{16,0},{24,8},{1,17},{9,25},{17,1},{25,9},{2,18},{10... | collective-permute-start | bytes 589832 | tf_op jit(solution)/shard_map/ppermute | solution.py:188
  82.2 3.4 %shard_map.50.refs_2_ = f32[2,128,128]{2,1,0:T(8,128)S(1)} custom-call(f32[2,128,128]{2,1,0:T(8,128)S(1)} %add.157.gram_ref, f32[2,128,128]{2,1,0:T(8,128)S(1)} %collective-permute-done.12.arrived_ref), custom_call_target="tpu_custom_call" | custom-call | flops 905969664 | bytes 393216 | tf_op jit(solution)/shard_map/pallas_call | solution.py:68
  86.2 0.9 collective-permute-done.18.refs_2_
  87.1 1.6 %collective-permute-start.14 = (f32[2,128,128]{2,1,0:T(8,128)S(1)}, f32[2,128,128]{2,1,0:T(8,128)S(1)}, u32[]{:S(2)}, u32[]{:S(2)}) collective-permute-start(f32[2,128,128]{2,1,0:T(8,128)S(1)} %shard_map.50.refs_2_), channel_id=1, source_target_pairs={{0,16},{8,24},{16,0},{24,8},{1,17},{9,25},{17,1},{25,9},{2,18},{10... | collective-permute-start | bytes 393224 | tf_op jit(solution)/shard_map/ppermute | solution.py:188
  88.7 2.8 %shard_map.52 = (f32[18,896,128]{2,1,0:T(8,128)}, bf16[18,896,128]{2,1,0:T(8,128)(2,1)}) custom-call(s32[1]{0:T(128)} %bitcast.place_ref, s32[18]{0:T(128)S(1)} %copy-done, bf16[5,448,128]{2,1,0:T(8,128)(2,1)S(1)} %bitcast.21, bf16[5,448,128]{2,1,0:T(8,128)(2,1)S(1)} %bitcast.22, f32[3,128,128]{2,1,0:T(8,128)S(1)} %shard_map.51.refs_2_, ...), custom_call_target="tpu_custom_call" | custom-call | flops 293601280 | bytes 6881280 | tf_op jit(solution)/shard_map/pallas_call | solution.py:160
  91.6 2.5 %shard_map.53 = (f32[18,896,128]{2,1,0:T(8,128)}, bf16[18,896,128]{2,1,0:T(8,128)(2,1)}) custom-call(s32[1]{0:T(128)} %bitcast.place_ref, s32[18]{0:T(128)S(1)} %copy-done, bf16[2,896,128]{2,1,0:T(8,128)(2,1)S(1)} %bitcast.20, bf16[2,896,128]{2,1,0:T(8,128)(2,1)S(1)} %bitcast.26, ...), custom_call_target="tpu_custom_call", output_to_operand_aliasing={{0}: (7, {}), {1}: (8, {})} | custom-call | flops 234881024 | bytes 5505024 | tf_op jit(solution)/shard_map/pallas_call | solution.py:160
  94.7 2.8 %shard_map.54 = (f32[18,896,128]{2,1,0:T(8,128)}, bf16[18,896,128]{2,1,0:T(8,128)(2,1)}) custom-call(s32[1]{0:T(128)} %bitcast.place_ref, s32[18]{0:T(128)S(1)} %copy-done, bf16[5,448,128]{2,1,0:T(8,128)(2,1)S(1)} %bitcast.23, bf16[5,448,128]{2,1,0:T(8,128)(2,1)S(1)} %bitcast.24, ...), custom_call_target="tpu_custom_call", output_to_operand_aliasing={{0}: (7, {}), {1}: (8, {})} | custom-call | flops 293601280 | bytes 6881280 | tf_op jit(solution)/shard_map/pallas_call | solution.py:160
  97.6 2.5 %shard_map.55 = (f32[18,896,128]{2,1,0:T(8,128)}, bf16[18,896,128]{2,1,0:T(8,128)(2,1)}) custom-call(s32[1]{0:T(128)} %bitcast.place_ref, s32[18]{0:T(128)S(1)} %copy-done, bf16[2,896,128]{2,1,0:T(8,128)(2,1)S(1)} %bitcast.25, bf16[2,896,128]{2,1,0:T(8,128)(2,1)S(1)} %bitcast.27, ...), custom_call_target="tpu_custom_call", output_to_operand_aliasing={{0}: (7, {}), {1}: (8, {})} | custom-call | flops 234881024 | bytes 5505024 | tf_op jit(solution)/shard_map/pallas_call | solution.py:160
  (45 shorter events, 4.7 us)
Async XLA Ops:
  2.3 15.8 %collective-permute-start = (bf16[2240,128]{1,0:T(8,128)(2,1)S(1)}, bf16[2240,128]{1,0:T(8,128)(2,1)S(1)}, u32[]{:S(2)}, u32[]{:S(2)}) collective-permute-start(bf16[2240,128]{1,0:T(8,128)(2,1)S(1)} %get-tuple-element.58), channel_id=1, source_target_pairs={{0,24},{8,16},{16,8},{24,0},{1,25},{9,17},{17,9},{25,1},{2,26},{10... | collective-permute-start | bytes 1720328 | tf_op jit(solution)/shard_map/ppermute | solution.py:188
  4.7 16.0 %collective-permute-start.3 = (bf16[2240,128]{1,0:T(8,128)(2,1)S(1)}, bf16[2240,128]{1,0:T(8,128)(2,1)S(1)}, u32[]{:S(2)}, u32[]{:S(2)}) collective-permute-start(bf16[2240,128]{1,0:T(8,128)(2,1)S(1)} %get-tuple-element.56), channel_id=1, source_target_pairs={{0,8},{8,0},{16,24},{24,16},{1,9},{9,1},{17,25},{25,17},{2,10},{10... | collective-permute-start | bytes 1720328 | tf_op jit(solution)/shard_map/ppermute | solution.py:188
  5.4 26.0 %collective-permute-start.4 = (bf16[2240,128]{1,0:T(8,128)(2,1)S(1)}, bf16[2240,128]{1,0:T(8,128)(2,1)S(1)}, u32[]{:S(2)}, u32[]{:S(2)}) collective-permute-start(bf16[2240,128]{1,0:T(8,128)(2,1)S(1)} %get-tuple-element.57), channel_id=1, source_target_pairs={{0,16},{8,24},{16,0},{24,8},{1,17},{9,25},{17,1},{25,9},{2,18},{10... | collective-permute-start | bytes 1720328 | tf_op jit(solution)/shard_map/ppermute | solution.py:188
  18.1 17.0 %collective-permute-start.1 = (bf16[1792,128]{1,0:T(8,128)(2,1)S(1)}, bf16[1792,128]{1,0:T(8,128)(2,1)S(1)}, u32[]{:S(2)}, u32[]{:S(2)}) collective-permute-start(bf16[1792,128]{1,0:T(8,128)(2,1)S(1)} %get-tuple-element.30), channel_id=1, source_target_pairs={{0,8},{8,0},{16,24},{24,16},{1,9},{9,1},{17,25},{25,17},{2,10},{10... | collective-permute-start | bytes 1376264 | tf_op jit(solution)/shard_map/ppermute | solution.py:188
  18.9 22.3 %collective-permute-start.2 = (bf16[1792,128]{1,0:T(8,128)(2,1)S(1)}, bf16[1792,128]{1,0:T(8,128)(2,1)S(1)}, u32[]{:S(2)}, u32[]{:S(2)}) collective-permute-start(bf16[1792,128]{1,0:T(8,128)(2,1)S(1)} %get-tuple-element.31), channel_id=1, source_target_pairs={{0,16},{8,24},{16,0},{24,8},{1,17},{9,25},{17,1},{25,9},{2,18},{10... | collective-permute-start | bytes 1376264 | tf_op jit(solution)/shard_map/ppermute | solution.py:188
  33.0 2.0 %collective-permute-start.5 = (f32[1,128,128]{2,1,0:T(8,128)S(1)}, f32[1,128,128]{2,1,0:T(8,128)S(1)}, u32[]{:S(2)}, u32[]{:S(2)}) collective-permute-start(f32[1,128,128]{2,1,0:T(8,128)S(1)} %convolution_bitcast_fusion), channel_id=1, source_target_pairs={{0,8},{8,0},{16,24},{24,16},{1,9},{9,1},{17,25},{25,17},{2,10},{10... | collective-permute-start | bytes 196616 | tf_op jit(solution)/shard_map/ppermute | solution.py:188
  33.1 16.9 %collective-permute-start.6 = (bf16[1792,128]{1,0:T(8,128)(2,1)S(1)}, bf16[1792,128]{1,0:T(8,128)(2,1)S(1)}, u32[]{:S(2)}, u32[]{:S(2)}) collective-permute-start(bf16[1792,128]{1,0:T(8,128)(2,1)S(1)} %get-tuple-element.36), channel_id=1, source_target_pairs={{0,24},{8,16},{16,8},{24,0},{1,25},{9,17},{17,9},{25,1},{2,26},{10... | collective-permute-start | bytes 1376264 | tf_op jit(solution)/shard_map/ppermute | solution.py:188
  34.7 54.0 %slice-start = ((s8[8257536]{0:T(1024)(128)(4,1)}), s8[4194304]{0:T(1024)(128)(4,1)S(1)}, s32[]{:S(2)}) async-start(s8[8257536]{0:T(1024)(128)(4,1)} %bitcast.17), calls=%async_computation | async-start | bytes 8388608
  41.2 6.5 %collective-permute-start.7 = (f32[3,128,128]{2,1,0:T(8,128)S(1)}, f32[3,128,128]{2,1,0:T(8,128)S(1)}, u32[]{:S(2)}, u32[]{:S(2)}) collective-permute-start(f32[3,128,128]{2,1,0:T(8,128)S(1)} %pad_maximum_fusion), channel_id=1, source_target_pairs={{0,1},{1,0},{2,3},{3,2},{4,5},{5,4},{6,7},{7,6},{8,9},{9,8},{10,11... | collective-permute-start | bytes 589832 | tf_op jit(solution)/shard_map/ppermute | solution.py:188
  42.7 42.8 %collective-permute-start.19 = (bf16[2240,128]{1,0:T(8,128)(2,1)S(1)}, bf16[2240,128]{1,0:T(8,128)(2,1)S(1)}, u32[]{:S(2)}, u32[]{:S(2)}) collective-permute-start(bf16[2240,128]{1,0:T(8,128)(2,1)S(1)} %add_convert_fusion), channel_id=1, source_target_pairs={{0,8},{8,0},{16,24},{24,16},{1,9},{9,1},{17,25},{25,17},{2,10},{10... | collective-permute-start | bytes 1720328 | tf_op jit(solution)/shard_map/ppermute | solution.py:188
  42.7 28.1 %collective-permute-start.22 = (bf16[2240,128]{1,0:T(8,128)(2,1)S(1)}, bf16[2240,128]{1,0:T(8,128)(2,1)S(1)}, u32[]{:S(2)}, u32[]{:S(2)}) collective-permute-start(bf16[2240,128]{1,0:T(8,128)(2,1)S(1)} %add_convert_fusion), channel_id=1, source_target_pairs={{0,16},{8,24},{16,0},{24,8},{1,17},{9,25},{17,1},{25,9},{2,18},{10... | collective-permute-start | bytes 1720328 | tf_op jit(solution)/shard_map/ppermute | solution.py:188
  50.1 7.6 %collective-permute-start.9 = (f32[3,128,128]{2,1,0:T(8,128)S(1)}, f32[3,128,128]{2,1,0:T(8,128)S(1)}, u32[]{:S(2)}, u32[]{:S(2)}) collective-permute-start(f32[3,128,128]{2,1,0:T(8,128)S(1)} %add.152), channel_id=1, source_target_pairs={{0,2},{1,3},{2,0},{3,1},{4,6},{5,7},{6,4},{7,5},{8,10},{9,11},{10,... | collective-permute-start | bytes 589832 | tf_op jit(solution)/shard_map/ppermute | solution.py:188
  52.8 24.1 %collective-permute-start.8 = (bf16[1792,128]{1,0:T(8,128)(2,1)S(1)}, bf16[1792,128]{1,0:T(8,128)(2,1)S(1)}, u32[]{:S(2)}, u32[]{:S(2)}) collective-permute-start(bf16[1792,128]{1,0:T(8,128)(2,1)S(1)} %add_convert_fusion.1), channel_id=1, source_target_pairs={{0,16},{8,24},{16,0},{24,8},{1,17},{9,25},{17,1},{25,9},{2,18},{10... | collective-permute-start | bytes 1376264 | tf_op jit(solution)/shard_map/ppermute | solution.py:188
  57.7 5.1 %collective-permute-start.10 = (f32[2,128,128]{2,1,0:T(8,128)S(1)}, f32[2,128,128]{2,1,0:T(8,128)S(1)}, u32[]{:S(2)}, u32[]{:S(2)}) collective-permute-start(f32[2,128,128]{2,1,0:T(8,128)S(1)} %fusion.3), channel_id=1, source_target_pairs={{0,1},{1,0},{2,3},{3,2},{4,5},{5,4},{6,7},{7,6},{8,9},{9,8},{10,11... | collective-permute-start | bytes 393224 | tf_op jit(solution)/shard_map/ppermute | solution.py:188
  59.4 13.3 %collective-permute-start.17 = (f32[3,128,128]{2,1,0:T(8,128)S(1)}, f32[3,128,128]{2,1,0:T(8,128)S(1)}, u32[]{:S(2)}, u32[]{:S(2)}) collective-permute-start(f32[3,128,128]{2,1,0:T(8,128)S(1)} %add.155.gram_ref), channel_id=1, source_target_pairs={{0,4},{1,5},{2,6},{3,7},{4,0},{5,1},{6,2},{7,3},{8,12},{9,13},{10,... | collective-permute-start | bytes 589832 | tf_op jit(solution)/shard_map/ppermute | solution.py:188
  62.8 8.0 %collective-permute-start.11 = (f32[2,128,128]{2,1,0:T(8,128)S(1)}, f32[2,128,128]{2,1,0:T(8,128)S(1)}, u32[]{:S(2)}, u32[]{:S(2)}) collective-permute-start(f32[2,128,128]{2,1,0:T(8,128)S(1)} %add.156), channel_id=1, source_target_pairs={{0,2},{1,3},{2,0},{3,1},{4,6},{5,7},{6,4},{7,5},{8,10},{9,11},{10,... | collective-permute-start | bytes 393224 | tf_op jit(solution)/shard_map/ppermute | solution.py:188
  70.8 20.7 %collective-permute-start.15 = (bf16[1792,128]{1,0:T(8,128)(2,1)S(1)}, bf16[1792,128]{1,0:T(8,128)(2,1)S(1)}, u32[]{:S(2)}, u32[]{:S(2)}) collective-permute-start(bf16[1792,128]{1,0:T(8,128)(2,1)S(1)} %add_convert_fusion.1), channel_id=1, source_target_pairs={{0,8},{8,0},{16,24},{24,16},{1,9},{9,1},{17,25},{25,17},{2,10},{10... | collective-permute-start | bytes 1376264 | tf_op jit(solution)/shard_map/ppermute | solution.py:188
  70.8 17.9 %slice-start.1 = ((s8[8257536]{0:T(1024)(128)(4,1)}), s8[4063232]{0:T(1024)(128)(4,1)S(1)}, s32[]{:S(2)}) async-start(s8[8257536]{0:T(1024)(128)(4,1)} %bitcast.17), calls=%async_computation.1 | async-start | bytes 8126464
  70.8 17.9 %copy-start = (s32[18]{0:T(128)S(1)}, s32[18]{0:T(128)}, u32[]{:S(2)}) copy-start(s32[18]{0:T(128)} %table_ref.7) | copy-start | bytes 220
  70.9 9.7 %collective-permute-start.12 = (f32[2,128,128]{2,1,0:T(8,128)S(1)}, f32[2,128,128]{2,1,0:T(8,128)S(1)}, u32[]{:S(2)}, u32[]{:S(2)}) collective-permute-start(f32[2,128,128]{2,1,0:T(8,128)S(1)} %add.157.gram_ref), channel_id=1, source_target_pairs={{0,4},{1,5},{2,6},{3,7},{4,0},{5,1},{6,2},{7,3},{8,12},{9,13},{10,... | collective-permute-start | bytes 393224 | tf_op jit(solution)/shard_map/ppermute | solution.py:188
  72.8 22.0 %collective-permute-start.23 = (bf16[2240,128]{1,0:T(8,128)(2,1)S(1)}, bf16[2240,128]{1,0:T(8,128)(2,1)S(1)}, u32[]{:S(2)}, u32[]{:S(2)}) collective-permute-start(bf16[2240,128]{1,0:T(8,128)(2,1)S(1)} %collective-permute-done.22), channel_id=1, source_target_pairs={{0,8},{8,0},{16,24},{24,16},{1,9},{9,1},{17,25},{25,17},{2,10},{10... | collective-permute-start | bytes 1720328 | tf_op jit(solution)/shard_map/ppermute | solution.py:188
  76.8 8.9 %collective-permute-start.20 = (f32[3,128,128]{2,1,0:T(8,128)S(1)}, f32[3,128,128]{2,1,0:T(8,128)S(1)}, u32[]{:S(2)}, u32[]{:S(2)}) collective-permute-start(f32[3,128,128]{2,1,0:T(8,128)S(1)} %shard_map.51.refs_2_), channel_id=1, source_target_pairs={{0,8},{8,0},{16,24},{24,16},{1,9},{9,1},{17,25},{25,17},{2,10},{10... | collective-permute-start | bytes 589832 | tf_op jit(solution)/shard_map/ppermute | solution.py:188
  80.6 6.5 %collective-permute-start.18 = (f32[3,128,128]{2,1,0:T(8,128)S(1)}, f32[3,128,128]{2,1,0:T(8,128)S(1)}, u32[]{:S(2)}, u32[]{:S(2)}) collective-permute-start(f32[3,128,128]{2,1,0:T(8,128)S(1)} %shard_map.51.refs_2_), channel_id=1, source_target_pairs={{0,16},{8,24},{16,0},{24,8},{1,17},{9,25},{17,1},{25,9},{2,18},{10... | collective-permute-start | bytes 589832 | tf_op jit(solution)/shard_map/ppermute | solution.py:188
  85.6 12.0 %collective-permute-start.13 = (bf16[1792,128]{1,0:T(8,128)(2,1)S(1)}, bf16[1792,128]{1,0:T(8,128)(2,1)S(1)}, u32[]{:S(2)}, u32[]{:S(2)}) collective-permute-start(bf16[1792,128]{1,0:T(8,128)(2,1)S(1)} %collective-permute-done.8), channel_id=1, source_target_pairs={{0,8},{8,0},{16,24},{24,16},{1,9},{9,1},{17,25},{25,17},{2,10},{10... | collective-permute-start | bytes 1376264 | tf_op jit(solution)/shard_map/ppermute | solution.py:188
  85.7 5.9 %collective-permute-start.16 = (f32[2,128,128]{2,1,0:T(8,128)S(1)}, f32[2,128,128]{2,1,0:T(8,128)S(1)}, u32[]{:S(2)}, u32[]{:S(2)}) collective-permute-start(f32[2,128,128]{2,1,0:T(8,128)S(1)} %shard_map.50.refs_2_), channel_id=1, source_target_pairs={{0,8},{8,0},{16,24},{24,16},{1,9},{9,1},{17,25},{25,17},{2,10},{10... | collective-permute-start | bytes 393224 | tf_op jit(solution)/shard_map/ppermute | solution.py:188
  87.1 7.1 %collective-permute-start.14 = (f32[2,128,128]{2,1,0:T(8,128)S(1)}, f32[2,128,128]{2,1,0:T(8,128)S(1)}, u32[]{:S(2)}, u32[]{:S(2)}) collective-permute-start(f32[2,128,128]{2,1,0:T(8,128)S(1)} %shard_map.50.refs_2_), channel_id=1, source_target_pairs={{0,16},{8,24},{16,0},{24,8},{1,17},{9,25},{17,1},{25,9},{2,18},{10... | collective-permute-start | bytes 393224 | tf_op jit(solution)/shard_map/ppermute | solution.py:188
  91.5 3.2 %collective-permute-start.24 = (f32[3,128,128]{2,1,0:T(8,128)S(1)}, f32[3,128,128]{2,1,0:T(8,128)S(1)}, u32[]{:S(2)}, u32[]{:S(2)}) collective-permute-start(f32[3,128,128]{2,1,0:T(8,128)S(1)} %collective-permute-done.18.refs_2_), channel_id=1, source_target_pairs={{0,8},{8,0},{16,24},{24,16},{1,9},{9,1},{17,25},{25,17},{2,10},{10... | collective-permute-start | bytes 589832 | tf_op jit(solution)/shard_map/ppermute | solution.py:188
  94.2 3.3 %collective-permute-start.21 = (f32[2,128,128]{2,1,0:T(8,128)S(1)}, f32[2,128,128]{2,1,0:T(8,128)S(1)}, u32[]{:S(2)}, u32[]{:S(2)}) collective-permute-start(f32[2,128,128]{2,1,0:T(8,128)S(1)} %collective-permute-done.14.refs_2_), channel_id=1, source_target_pairs={{0,8},{8,0},{16,24},{24,16},{1,9},{9,1},{17,25},{25,17},{2,10},{10... | collective-permute-start | bytes 393224 | tf_op jit(solution)/shard_map/ppermute | solution.py:188

commit v8 on v7

--- a/solution.py
+++ b/solution.py
@@ -105,16 +105,18 @@
         for unit in range(units)
     ]
 
-    def compute(index, unit, item, head, span, slot):
+    def product(index, unit, slot):
         q = qs[index][slot]
         high = q.astype(jnp.bfloat16)
         low = (q - high.astype(jnp.float32)).astype(jnp.bfloat16)
         rows = sources[index][unit]
-        ortho = jnp.dot(
+        return jnp.dot(
             jnp.concatenate([rows, rows], axis=1),
             jnp.concatenate([high, low], axis=0),
             preferred_element_type=jnp.float32,
         )
+
+    def update(ortho, item, head, span):
         ortho = ortho.astype(jnp.bfloat16).astype(jnp.float32)
         scaled = 0.2 * math.sqrt(max(D, V)) * ortho
         params = params_ref[head, span]
@@ -125,6 +127,9 @@
             update_buf.at[item], update_ref.at[head, span], update_sems.at[item]
         ).start()
 
+    def compute(index, unit, item, head, span, slot):
+        update(product(index, unit, slot), item, head, span)
+
     def finish(item):
         span = pl.ds(0, unit_rows)
         pltpu.make_async_copy(new_buf.at[item], new_ref.at[0, span], new_sems.at[item]).wait()
@@ -132,9 +137,15 @@
             update_buf.at[item], update_ref.at[0, span], update_sems.at[item]
         ).wait()
 
-    for index, unit, item, (valid, head, span, slot) in items:
-        run = functools.partial(compute, index, unit, item, head, span, slot)
-        pl.when(valid)(run) if padded else run()
+    if padded:
+        for index, unit, item, (valid, head, span, slot) in items:
+            pl.when(valid)(functools.partial(compute, index, unit, item, head, span, slot))
+    else:
+        products = [product(index, unit, found[3]) for index, unit, _, found in items[:1]]
+        for number, (_, _, item, (_, head, span, _)) in enumerate(items):
+            for index, unit, _, found in items[number + 1 : number + 2]:
+                products.append(product(index, unit, found[3]))
+            update(products[number], item, head, span)
     for index, unit, item, (valid, head, span, slot) in items:
         run = functools.partial(finish, item)
         pl.when(valid)(run) if padded else run()
@@ -251,6 +262,25 @@
         terms[-1], *pieces = lax.optimization_barrier((terms[-1], *pieces))
         *seconds, late = exchange(pieces)
 
+    def apply_one(distance, index, sources, pair_q, outputs):
+        size = sizes[index]
+        per_block = 2 if size % 2 else 1
+        units = size * per_block // CORES
+        return apply_side(
+            [array.reshape(units, rows // per_block, width) for array in sources],
+            pair_q,
+            params,
+            outputs,
+            place.reshape(1),
+            table,
+            CORES * distance,
+            0,
+            size,
+            sum(sizes[:index]),
+            own,
+            padded,
+        )
+
     first = total_of(terms).astype(jnp.bfloat16)
     whole = size // 2
     if size % 2:
@@ -273,39 +303,26 @@
         gram_second, gram = lax.optimization_barrier((gram_of(second, rows), gram))
         qs.append(newton_schulz(*reduce_gram(gram, 4)))
         pair = reduce_gram(gram_second)
+        outputs = apply_one(0, 0, over_cores(first), over_cores(qs[0]), [])
+        pair, outputs = lax.optimization_barrier((pair, list(outputs)))
         qs.append(newton_schulz(*pair))
     else:
         qs.append(newton_schulz(*reduce_gram(gram)))
 
     arrived_q = [over_chips(q) for q in qs]
     arrived_rows = [over_chips(total) for total in totals]
-    outputs = []
+    if len(sizes) == 1:
+        outputs = []
     for distance in range(members):
-        for index, size in enumerate(sizes):
-            rows_here, q = totals[index], qs[index]
-            if distance:
-                tie = qs[-1] if index == len(sizes) - 1 else pair[0]
-                rows_here = lax.optimization_barrier((arrived_rows[index][distance - 1], tie))[0]
-                q = arrived_q[index][distance - 1]
-            per_block = 2 if size % 2 else 1
-            units = size * per_block // CORES
-            outputs = apply_side(
-                [
-                    array.reshape(units, rows // per_block, width)
-                    for array in over_cores(rows_here)
-                ],
-                over_cores(q),
-                params,
-                outputs,
-                place.reshape(1),
-                table,
-                CORES * distance,
-                0,
-                size,
-                sum(sizes[:index]),
-                own,
-                padded,
-            )
+        for index in range(len(sizes)):
+            if distance or index or len(sizes) == 1:
+                rows_here, q = totals[index], qs[index]
+                if distance:
+                    tie = qs[-1] if index == len(sizes) - 1 else pair[0]
+                    rows_here = arrived_rows[index][distance - 1]
+                    rows_here = lax.optimization_barrier((rows_here, tie))[0]
+                    q = arrived_q[index][distance - 1]
+                outputs = apply_one(distance, index, over_cores(rows_here), over_cores(q), outputs)
             if distance == 0:
                 first_q, *outputs = lax.optimization_barrier((arrived_q[index][0], *outputs))
                 arrived_q[index][0] = first_q

time: 100 us -> 101 us (1.010)
  waiting for transfers between devices: 48 us -> 51.5 us
  starting transfers between devices: 27.6 us -> 24.6 us
    ppermute x25, waiting for transfers between devices: 48 us -> 51.5 us  [swap(): return lax.ppermute(array, axis, [(i, i ^ distance) for i in range(size)])]
    ppermute x25, starting transfers between devices: 27.6 us -> 24.6 us  [swap(): return lax.ppermute(array, axis, [(i, i ^ distance) for i in range(size)])]
  transfers between devices with their start and end apart: 25 -> 25, of which waited for: 10 -> 12; matrix products, arithmetic and copies ran while one was open for 4% -> 4% of each run, Pallas kernels for 15% -> 15%
where the time goes in v8:
time: 101 us
  waiting for transfers between devices  51.5 us (51%)
  starting transfers between devices  24.6 us (24%)
  Pallas kernels  17.8 us (18%)
  local copies, waits for them, and re-layouts  3.15 us (3%)
  other arithmetic  1.86 us (2%)
    ppermute x25, waiting for transfers between devices, swap(): return lax.ppermute(array, axis, [(i, i ^ distance) for i in range(size)])  51.5 us
    ppermute x25, starting transfers between devices, swap(): return lax.ppermute(array, axis, [(i, i ^ distance) for i in range(size)])  24.6 us
    pallas_call x4, Pallas kernels, apply_side(): pl.pallas_call(functools.partial(apply_kernel, layout), in_specs=in_specs...  10.7 us
    pallas_call x2, Pallas kernels, newton_schulz(): pl.pallas_call(newton_kernel, out_shape=jax.ShapeDtypeStruct((slots, V, V...  7.15 us
    dynamic_slice x2, local copies, waits for them, and re-layouts, rows_of(): lax.dynamic_slice_in_dim(flat, (chip * own + offset) * rows + which * len...  3.09 us
  transfers between devices with their start and end apart: 25, of which 12 were waited for; matrix products, arithmetic and copies ran while one was open for 4% of the time, Pallas kernels for 15%

profile of v8, /device:TPU:0, one launch (start us, length us, event | category | flops | bytes accessed | tf_op | source)
XLA Modules:
  0.0 100.8 jit_solution(872586896912895906)
XLA Ops:
  0.7 1.5 %constant_dynamic-slice_fusion.2 = (bf16[2240,128]{1,0:T(8,128)(2,1)S(1)}, bf16[2240,128]{1,0:T(8,128)(2,1)S(1)}, bf16[2240,128]{1,0:T(8,128)(2,1)S(1)}) fusion(bf16[16128,128]{1,0:T(8,128)(2,1)} %bitcast.29, s32[]{:T(128)S(6)} %select_n.90, s32[]{:T(128)S(6)} %select_n.91, s32[]{:T(128)S(6)} %select_n.78), kind=kLoop, calls=%fused_computation.8 | loop fusion | bytes 3440652 | tf_op jit(solution)/shard_map/dynamic_slice | solution.py:225
  2.3 2.5 %collective-permute-start = (bf16[2240,128]{1,0:T(8,128)(2,1)S(1)}, bf16[2240,128]{1,0:T(8,128)(2,1)S(1)}, u32[]{:S(2)}, u32[]{:S(2)}) collective-permute-start(bf16[2240,128]{1,0:T(8,128)(2,1)S(1)} %get-tuple-element.66), channel_id=1, source_target_pairs={{0,24},{8,16},{16,8},{24,0},{1,25},{9,17},{17,9},{25,1},{2,26},{10... | collective-permute-start | bytes 1720328 | tf_op jit(solution)/shard_map/ppermute | solution.py:199
  5.5 1.6 %constant_dynamic-slice_fusion.3 = (bf16[1792,128]{1,0:T(8,128)(2,1)S(1)}, bf16[1792,128]{1,0:T(8,128)(2,1)S(1)}, bf16[1792,128]{1,0:T(8,128)(2,1)S(1)}, bf16[1792,128]{1,0:T(8,128)(2,1)S(1)}) fusion(bf16[16128,128]{1,0:T(8,128)(2,1)} %bitcast.30, s32[]{:T(128)S(6)} %select_n.88, s32[]{:T(128)S(6)} %select_n.87, s32[]{:T(128)S(6)} %select_n.84, s32[]{:T(128)S(6)} %select_n.81), kind=kLoop, calls=%fused_computation.9 | loop fusion | bytes 3670032 | tf_op jit(solution)/shard_map/dynamic_slice | solution.py:225
  7.0 11.1 %collective-permute-done = bf16[2240,128]{1,0:T(8,128)(2,1)S(1)} collective-permute-done((bf16[2240,128]{1,0:T(8,128)(2,1)S(1)}, bf16[2240,128]{1,0:T(8,128)(2,1)S(1)}, u32[]{:S(2)}, u32[]{:S(2)}) %collective-permute-start) | collective-permute-done | bytes 573472 | tf_op jit(solution)/shard_map/ppermute | solution.py:199
  18.9 1.8 %collective-permute-start.2 = (bf16[1792,128]{1,0:T(8,128)(2,1)S(1)}, bf16[1792,128]{1,0:T(8,128)(2,1)S(1)}, u32[]{:S(2)}, u32[]{:S(2)}) collective-permute-start(bf16[1792,128]{1,0:T(8,128)(2,1)S(1)} %get-tuple-element.35), channel_id=1, source_target_pairs={{0,16},{8,24},{16,0},{24,8},{1,17},{9,25},{17,1},{25,9},{2,18},{10... | collective-permute-start | bytes 1376264 | tf_op jit(solution)/shard_map/ppermute | solution.py:199
  20.7 10.7 %collective-permute-done.4 = bf16[2240,128]{1,0:T(8,128)(2,1)S(1)} collective-permute-done((bf16[2240,128]{1,0:T(8,128)(2,1)S(1)}, bf16[2240,128]{1,0:T(8,128)(2,1)S(1)}, u32[]{:S(2)}, u32[]{:S(2)}) %collective-permute-start.4) | collective-permute-done | bytes 573472 | tf_op jit(solution)/shard_map/ppermute | solution.py:199
  31.4 1.5 %add_convert_fusion = bf16[2240,128]{1,0:T(8,128)(2,1)S(1)} fusion(bf16[2240,128]{1,0:T(8,128)(2,1)S(1)} %collective-permute-done, bf16[2240,128]{1,0:T(8,128)(2,1)S(1)} %collective-permute-done.4, bf16[2240,128]{1,0:T(8,128)(2,1)S(1)} %collective-permute-done.3, bf16[16128,128]{1,0:T(8,128)(2,1)} %bitcast.31, s32[]{:T(128)S(6)} %select_n.89), kind=kLoop, calls=%fused_computation | loop fusion | flops 2293760 | bytes 2867204 | tf_op jit(solution)/shard_map/convert_element_type | solution.py:284
  33.3 1.6 %collective-permute-start.6 = (bf16[1792,128]{1,0:T(8,128)(2,1)S(1)}, bf16[1792,128]{1,0:T(8,128)(2,1)S(1)}, u32[]{:S(2)}, u32[]{:S(2)}) collective-permute-start(bf16[1792,128]{1,0:T(8,128)(2,1)S(1)} %get-tuple-element.40), channel_id=1, source_target_pairs={{0,24},{8,16},{16,8},{24,0},{1,25},{9,17},{17,9},{25,1},{2,26},{10... | collective-permute-start | bytes 1376264 | tf_op jit(solution)/shard_map/ppermute | solution.py:199
  35.3 6.0 %collective-permute-done.2 = bf16[1792,128]{1,0:T(8,128)(2,1)S(1)} collective-permute-done((bf16[1792,128]{1,0:T(8,128)(2,1)S(1)}, bf16[1792,128]{1,0:T(8,128)(2,1)S(1)}, u32[]{:S(2)}, u32[]{:S(2)}) %collective-permute-start.2) | collective-permute-done | bytes 458784 | tf_op jit(solution)/shard_map/ppermute | solution.py:199
  41.2 1.5 %collective-permute-start.7 = (f32[3,128,128]{2,1,0:T(8,128)S(1)}, f32[3,128,128]{2,1,0:T(8,128)S(1)}, u32[]{:S(2)}, u32[]{:S(2)}) collective-permute-start(f32[3,128,128]{2,1,0:T(8,128)S(1)} %pad_maximum_fusion), channel_id=1, source_target_pairs={{0,1},{1,0},{2,3},{3,2},{4,5},{5,4},{6,7},{7,6},{8,9},{9,8},{10,11... | collective-permute-start | bytes 589832 | tf_op jit(solution)/shard_map/ppermute | solution.py:199
  42.7 1.5 %collective-permute-start.22 = (bf16[2240,128]{1,0:T(8,128)(2,1)S(1)}, bf16[2240,128]{1,0:T(8,128)(2,1)S(1)}, u32[]{:S(2)}, u32[]{:S(2)}) collective-permute-start(bf16[2240,128]{1,0:T(8,128)(2,1)S(1)} %add_convert_fusion), channel_id=1, source_target_pairs={{0,16},{8,24},{16,0},{24,8},{1,17},{9,25},{17,1},{25,9},{2,18},{10... | collective-permute-start | bytes 1720328 | tf_op jit(solution)/shard_map/ppermute | solution.py:199
  44.2 3.6 %collective-permute-done.7 = f32[3,128,128]{2,1,0:T(8,128)S(1)} collective-permute-done((f32[3,128,128]{2,1,0:T(8,128)S(1)}, f32[3,128,128]{2,1,0:T(8,128)S(1)}, u32[]{:S(2)}, u32[]{:S(2)}) %collective-permute-start.7) | collective-permute-done | bytes 196640 | tf_op jit(solution)/shard_map/ppermute | solution.py:199
  47.8 2.2 %collective-permute-done.6 = bf16[1792,128]{1,0:T(8,128)(2,1)S(1)} collective-permute-done((bf16[1792,128]{1,0:T(8,128)(2,1)S(1)}, bf16[1792,128]{1,0:T(8,128)(2,1)S(1)}, u32[]{:S(2)}, u32[]{:S(2)}) %collective-permute-start.6) | collective-permute-done | bytes 458784 | tf_op jit(solution)/shard_map/ppermute | solution.py:199
  50.1 2.5 %collective-permute-start.9 = (f32[3,128,128]{2,1,0:T(8,128)S(1)}, f32[3,128,128]{2,1,0:T(8,128)S(1)}, u32[]{:S(2)}, u32[]{:S(2)}) collective-permute-start(f32[3,128,128]{2,1,0:T(8,128)S(1)} %add.152), channel_id=1, source_target_pairs={{0,2},{1,3},{2,0},{3,1},{4,6},{5,7},{6,4},{7,5},{8,10},{9,11},{10,... | collective-permute-start | bytes 589832 | tf_op jit(solution)/shard_map/ppermute | solution.py:199
  53.1 4.6 %collective-permute-done.9 = f32[3,128,128]{2,1,0:T(8,128)S(1)} collective-permute-done((f32[3,128,128]{2,1,0:T(8,128)S(1)}, f32[3,128,128]{2,1,0:T(8,128)S(1)}, u32[]{:S(2)}, u32[]{:S(2)}) %collective-permute-start.9) | collective-permute-done | bytes 196640 | tf_op jit(solution)/shard_map/ppermute | solution.py:199
  57.7 2.8 %collective-permute-start.14 = (f32[3,128,128]{2,1,0:T(8,128)S(1)}, f32[3,128,128]{2,1,0:T(8,128)S(1)}, u32[]{:S(2)}, u32[]{:S(2)}) collective-permute-start(f32[3,128,128]{2,1,0:T(8,128)S(1)} %add.155.gram_ref), channel_id=1, source_target_pairs={{0,4},{1,5},{2,6},{3,7},{4,0},{5,1},{6,2},{7,3},{8,12},{9,13},{10,... | collective-permute-start | bytes 589832 | tf_op jit(solution)/shard_map/ppermute | solution.py:199
  60.5 1.5 %collective-permute-start.10 = (f32[2,128,128]{2,1,0:T(8,128)S(1)}, f32[2,128,128]{2,1,0:T(8,128)S(1)}, u32[]{:S(2)}, u32[]{:S(2)}) collective-permute-start(f32[2,128,128]{2,1,0:T(8,128)S(1)} %fusion.3), channel_id=1, source_target_pairs={{0,1},{1,0},{2,3},{3,2},{4,5},{5,4},{6,7},{7,6},{8,9},{9,8},{10,11... | collective-permute-start | bytes 393224 | tf_op jit(solution)/shard_map/ppermute | solution.py:199
  62.0 1.6 %collective-permute-start.8 = (bf16[1792,128]{1,0:T(8,128)(2,1)S(1)}, bf16[1792,128]{1,0:T(8,128)(2,1)S(1)}, u32[]{:S(2)}, u32[]{:S(2)}) collective-permute-start(bf16[1792,128]{1,0:T(8,128)(2,1)S(1)} %add_convert_fusion.1), channel_id=1, source_target_pairs={{0,16},{8,24},{16,0},{24,8},{1,17},{9,25},{17,1},{25,9},{2,18},{10... | collective-permute-start | bytes 1376264 | tf_op jit(solution)/shard_map/ppermute | solution.py:199
  63.6 1.9 %collective-permute-done.10 = f32[2,128,128]{2,1,0:T(8,128)S(1)} collective-permute-done((f32[2,128,128]{2,1,0:T(8,128)S(1)}, f32[2,128,128]{2,1,0:T(8,128)S(1)}, u32[]{:S(2)}, u32[]{:S(2)}) %collective-permute-start.10) | collective-permute-done | bytes 131104 | tf_op jit(solution)/shard_map/ppermute | solution.py:199
  65.5 1.6 %collective-permute-start.11 = (f32[2,128,128]{2,1,0:T(8,128)S(1)}, f32[2,128,128]{2,1,0:T(8,128)S(1)}, u32[]{:S(2)}, u32[]{:S(2)}) collective-permute-start(f32[2,128,128]{2,1,0:T(8,128)S(1)} %add.156), channel_id=1, source_target_pairs={{0,2},{1,3},{2,0},{3,1},{4,6},{5,7},{6,4},{7,5},{8,10},{9,11},{10,... | collective-permute-start | bytes 393224 | tf_op jit(solution)/shard_map/ppermute | solution.py:199
  67.2 2.2 %collective-permute-done.14.arrived_ref = f32[3,128,128]{2,1,0:T(8,128)S(1)} collective-permute-done((f32[3,128,128]{2,1,0:T(8,128)S(1)}, f32[3,128,128]{2,1,0:T(8,128)S(1)}, u32[]{:S(2)}, u32[]{:S(2)}) %collective-permute-start.14) | collective-permute-done | bytes 196640 | tf_op jit(solution)/shard_map/ppermute | solution.py:199
  69.4 3.8 %shard_map.50.refs_2_ = f32[3,128,128]{2,1,0:T(8,128)S(1)} custom-call(f32[3,128,128]{2,1,0:T(8,128)S(1)} %add.155.gram_ref, f32[3,128,128]{2,1,0:T(8,128)S(1)} %collective-permute-done.14.arrived_ref), custom_call_target="tpu_custom_call" | custom-call | flops 1358954496 | bytes 589824 | tf_op jit(solution)/shard_map/pallas_call | solution.py:68
  74.7 2.8 %shard_map.51 = (f32[18,896,128]{2,1,0:T(8,128)}, bf16[18,896,128]{2,1,0:T(8,128)(2,1)}) custom-call(s32[1]{0:T(128)} %bitcast.place_ref, s32[18]{0:T(128)S(1)} %copy-done, bf16[5,448,128]{2,1,0:T(8,128)(2,1)S(1)} %bitcast.21, bf16[5,448,128]{2,1,0:T(8,128)(2,1)S(1)} %bitcast.22, f32[3,128,128]{2,1,0:T(8,128)S(1)} %shard_map.50.refs_2_, ...), custom_call_target="tpu_custom_call" | custom-call | flops 293601280 | bytes 6881280 | tf_op jit(solution)/shard_map/pallas_call | solution.py:171
  77.5 5.5 %collective-permute-done.12.arrived_ref = f32[2,128,128]{2,1,0:T(8,128)S(1)} collective-permute-done((f32[2,128,128]{2,1,0:T(8,128)S(1)}, f32[2,128,128]{2,1,0:T(8,128)S(1)}, u32[]{:S(2)}, u32[]{:S(2)}) %collective-permute-start.12) | collective-permute-done | bytes 131104 | tf_op jit(solution)/shard_map/ppermute | solution.py:199
  83.0 1.4 %collective-permute-start.20 = (f32[3,128,128]{2,1,0:T(8,128)S(1)}, f32[3,128,128]{2,1,0:T(8,128)S(1)}, u32[]{:S(2)}, u32[]{:S(2)}) collective-permute-start(f32[3,128,128]{2,1,0:T(8,128)S(1)} %shard_map.50.refs_2_), channel_id=1, source_target_pairs={{0,16},{8,24},{16,0},{24,8},{1,17},{9,25},{17,1},{25,9},{2,18},{10... | collective-permute-start | bytes 589832 | tf_op jit(solution)/shard_map/ppermute | solution.py:199
  84.4 3.4 %shard_map.52.refs_2_ = f32[2,128,128]{2,1,0:T(8,128)S(1)} custom-call(f32[2,128,128]{2,1,0:T(8,128)S(1)} %add.157.gram_ref, f32[2,128,128]{2,1,0:T(8,128)S(1)} %collective-permute-done.12.arrived_ref), custom_call_target="tpu_custom_call" | custom-call | flops 905969664 | bytes 393216 | tf_op jit(solution)/shard_map/pallas_call | solution.py:68
  88.4 1.9 %collective-permute-done.20.refs_2_ = f32[3,128,128]{2,1,0:T(8,128)S(1)} collective-permute-done((f32[3,128,128]{2,1,0:T(8,128)S(1)}, f32[3,128,128]{2,1,0:T(8,128)S(1)}, u32[]{:S(2)}, u32[]{:S(2)}) %collective-permute-start.20) | collective-permute-done | bytes 196640 | tf_op jit(solution)/shard_map/ppermute | solution.py:199
  90.3 1.4 %collective-permute-start.17 = (f32[2,128,128]{2,1,0:T(8,128)S(1)}, f32[2,128,128]{2,1,0:T(8,128)S(1)}, u32[]{:S(2)}, u32[]{:S(2)}) collective-permute-start(f32[2,128,128]{2,1,0:T(8,128)S(1)} %shard_map.52.refs_2_), channel_id=1, source_target_pairs={{0,16},{8,24},{16,0},{24,8},{1,17},{9,25},{17,1},{25,9},{2,18},{10... | collective-permute-start | bytes 393224 | tf_op jit(solution)/shard_map/ppermute | solution.py:199
  91.7 2.5 %shard_map.53 = (f32[18,896,128]{2,1,0:T(8,128)}, bf16[18,896,128]{2,1,0:T(8,128)(2,1)}) custom-call(s32[1]{0:T(128)} %bitcast.place_ref, s32[18]{0:T(128)S(1)} %copy-done, bf16[2,896,128]{2,1,0:T(8,128)(2,1)S(1)} %bitcast.20, bf16[2,896,128]{2,1,0:T(8,128)(2,1)S(1)} %bitcast.27, ...), custom_call_target="tpu_custom_call", output_to_operand_aliasing={{0}: (7, {}), {1}: (8, {})} | custom-call | flops 234881024 | bytes 5505024 | tf_op jit(solution)/shard_map/pallas_call | solution.py:171
  94.3 1.1 %collective-permute-done.17.refs_2_ = f32[2,128,128]{2,1,0:T(8,128)S(1)} collective-permute-done((f32[2,128,128]{2,1,0:T(8,128)S(1)}, f32[2,128,128]{2,1,0:T(8,128)S(1)}, u32[]{:S(2)}, u32[]{:S(2)}) %collective-permute-start.17) | collective-permute-done | bytes 131104 | tf_op jit(solution)/shard_map/ppermute | solution.py:199
  95.4 2.8 %shard_map.54 = (f32[18,896,128]{2,1,0:T(8,128)}, bf16[18,896,128]{2,1,0:T(8,128)(2,1)}) custom-call(s32[1]{0:T(128)} %bitcast.place_ref, s32[18]{0:T(128)S(1)} %copy-done, bf16[5,448,128]{2,1,0:T(8,128)(2,1)S(1)} %bitcast.23, bf16[5,448,128]{2,1,0:T(8,128)(2,1)S(1)} %bitcast.24, ...), custom_call_target="tpu_custom_call", output_to_operand_aliasing={{0}: (7, {}), {1}: (8, {})} | custom-call | flops 293601280 | bytes 6881280 | tf_op jit(solution)/shard_map/pallas_call | solution.py:171
  98.2 2.5 %shard_map.55 = (f32[18,896,128]{2,1,0:T(8,128)}, bf16[18,896,128]{2,1,0:T(8,128)(2,1)}) custom-call(s32[1]{0:T(128)} %bitcast.place_ref, s32[18]{0:T(128)S(1)} %copy-done, bf16[2,896,128]{2,1,0:T(8,128)(2,1)S(1)} %bitcast.25, bf16[2,896,128]{2,1,0:T(8,128)(2,1)S(1)} %bitcast.26, ...), custom_call_target="tpu_custom_call", output_to_operand_aliasing={{0}: (7, {}), {1}: (8, {})} | custom-call | flops 234881024 | bytes 5505024 | tf_op jit(solution)/shard_map/pallas_call | solution.py:171
  (45 shorter events, 5.0 us)
Async XLA Ops:
  2.3 15.8 %collective-permute-start = (bf16[2240,128]{1,0:T(8,128)(2,1)S(1)}, bf16[2240,128]{1,0:T(8,128)(2,1)S(1)}, u32[]{:S(2)}, u32[]{:S(2)}) collective-permute-start(bf16[2240,128]{1,0:T(8,128)(2,1)S(1)} %get-tuple-element.66), channel_id=1, source_target_pairs={{0,24},{8,16},{16,8},{24,0},{1,25},{9,17},{17,9},{25,1},{2,26},{10... | collective-permute-start | bytes 1720328 | tf_op jit(solution)/shard_map/ppermute | solution.py:199
  4.7 16.0 %collective-permute-start.3 = (bf16[2240,128]{1,0:T(8,128)(2,1)S(1)}, bf16[2240,128]{1,0:T(8,128)(2,1)S(1)}, u32[]{:S(2)}, u32[]{:S(2)}) collective-permute-start(bf16[2240,128]{1,0:T(8,128)(2,1)S(1)} %get-tuple-element.64), channel_id=1, source_target_pairs={{0,8},{8,0},{16,24},{24,16},{1,9},{9,1},{17,25},{25,17},{2,10},{10... | collective-permute-start | bytes 1720328 | tf_op jit(solution)/shard_map/ppermute | solution.py:199
  5.4 26.0 %collective-permute-start.4 = (bf16[2240,128]{1,0:T(8,128)(2,1)S(1)}, bf16[2240,128]{1,0:T(8,128)(2,1)S(1)}, u32[]{:S(2)}, u32[]{:S(2)}) collective-permute-start(bf16[2240,128]{1,0:T(8,128)(2,1)S(1)} %get-tuple-element.65), channel_id=1, source_target_pairs={{0,16},{8,24},{16,0},{24,8},{1,17},{9,25},{17,1},{25,9},{2,18},{10... | collective-permute-start | bytes 1720328 | tf_op jit(solution)/shard_map/ppermute | solution.py:199
  18.1 17.1 %collective-permute-start.1 = (bf16[1792,128]{1,0:T(8,128)(2,1)S(1)}, bf16[1792,128]{1,0:T(8,128)(2,1)S(1)}, u32[]{:S(2)}, u32[]{:S(2)}) collective-permute-start(bf16[1792,128]{1,0:T(8,128)(2,1)S(1)} %get-tuple-element.34), channel_id=1, source_target_pairs={{0,8},{8,0},{16,24},{24,16},{1,9},{9,1},{17,25},{25,17},{2,10},{10... | collective-permute-start | bytes 1376264 | tf_op jit(solution)/shard_map/ppermute | solution.py:199
  18.9 22.3 %collective-permute-start.2 = (bf16[1792,128]{1,0:T(8,128)(2,1)S(1)}, bf16[1792,128]{1,0:T(8,128)(2,1)S(1)}, u32[]{:S(2)}, u32[]{:S(2)}) collective-permute-start(bf16[1792,128]{1,0:T(8,128)(2,1)S(1)} %get-tuple-element.35), channel_id=1, source_target_pairs={{0,16},{8,24},{16,0},{24,8},{1,17},{9,25},{17,1},{25,9},{2,18},{10... | collective-permute-start | bytes 1376264 | tf_op jit(solution)/shard_map/ppermute | solution.py:199
  31.4 43.3 %slice-start = ((s8[8257536]{0:T(1024)(128)(4,1)}), s8[4194304]{0:T(1024)(128)(4,1)S(1)}, s32[]{:S(2)}) async-start(s8[8257536]{0:T(1024)(128)(4,1)} %bitcast.17), calls=%async_computation | async-start | bytes 8388608
  33.2 2.0 %collective-permute-start.5 = (f32[1,128,128]{2,1,0:T(8,128)S(1)}, f32[1,128,128]{2,1,0:T(8,128)S(1)}, u32[]{:S(2)}, u32[]{:S(2)}) collective-permute-start(f32[1,128,128]{2,1,0:T(8,128)S(1)} %convolution_bitcast_fusion), channel_id=1, source_target_pairs={{0,8},{8,0},{16,24},{24,16},{1,9},{9,1},{17,25},{25,17},{2,10},{10... | collective-permute-start | bytes 196616 | tf_op jit(solution)/shard_map/ppermute | solution.py:199
  33.3 16.8 %collective-permute-start.6 = (bf16[1792,128]{1,0:T(8,128)(2,1)S(1)}, bf16[1792,128]{1,0:T(8,128)(2,1)S(1)}, u32[]{:S(2)}, u32[]{:S(2)}) collective-permute-start(bf16[1792,128]{1,0:T(8,128)(2,1)S(1)} %get-tuple-element.40), channel_id=1, source_target_pairs={{0,24},{8,16},{16,8},{24,0},{1,25},{9,17},{17,9},{25,1},{2,26},{10... | collective-permute-start | bytes 1376264 | tf_op jit(solution)/shard_map/ppermute | solution.py:199
  41.2 6.5 %collective-permute-start.7 = (f32[3,128,128]{2,1,0:T(8,128)S(1)}, f32[3,128,128]{2,1,0:T(8,128)S(1)}, u32[]{:S(2)}, u32[]{:S(2)}) collective-permute-start(f32[3,128,128]{2,1,0:T(8,128)S(1)} %pad_maximum_fusion), channel_id=1, source_target_pairs={{0,1},{1,0},{2,3},{3,2},{4,5},{5,4},{6,7},{7,6},{8,9},{9,8},{10,11... | collective-permute-start | bytes 589832 | tf_op jit(solution)/shard_map/ppermute | solution.py:199
  42.7 30.6 %collective-permute-start.13 = (bf16[2240,128]{1,0:T(8,128)(2,1)S(1)}, bf16[2240,128]{1,0:T(8,128)(2,1)S(1)}, u32[]{:S(2)}, u32[]{:S(2)}) collective-permute-start(bf16[2240,128]{1,0:T(8,128)(2,1)S(1)} %add_convert_fusion), channel_id=1, source_target_pairs={{0,8},{8,0},{16,24},{24,16},{1,9},{9,1},{17,25},{25,17},{2,10},{10... | collective-permute-start | bytes 1720328 | tf_op jit(solution)/shard_map/ppermute | solution.py:199
  42.7 40.2 %collective-permute-start.22 = (bf16[2240,128]{1,0:T(8,128)(2,1)S(1)}, bf16[2240,128]{1,0:T(8,128)(2,1)S(1)}, u32[]{:S(2)}, u32[]{:S(2)}) collective-permute-start(bf16[2240,128]{1,0:T(8,128)(2,1)S(1)} %add_convert_fusion), channel_id=1, source_target_pairs={{0,16},{8,24},{16,0},{24,8},{1,17},{9,25},{17,1},{25,9},{2,18},{10... | collective-permute-start | bytes 1720328 | tf_op jit(solution)/shard_map/ppermute | solution.py:199
  47.8 26.9 %slice-start.1 = ((s8[8257536]{0:T(1024)(128)(4,1)}), s8[4063232]{0:T(1024)(128)(4,1)S(1)}, s32[]{:S(2)}) async-start(s8[8257536]{0:T(1024)(128)(4,1)} %bitcast.17), calls=%async_computation.1 | async-start | bytes 8126464
  50.1 7.6 %collective-permute-start.9 = (f32[3,128,128]{2,1,0:T(8,128)S(1)}, f32[3,128,128]{2,1,0:T(8,128)S(1)}, u32[]{:S(2)}, u32[]{:S(2)}) collective-permute-start(f32[3,128,128]{2,1,0:T(8,128)S(1)} %add.152), channel_id=1, source_target_pairs={{0,2},{1,3},{2,0},{3,1},{4,6},{5,7},{6,4},{7,5},{8,10},{9,11},{10,... | collective-permute-start | bytes 589832 | tf_op jit(solution)/shard_map/ppermute | solution.py:199
  52.8 22.0 %copy-start = (s32[18]{0:T(128)S(1)}, s32[18]{0:T(128)}, u32[]{:S(2)}) copy-start(s32[18]{0:T(128)} %table_ref.7) | copy-start | bytes 220
  57.7 11.7 %collective-permute-start.14 = (f32[3,128,128]{2,1,0:T(8,128)S(1)}, f32[3,128,128]{2,1,0:T(8,128)S(1)}, u32[]{:S(2)}, u32[]{:S(2)}) collective-permute-start(f32[3,128,128]{2,1,0:T(8,128)S(1)} %add.155.gram_ref), channel_id=1, source_target_pairs={{0,4},{1,5},{2,6},{3,7},{4,0},{5,1},{6,2},{7,3},{8,12},{9,13},{10,... | collective-permute-start | bytes 589832 | tf_op jit(solution)/shard_map/ppermute | solution.py:199
  60.5 5.0 %collective-permute-start.10 = (f32[2,128,128]{2,1,0:T(8,128)S(1)}, f32[2,128,128]{2,1,0:T(8,128)S(1)}, u32[]{:S(2)}, u32[]{:S(2)}) collective-permute-start(f32[2,128,128]{2,1,0:T(8,128)S(1)} %fusion.3), channel_id=1, source_target_pairs={{0,1},{1,0},{2,3},{3,2},{4,5},{5,4},{6,7},{7,6},{8,9},{9,8},{10,11... | collective-permute-start | bytes 393224 | tf_op jit(solution)/shard_map/ppermute | solution.py:199
  62.0 25.7 %collective-permute-start.8 = (bf16[1792,128]{1,0:T(8,128)(2,1)S(1)}, bf16[1792,128]{1,0:T(8,128)(2,1)S(1)}, u32[]{:S(2)}, u32[]{:S(2)}) collective-permute-start(bf16[1792,128]{1,0:T(8,128)(2,1)S(1)} %add_convert_fusion.1), channel_id=1, source_target_pairs={{0,16},{8,24},{16,0},{24,8},{1,17},{9,25},{17,1},{25,9},{2,18},{10... | collective-permute-start | bytes 1376264 | tf_op jit(solution)/shard_map/ppermute | solution.py:199
  65.5 7.7 %collective-permute-start.11 = (f32[2,128,128]{2,1,0:T(8,128)S(1)}, f32[2,128,128]{2,1,0:T(8,128)S(1)}, u32[]{:S(2)}, u32[]{:S(2)}) collective-permute-start(f32[2,128,128]{2,1,0:T(8,128)S(1)} %add.156), channel_id=1, source_target_pairs={{0,2},{1,3},{2,0},{3,1},{4,6},{5,7},{6,4},{7,5},{8,10},{9,11},{10,... | collective-permute-start | bytes 393224 | tf_op jit(solution)/shard_map/ppermute | solution.py:199
  73.2 1.5 %collective-permute-start.15 = (f32[3,128,128]{2,1,0:T(8,128)S(1)}, f32[3,128,128]{2,1,0:T(8,128)S(1)}, u32[]{:S(2)}, u32[]{:S(2)}) collective-permute-start(f32[3,128,128]{2,1,0:T(8,128)S(1)} %shard_map.50.refs_2_), channel_id=1, source_target_pairs={{0,8},{8,0},{16,24},{24,16},{1,9},{9,1},{17,25},{25,17},{2,10},{10... | collective-permute-start | bytes 589832 | tf_op jit(solution)/shard_map/ppermute | solution.py:199
  73.3 9.7 %collective-permute-start.12 = (f32[2,128,128]{2,1,0:T(8,128)S(1)}, f32[2,128,128]{2,1,0:T(8,128)S(1)}, u32[]{:S(2)}, u32[]{:S(2)}) collective-permute-start(f32[2,128,128]{2,1,0:T(8,128)S(1)} %add.157.gram_ref), channel_id=1, source_target_pairs={{0,4},{1,5},{2,6},{3,7},{4,0},{5,1},{6,2},{7,3},{8,12},{9,13},{10,... | collective-permute-start | bytes 393224 | tf_op jit(solution)/shard_map/ppermute | solution.py:199
  73.4 18.3 %collective-permute-start.18 = (bf16[1792,128]{1,0:T(8,128)(2,1)S(1)}, bf16[1792,128]{1,0:T(8,128)(2,1)S(1)}, u32[]{:S(2)}, u32[]{:S(2)}) collective-permute-start(bf16[1792,128]{1,0:T(8,128)(2,1)S(1)} %add_convert_fusion.1), channel_id=1, source_target_pairs={{0,8},{8,0},{16,24},{24,16},{1,9},{9,1},{17,25},{25,17},{2,10},{10... | collective-permute-start | bytes 1376264 | tf_op jit(solution)/shard_map/ppermute | solution.py:199
  83.0 12.5 %collective-permute-start.23 = (bf16[2240,128]{1,0:T(8,128)(2,1)S(1)}, bf16[2240,128]{1,0:T(8,128)(2,1)S(1)}, u32[]{:S(2)}, u32[]{:S(2)}) collective-permute-start(bf16[2240,128]{1,0:T(8,128)(2,1)S(1)} %collective-permute-done.22), channel_id=1, source_target_pairs={{0,8},{8,0},{16,24},{24,16},{1,9},{9,1},{17,25},{25,17},{2,10},{10... | collective-permute-start | bytes 1720328 | tf_op jit(solution)/shard_map/ppermute | solution.py:199
  83.0 7.3 %collective-permute-start.20 = (f32[3,128,128]{2,1,0:T(8,128)S(1)}, f32[3,128,128]{2,1,0:T(8,128)S(1)}, u32[]{:S(2)}, u32[]{:S(2)}) collective-permute-start(f32[3,128,128]{2,1,0:T(8,128)S(1)} %shard_map.50.refs_2_), channel_id=1, source_target_pairs={{0,16},{8,24},{16,0},{24,8},{1,17},{9,25},{17,1},{25,9},{2,18},{10... | collective-permute-start | bytes 589832 | tf_op jit(solution)/shard_map/ppermute | solution.py:199
  87.8 10.4 %collective-permute-start.16 = (bf16[1792,128]{1,0:T(8,128)(2,1)S(1)}, bf16[1792,128]{1,0:T(8,128)(2,1)S(1)}, u32[]{:S(2)}, u32[]{:S(2)}) collective-permute-start(bf16[1792,128]{1,0:T(8,128)(2,1)S(1)} %collective-permute-done.8), channel_id=1, source_target_pairs={{0,8},{8,0},{16,24},{24,16},{1,9},{9,1},{17,25},{25,17},{2,10},{10... | collective-permute-start | bytes 1376264 | tf_op jit(solution)/shard_map/ppermute | solution.py:199
  88.1 3.6 %collective-permute-start.19 = (f32[2,128,128]{2,1,0:T(8,128)S(1)}, f32[2,128,128]{2,1,0:T(8,128)S(1)}, u32[]{:S(2)}, u32[]{:S(2)}) collective-permute-start(f32[2,128,128]{2,1,0:T(8,128)S(1)} %shard_map.52.refs_2_), channel_id=1, source_target_pairs={{0,8},{8,0},{16,24},{24,16},{1,9},{9,1},{17,25},{25,17},{2,10},{10... | collective-permute-start | bytes 393224 | tf_op jit(solution)/shard_map/ppermute | solution.py:199
  90.3 5.1 %collective-permute-start.17 = (f32[2,128,128]{2,1,0:T(8,128)S(1)}, f32[2,128,128]{2,1,0:T(8,128)S(1)}, u32[]{:S(2)}, u32[]{:S(2)}) collective-permute-start(f32[2,128,128]{2,1,0:T(8,128)S(1)} %shard_map.52.refs_2_), channel_id=1, source_target_pairs={{0,16},{8,24},{16,0},{24,8},{1,17},{9,25},{17,1},{25,9},{2,18},{10... | collective-permute-start | bytes 393224 | tf_op jit(solution)/shard_map/ppermute | solution.py:199
  91.7 3.7 %collective-permute-start.24 = (f32[3,128,128]{2,1,0:T(8,128)S(1)}, f32[3,128,128]{2,1,0:T(8,128)S(1)}, u32[]{:S(2)}, u32[]{:S(2)}) collective-permute-start(f32[3,128,128]{2,1,0:T(8,128)S(1)} %collective-permute-done.20.refs_2_), channel_id=1, source_target_pairs={{0,8},{8,0},{16,24},{24,16},{1,9},{9,1},{17,25},{25,17},{2,10},{10... | collective-permute-start | bytes 589832 | tf_op jit(solution)/shard_map/ppermute | solution.py:199
  95.4 2.8 %collective-permute-start.21 = (f32[2,128,128]{2,1,0:T(8,128)S(1)}, f32[2,128,128]{2,1,0:T(8,128)S(1)}, u32[]{:S(2)}, u32[]{:S(2)}) collective-permute-start(f32[2,128,128]{2,1,0:T(8,128)S(1)} %collective-permute-done.17.refs_2_), channel_id=1, source_target_pairs={{0,8},{8,0},{16,24},{24,16},{1,9},{9,1},{17,25},{25,17},{2,10},{10... | collective-permute-start | bytes 393224 | tf_op jit(solution)/shard_map/ppermute | solution.py:199
